TPU v7x, 32 devices: a whole 2x2x4 slice. The times are simulated.
32 devices in a mesh: groups: 2 (over x), rows: 16 (over z, y, core).
Axes of the slice: x: 2, y: 2, z: 4, core: 2. Of those that a mesh axis runs over, the one named last changes fastest.
Arguments:
- embeddings: bfloat16 [65536, 1024], P(('groups', 'rows')), parts along dimension 0, may hold values from -6 to 6
- block_pairs: int32 [480, 2], P(('groups', 'rows')), parts along dimension 0, may hold values from 0 to 63, as said below
- pair_count: int32 [32], P(('groups', 'rows')), parts along dimension 0, may hold values from 3 to 15
- start_panel: float32 [64, 65536], P(None, ('groups', 'rows')), parts along dimension 1, may hold values from -6 to 6
Outputs:
- basis: float32 [64, 65536], P(None, ('groups', 'rows')), parts along dimension 1
There are 2 independent parts, one for each index of `groups`. A program takes and returns all parts, laid end to end along the dimension named above; each array names one. Nothing has to cross between parts.
Inputs may be any that keep to these rules, and one draw needn't show every extreme that they name: `block_pairs`: row and column block numbers. The row blocks named in the slots of device d (slots d * 15 to (d + 1) * 15 - 1) are d's own blocks d * 4 to (d + 1) * 4 - 1. Of these slots, exactly one names a column block of each device d + o and d - o (taken modulo the number of devices along rows) for o = 1 to 7, and the other 1 name a column block of d itself, different from the slot's row block. Over all slots of a part no unordered pair of blocks appears twice.
All inputs are finite; a program needn't handle non-finite values.
Results may differ from a plain program's by a relative error of at most 0.012.
The roundings to bfloat16 on the way count: a program that leaves them out, or rounds other values in their place, can miss the bound.
Values may be sent and summed in bfloat16 or wider, within the bound.
No kernel may reach another device: no remote copies, remote signals or barrier semaphores. Data moves between devices by JAX's collectives and lax.ppermute only.
A program may use at most 128 MiB of HBM per device.

v0:
```python
import jax
import jax.numpy as jnp
from jax import lax
from jax.sharding import PartitionSpec as P

BLOCK = 512
ITERS = 2
REACH = 7


SHARPNESS = 24.0


def from_behind(value, axis, steps):
    count = lax.axis_size(axis)
    pairs = [(source, (source + steps) % count) for source in range(count)]
    return lax.ppermute(value, axis, pairs)


def normalize_rows(rows_in):
    values = rows_in.astype(jnp.float32)
    factor = lax.rsqrt(jnp.mean(values * values, axis=-1, keepdims=True) + 1e-06) * values.shape[
        -1
    ] ** (-0.5)
    return (values * factor).astype(jnp.bfloat16)


def affinity_tile(left, right):
    scores = lax.dot_general(
        left, right, (((1,), (1,)), ((), ())), preferred_element_type=jnp.float32
    )
    return jnp.sinh(SHARPNESS * scores).astype(jnp.bfloat16)


def fetch_rows(outgoing):
    received = []
    for offset in range(1, REACH + 1):
        received.append(from_behind(outgoing[offset - 1], "rows", -offset))
    for offset in range(1, REACH + 1):
        received.append(from_behind(outgoing[REACH + offset - 1], "rows", offset))
    return jnp.stack(received)


def fetch_panels(outgoing):
    received = []
    for offset in range(1, REACH + 1):
        received.append(from_behind(outgoing[offset - 1], "rows", -offset))
    for offset in range(1, REACH + 1):
        received.append(from_behind(outgoing[REACH + offset - 1], "rows", offset))
    return jnp.stack(received)


def send_back(outgoing):
    received = []
    for offset in range(1, REACH + 1):
        received.append(from_behind(outgoing[offset - 1], "rows", offset))
    for offset in range(1, REACH + 1):
        received.append(from_behind(outgoing[REACH + offset - 1], "rows", -offset))
    return jnp.stack(received)


def on_device(embeddings, block_pairs, pair_count, start_panel):
    peer_count = lax.axis_size("rows")
    my_index = lax.axis_index("rows")
    blocks_here = embeddings.shape[0] // BLOCK
    panel_width = start_panel.shape[0]
    unit_rows = normalize_rows(embeddings).reshape(blocks_here, BLOCK, embeddings.shape[1])
    live_pairs = pair_count[0]
    slot_total = block_pairs.shape[0]
    col_owner = block_pairs[:, 1] // blocks_here
    row_local = block_pairs[:, 0] % blocks_here
    col_local = block_pairs[:, 1] % blocks_here
    is_live = jnp.arange(slot_total, dtype=jnp.int32) < live_pairs
    is_remote = jnp.logical_and(is_live, col_owner != my_index)
    offsets = jnp.arange(1, REACH + 1, dtype=jnp.int32)
    targets = jnp.concatenate(
        [(my_index + offsets) % peer_count, (my_index - offsets + peer_count) % peer_count]
    )
    match_table = jnp.logical_and(is_remote[None, :], col_owner[None, :] == targets[:, None])
    wanted = jnp.max(jnp.where(match_table, col_local[None, :], -1), axis=1)
    asked_list = []
    for offset in range(1, REACH + 1):
        asked_list.append(from_behind(wanted[offset - 1 : offset], "rows", offset))
    for offset in range(1, REACH + 1):
        asked_list.append(from_behind(wanted[REACH + offset - 1 : REACH + offset], "rows", -offset))
    asked_here = jnp.concatenate(asked_list)
    distance = (col_owner - my_index + peer_count) % peer_count
    slot_remote = jnp.where(distance <= REACH, distance - 1, REACH + peer_count - distance - 1)
    slot_remote = jnp.clip(slot_remote, 0, 2 * REACH - 1)
    partner_total = 2 * REACH
    asked_ok = (asked_here >= 0).astype(jnp.bfloat16)
    asked_index = jnp.maximum(asked_here, 0)
    selector = (asked_here[:, None] == jnp.arange(blocks_here, dtype=jnp.int32)[None, :]).astype(
        jnp.float32
    )
    remote_rows = fetch_rows(jnp.take(unit_rows, asked_index, axis=0) * asked_ok[:, None, None])
    panel = start_panel
    for sweep_index in range(ITERS):
        panel_blocks = (
            panel.astype(jnp.bfloat16).reshape(panel_width, blocks_here, BLOCK).transpose(1, 0, 2)
        )
        outgoing_panel = jnp.take(panel_blocks, asked_index, axis=0) * asked_ok[:, None, None]
        remote_panel = fetch_panels(outgoing_panel)

        def pair_work(slot_id, carry):
            accum_own, outgoing = carry
            row_blk = row_local[slot_id]
            col_blk = col_local[slot_id]
            remote_now = col_owner[slot_id] != my_index
            remote_at = slot_remote[slot_id]
            col_unit = jnp.where(remote_now, remote_rows[remote_at], unit_rows[col_blk])
            col_panel = jnp.where(remote_now, remote_panel[remote_at], panel_blocks[col_blk])
            affinity = affinity_tile(unit_rows[row_blk], col_unit)
            forward = lax.dot_general(
                col_panel, affinity, (((1,), (1,)), ((), ())), preferred_element_type=jnp.float32
            )
            mirror = lax.dot_general(
                panel_blocks[row_blk],
                affinity,
                (((1,), (0,)), ((), ())),
                preferred_element_type=jnp.float32,
            )
            accum_own = accum_own.at[row_blk].add(forward)
            keep_here = jnp.logical_and(jnp.logical_not(remote_now), row_blk != col_blk)
            accum_own = accum_own.at[col_blk].add(jnp.where(keep_here, mirror, jnp.float32(0.0)))
            outgoing = outgoing.at[remote_at].add(jnp.where(remote_now, mirror, jnp.float32(0.0)))
            return (accum_own, outgoing)

        initial = (
            jnp.zeros((blocks_here, panel_width, BLOCK), jnp.float32),
            jnp.zeros((partner_total, panel_width, BLOCK), jnp.float32),
        )
        accum_own, outgoing = lax.fori_loop(0, live_pairs, pair_work, initial)
        returned = send_back(outgoing.astype(jnp.bfloat16))
        accum_own = accum_own + jnp.einsum(
            "pb,pkr->bkr", selector, returned.astype(jnp.float32), precision=lax.Precision.HIGHEST
        )
        gathered = accum_own.transpose(1, 0, 2).reshape(panel_width, blocks_here * BLOCK)
        gram_local = jnp.dot(gathered, gathered.T, precision=lax.Precision.HIGHEST)
        gram_total = lax.psum(gram_local, "rows") / (peer_count * embeddings.shape[0])
        lower_factor = jnp.linalg.cholesky(gram_total)
        panel = lax.linalg.triangular_solve(lower_factor, gathered, left_side=True, lower=True)
    return panel


def solution(mesh):
    in_specs = (
        P(("groups", "rows"), None),
        P(("groups", "rows"), None),
        P(("groups", "rows")),
        P(None, ("groups", "rows")),
    )
    out_specs = P(None, ("groups", "rows"))
    return jax.shard_map(
        on_device, mesh=mesh, in_specs=in_specs, out_specs=out_specs, check_vma=False
    )
```

profile of v0, /device:TPU:2, one launch (start us, length us, event | category | flops | bytes accessed | tf_op | source)
XLA Modules:
  0.0 1289.8 jit_solution(13643931324464973773)
XLA Ops:
  8.9 3.1 fusion.60
  11.9 4.9 fusion.61
  19.2 4.3 collective-permute-start.6
  28.1 3.1 collective-permute-start.12
  35.3 8.7 concatenate.74
  44.1 8.7 concatenate.89
  52.8 8.8 gather_fusion
  62.2 7.8 select_multiply_fusion
  70.3 3.4 slice_bitcast_fusion
  73.7 3.0 collective-permute-start.28
  79.0 78.6 %collective-permute-done.15 = bf16[64,512]{1,0:T(8,128)(2,1)S(1)} collective-permute-done((bf16[64,512]{1,0:T(8,128)(2,1)S(1)}, bf16[64,512]{1,0:T(8,128)(2,1)S(1)}, u32[]{:S(2)}, u32[]{:S(2)}) %collective-permute-start.15) | collective-permute-done | bytes 65568 | tf_op jit(solution)/shard_map/ppermute | solution.py:17
  157.6 3.7 collective-permute-done.16
  162.0 3.6 collective-permute-done.17
  170.4 5.7 collective-permute-start.19
  178.0 3.9 collective-permute-start.20
  186.8 3.7 collective-permute-done.21
  192.3 6.6 collective-permute-done.22
  198.9 5.5 collective-permute-done.23
  204.4 6.1 collective-permute-done.24
  210.5 5.5 collective-permute-done.25
  215.9 6.1 collective-permute-done.26
  222.0 4.6 collective-permute-done.27
  230.2 3.9 collective-permute-start.36
  234.1 16.3 %collective-permute-done.32 = bf16[512,1024]{1,0:T(8,128)(2,1)S(1)} collective-permute-done((bf16[512,1024]{1,0:T(8,128)(2,1)}, bf16[512,1024]{1,0:T(8,128)(2,1)S(1)}, u32[]{:S(2)}, u32[]{:S(2)}) %collective-permute-start.32) | collective-permute-done | bytes 1048608 | tf_op jit(solution)/shard_map/ppermute | solution.py:17
  250.4 82.5 %collective-permute-start.37 = (bf16[512,1024]{1,0:T(8,128)(2,1)S(1)}, bf16[512,1024]{1,0:T(8,128)(2,1)S(1)}, u32[]{:S(2)}, u32[]{:S(2)}) collective-permute-start(bf16[512,1024]{1,0:T(8,128)(2,1)S(1)} %get-tuple-element.304), channel_id=1, source_target_pairs={{0,3},{1,4},{2,5},{3,6},{4,7},{5,8},{6,9},{7,10},{8,11},{9,12},{10... | collective-permute-start | bytes 3145736 | tf_op jit(solution)/shard_map/ppermute | solution.py:17
  333.0 3.7 collective-permute-start.38
  336.8 23.2 %collective-permute-start.39 = (bf16[512,1024]{1,0:T(8,128)(2,1)S(1)}, bf16[512,1024]{1,0:T(8,128)(2,1)S(1)}, u32[]{:S(2)}, u32[]{:S(2)}) collective-permute-start(bf16[512,1024]{1,0:T(8,128)(2,1)S(1)} %get-tuple-element.302), channel_id=1, source_target_pairs={{0,5},{1,6},{2,7},{3,8},{4,9},{5,10},{6,11},{7,12},{8,13},{9,14},{... | collective-permute-start | bytes 3145736 | tf_op jit(solution)/shard_map/ppermute | solution.py:17
  360.1 3.0 collective-permute-start.40
  363.1 25.6 %collective-permute-start.41 = (bf16[512,1024]{1,0:T(8,128)(2,1)S(1)}, bf16[512,1024]{1,0:T(8,128)(2,1)S(1)}, u32[]{:S(2)}, u32[]{:S(2)}) collective-permute-start(bf16[512,1024]{1,0:T(8,128)(2,1)S(1)} %get-tuple-element.300), channel_id=1, source_target_pairs={{0,7},{1,8},{2,9},{3,10},{4,11},{5,12},{6,13},{7,14},{8,15},{9,0},... | collective-permute-start | bytes 3145736 | tf_op jit(solution)/shard_map/ppermute | solution.py:17
  388.9 84.7 %collective-permute-done.39 = bf16[512,1024]{1,0:T(8,128)(2,1)S(1)} collective-permute-done((bf16[512,1024]{1,0:T(8,128)(2,1)S(1)}, bf16[512,1024]{1,0:T(8,128)(2,1)S(1)}, u32[]{:S(2)}, u32[]{:S(2)}) %collective-permute-start.39) | collective-permute-done | bytes 1048608 | tf_op jit(solution)/shard_map/ppermute | solution.py:17
  473.7 4.5 collective-permute-done.40
  478.7 4.9 copy-done.1
  483.6 110.3 %while.30 = (s32[]{:T(128)}, f32[4,64,512]{2,1,0:T(8,128)S(1)}, f32[14,64,512]{2,1,0:T(8,128)S(1)}, s32[]{:T(128)}, s32[15]{0:T(128)S(1)}, /*index=5*/s32[15]{0:...) while((s32[]{:T(128)}, f32[4,64,512]{2,1,0:T(8,128)S(1)}, ...), condition=%wide.region_6.8_spmd, body=%wide.region_2.7_spmd.sunk | while | flops 607944768 | bytes 5705673 | solution.py:133
  493.4 3.3 fusion.113
  511.6 3.3 fusion.113
  529.9 3.3 fusion.113
  548.1 3.3 fusion.113
  566.3 3.3 fusion.113
  584.6 3.3 fusion.113
  594.0 113.5 %collective-permute-start.42 = (bf16[64,512]{1,0:T(8,128)(2,1)S(1)}, bf16[64,512]{1,0:T(8,128)(2,1)S(1)}, u32[]{:S(2)}, u32[]{:S(2)}) collective-permute-start(bf16[64,512]{1,0:T(8,128)(2,1)S(1)} %get-tuple-element.355), channel_id=1, source_target_pairs={{0,1},{1,2},{2,3},{3,4},{4,5},{5,6},{6,7},{7,8},{8,9},{9,10},{10,1... | collective-permute-start | bytes 196616 | tf_op jit(solution)/shard_map/ppermute | solution.py:17
  707.5 36.5 %collective-permute-start.44 = (bf16[64,512]{1,0:T(8,128)(2,1)S(1)}, bf16[64,512]{1,0:T(8,128)(2,1)S(1)}, u32[]{:S(2)}, u32[]{:S(2)}) collective-permute-start(bf16[64,512]{1,0:T(8,128)(2,1)S(1)} %get-tuple-element.353), channel_id=1, source_target_pairs={{0,3},{1,4},{2,5},{3,6},{4,7},{5,8},{6,9},{7,10},{8,11},{9,12},{10... | collective-permute-start | bytes 196616 | tf_op jit(solution)/shard_map/ppermute | solution.py:17
  744.0 38.4 %collective-permute-start.45 = (bf16[64,512]{1,0:T(8,128)(2,1)S(1)}, bf16[64,512]{1,0:T(8,128)(2,1)S(1)}, u32[]{:S(2)}, u32[]{:S(2)}) collective-permute-start(bf16[64,512]{1,0:T(8,128)(2,1)S(1)} %get-tuple-element.352), channel_id=1, source_target_pairs={{0,4},{1,5},{2,6},{3,7},{4,8},{5,9},{6,10},{7,11},{8,12},{9,13},{1... | collective-permute-start | bytes 196616 | tf_op jit(solution)/shard_map/ppermute | solution.py:17
  782.4 4.5 collective-permute-start.48
  792.3 2.9 collective-permute-start.52
  802.8 2.8 stack.269
  806.8 63.0 %psum.14 = f32[64,64]{0,1:T(8,128)S(1)} all-reduce(f32[64,64]{0,1:T(8,128)S(1)} %convolution_bitcast_fusion.3), channel_id=1, replica_groups=mesh['groups'=2,'rows'=16] {'rows'}, use_global_device_ids=true, to_apply=%region_7.9 | all-reduce | flops 4096 | bytes 32768 | tf_op jit(solution)/shard_map/psum | solution.py:140
  870.0 5.8 cholesky.44
  877.1 4.9 custom-call.6
  886.3 3.2 collective-permute-start.61
  903.4 3.2 collective-permute-start.69
  910.6 110.3 %while.31 = (s32[]{:T(128)}, f32[4,64,512]{2,1,0:T(8,128)S(1)}, f32[14,64,512]{2,1,0:T(8,128)S(1)}, s32[]{:T(128)}, s32[15]{0:T(128)S(1)}, /*index=5*/s32[15]{0:...) while((s32[]{:T(128)}, f32[4,64,512]{2,1,0:T(8,128)S(1)}, ...), condition=%wide.region_14.18_spmd, body=%wide.region_10.17_spmd.sunk | while | flops 607944768 | bytes 5705673 | solution.py:133
  920.5 3.3 fusion.121
  938.7 3.3 fusion.121
  957.0 3.3 fusion.121
  975.2 3.3 fusion.121
  993.4 3.3 fusion.121
  1011.7 3.3 fusion.121
  1021.1 93.2 %collective-permute-start.70 = (bf16[64,512]{1,0:T(8,128)(2,1)S(1)}, bf16[64,512]{1,0:T(8,128)(2,1)S(1)}, u32[]{:S(2)}, u32[]{:S(2)}) collective-permute-start(bf16[64,512]{1,0:T(8,128)(2,1)S(1)} %get-tuple-element.327), channel_id=1, source_target_pairs={{0,1},{1,2},{2,3},{3,4},{4,5},{5,6},{6,7},{7,8},{8,9},{9,10},{10,1... | collective-permute-start | bytes 196616 | tf_op jit(solution)/shard_map/ppermute | solution.py:17
  1114.3 72.9 %collective-permute-start.72 = (bf16[64,512]{1,0:T(8,128)(2,1)S(1)}, bf16[64,512]{1,0:T(8,128)(2,1)S(1)}, u32[]{:S(2)}, u32[]{:S(2)}) collective-permute-start(bf16[64,512]{1,0:T(8,128)(2,1)S(1)} %get-tuple-element.325), channel_id=1, source_target_pairs={{0,3},{1,4},{2,5},{3,6},{4,7},{5,8},{6,9},{7,10},{8,11},{9,12},{10... | collective-permute-start | bytes 196616 | tf_op jit(solution)/shard_map/ppermute | solution.py:17
  1196.4 3.9 collective-permute-done.74
  1202.3 3.0 collective-permute-start.82
  1214.0 62.0 %psum.15 = f32[64,64]{0,1:T(8,128)S(1)} all-reduce(f32[64,64]{0,1:T(8,128)S(1)} %convolution_bitcast_fusion.2), channel_id=1, replica_groups=mesh['groups'=2,'rows'=16] {'rows'}, use_global_device_ids=true, to_apply=%region_15.19 | all-reduce | flops 4096 | bytes 32768 | tf_op jit(solution)/shard_map/psum | solution.py:140
  1276.1 5.8 cholesky.55
  1283.3 4.9 custom-call.7
  (345 shorter events, 180.4 us)
Async XLA Ops:
  2.3 15.6 %collective-permute-start = (s32[1]{0:T(128)}, s32[1]{0:T(128)}, u32[]{:S(2)}, u32[]{:S(2)}) collective-permute-start(s32[1]{0:T(128)} %get-tuple-element.385), channel_id=1, source_target_pairs={{0,1},{1,2},{2,3},{3,4},{4,5},{5,6},{6,7},{7,8},{8,9},{9,10},{10,1... | collective-permute-start | bytes 20 | tf_op jit(solution)/shard_map/ppermute | solution.py:17
  2.4 16.8 %collective-permute-start.1 = (s32[1]{0:T(128)}, s32[1]{0:T(128)}, u32[]{:S(2)}, u32[]{:S(2)}) collective-permute-start(s32[1]{0:T(128)} %get-tuple-element.384), channel_id=1, source_target_pairs={{0,2},{1,3},{2,4},{3,5},{4,6},{5,7},{6,8},{7,9},{8,10},{9,11},{10,... | collective-permute-start | bytes 20 | tf_op jit(solution)/shard_map/ppermute | solution.py:17
  4.0 19.5 %collective-permute-start.2 = (s32[1]{0:T(128)}, s32[1]{0:T(128)}, u32[]{:S(2)}, u32[]{:S(2)}) collective-permute-start(s32[1]{0:T(128)} %get-tuple-element.383), channel_id=1, source_target_pairs={{0,3},{1,4},{2,5},{3,6},{4,7},{5,8},{6,9},{7,10},{8,11},{9,12},{10... | collective-permute-start | bytes 20 | tf_op jit(solution)/shard_map/ppermute | solution.py:17
  6.4 17.4 %collective-permute-start.3 = (s32[1]{0:T(128)}, s32[1]{0:T(128)}, u32[]{:S(2)}, u32[]{:S(2)}) collective-permute-start(s32[1]{0:T(128)} %get-tuple-element.382), channel_id=1, source_target_pairs={{0,4},{1,5},{2,6},{3,7},{4,8},{5,9},{6,10},{7,11},{8,12},{9,13},{1... | collective-permute-start | bytes 20 | tf_op jit(solution)/shard_map/ppermute | solution.py:17
  8.0 17.0 %collective-permute-start.4 = (s32[1]{0:T(128)}, s32[1]{0:T(128)}, u32[]{:S(2)}, u32[]{:S(2)}) collective-permute-start(s32[1]{0:T(128)} %get-tuple-element.381), channel_id=1, source_target_pairs={{0,5},{1,6},{2,7},{3,8},{4,9},{5,10},{6,11},{7,12},{8,13},{9,14},{... | collective-permute-start | bytes 20 | tf_op jit(solution)/shard_map/ppermute | solution.py:17
  18.0 8.2 collective-permute-start.5
  19.2 8.3 collective-permute-start.6
  23.8 7.3 collective-permute-start.8
  70.2 8.4 collective-permute-start.14
  73.7 152.9 %collective-permute-start.28 = (bf16[512,1024]{1,0:T(8,128)(2,1)}, bf16[512,1024]{1,0:T(8,128)(2,1)S(1)}, u32[]{:S(2)}, u32[]{:S(2)}) collective-permute-start(bf16[512,1024]{1,0:T(8,128)(2,1)} %get-tuple-element.313), channel_id=1, source_target_pairs={{0,15},{1,0},{2,1},{3,2},{4,3},{5,4},{6,5},{7,6},{8,7},{9,8},{10,9... | collective-permute-start | bytes 3145736 | tf_op jit(solution)/shard_map/ppermute | solution.py:17
  76.8 151.7 %collective-permute-start.29 = (bf16[512,1024]{1,0:T(8,128)(2,1)}, bf16[512,1024]{1,0:T(8,128)(2,1)S(1)}, u32[]{:S(2)}, u32[]{:S(2)}) collective-permute-start(bf16[512,1024]{1,0:T(8,128)(2,1)} %get-tuple-element.312), channel_id=1, source_target_pairs={{0,14},{1,15},{2,0},{3,1},{4,2},{5,3},{6,4},{7,5},{8,6},{9,7},{10,... | collective-permute-start | bytes 3145736 | tf_op jit(solution)/shard_map/ppermute | solution.py:17
  78.6 151.4 %collective-permute-start.30 = (bf16[512,1024]{1,0:T(8,128)(2,1)}, bf16[512,1024]{1,0:T(8,128)(2,1)S(1)}, u32[]{:S(2)}, u32[]{:S(2)}) collective-permute-start(bf16[512,1024]{1,0:T(8,128)(2,1)} %get-tuple-element.311), channel_id=1, source_target_pairs={{0,13},{1,14},{2,15},{3,0},{4,1},{5,2},{6,3},{7,4},{8,5},{9,6},{10... | collective-permute-start | bytes 3145736 | tf_op jit(solution)/shard_map/ppermute | solution.py:17
  78.6 151.5 %collective-permute-start.31 = (bf16[512,1024]{1,0:T(8,128)(2,1)}, bf16[512,1024]{1,0:T(8,128)(2,1)S(1)}, u32[]{:S(2)}, u32[]{:S(2)}) collective-permute-start(bf16[512,1024]{1,0:T(8,128)(2,1)} %get-tuple-element.310), channel_id=1, source_target_pairs={{0,12},{1,13},{2,14},{3,15},{4,0},{5,1},{6,2},{7,3},{8,4},{9,5},{1... | collective-permute-start | bytes 3145736 | tf_op jit(solution)/shard_map/ppermute | solution.py:17
  78.7 78.9 %collective-permute-start.15 = (bf16[64,512]{1,0:T(8,128)(2,1)S(1)}, bf16[64,512]{1,0:T(8,128)(2,1)S(1)}, u32[]{:S(2)}, u32[]{:S(2)}) collective-permute-start(bf16[64,512]{1,0:T(8,128)(2,1)S(1)} %get-tuple-element.368), channel_id=1, source_target_pairs={{0,14},{1,15},{2,0},{3,1},{4,2},{5,3},{6,4},{7,5},{8,6},{9,7},{10,... | collective-permute-start | bytes 196616 | tf_op jit(solution)/shard_map/ppermute | solution.py:17
  170.4 7.6 collective-permute-start.19
  184.1 6.4 collective-permute-start.21
  190.5 8.4 collective-permute-start.22
  226.6 23.8 %collective-permute-start.32 = (bf16[512,1024]{1,0:T(8,128)(2,1)}, bf16[512,1024]{1,0:T(8,128)(2,1)S(1)}, u32[]{:S(2)}, u32[]{:S(2)}) collective-permute-start(bf16[512,1024]{1,0:T(8,128)(2,1)} %get-tuple-element.309), channel_id=1, source_target_pairs={{0,11},{1,12},{2,13},{3,14},{4,15},{5,0},{6,1},{7,2},{8,3},{9,4},{... | collective-permute-start | bytes 3145736 | tf_op jit(solution)/shard_map/ppermute | solution.py:17
  227.5 105.4 %collective-permute-start.33 = (bf16[512,1024]{1,0:T(8,128)(2,1)S(1)}, bf16[512,1024]{1,0:T(8,128)(2,1)S(1)}, u32[]{:S(2)}, u32[]{:S(2)}) collective-permute-start(bf16[512,1024]{1,0:T(8,128)(2,1)S(1)} %get-tuple-element.308), channel_id=1, source_target_pairs={{0,10},{1,11},{2,12},{3,13},{4,14},{5,15},{6,0},{7,1},{8,2},{9,3},... | collective-permute-start | bytes 3145736 | tf_op jit(solution)/shard_map/ppermute | solution.py:17
  228.6 108.2 %collective-permute-start.34 = (bf16[512,1024]{1,0:T(8,128)(2,1)S(1)}, bf16[512,1024]{1,0:T(8,128)(2,1)S(1)}, u32[]{:S(2)}, u32[]{:S(2)}) collective-permute-start(bf16[512,1024]{1,0:T(8,128)(2,1)S(1)} %get-tuple-element.307), channel_id=1, source_target_pairs={{0,9},{1,10},{2,11},{3,12},{4,13},{5,14},{6,15},{7,0},{8,1},{9,2},... | collective-permute-start | bytes 3145736 | tf_op jit(solution)/shard_map/ppermute | solution.py:17
  230.0 130.0 %collective-permute-start.35 = (bf16[512,1024]{1,0:T(8,128)(2,1)S(1)}, bf16[512,1024]{1,0:T(8,128)(2,1)S(1)}, u32[]{:S(2)}, u32[]{:S(2)}) collective-permute-start(bf16[512,1024]{1,0:T(8,128)(2,1)S(1)} %get-tuple-element.306), channel_id=1, source_target_pairs={{0,1},{1,2},{2,3},{3,4},{4,5},{5,6},{6,7},{7,8},{8,9},{9,10},{10,1... | collective-permute-start | bytes 3145736 | tf_op jit(solution)/shard_map/ppermute | solution.py:17
  230.2 132.9 %collective-permute-start.36 = (bf16[512,1024]{1,0:T(8,128)(2,1)S(1)}, bf16[512,1024]{1,0:T(8,128)(2,1)S(1)}, u32[]{:S(2)}, u32[]{:S(2)}) collective-permute-start(bf16[512,1024]{1,0:T(8,128)(2,1)S(1)} %get-tuple-element.305), channel_id=1, source_target_pairs={{0,2},{1,3},{2,4},{3,5},{4,6},{5,7},{6,8},{7,9},{8,10},{9,11},{10,... | collective-permute-start | bytes 3145736 | tf_op jit(solution)/shard_map/ppermute | solution.py:17
  250.4 138.3 %collective-permute-start.37 = (bf16[512,1024]{1,0:T(8,128)(2,1)S(1)}, bf16[512,1024]{1,0:T(8,128)(2,1)S(1)}, u32[]{:S(2)}, u32[]{:S(2)}) collective-permute-start(bf16[512,1024]{1,0:T(8,128)(2,1)S(1)} %get-tuple-element.304), channel_id=1, source_target_pairs={{0,3},{1,4},{2,5},{3,6},{4,7},{5,8},{6,9},{7,10},{8,11},{9,12},{10... | collective-permute-start | bytes 3145736 | tf_op jit(solution)/shard_map/ppermute | solution.py:17
  333.0 55.9 %collective-permute-start.38 = (bf16[512,1024]{1,0:T(8,128)(2,1)S(1)}, bf16[512,1024]{1,0:T(8,128)(2,1)S(1)}, u32[]{:S(2)}, u32[]{:S(2)}) collective-permute-start(bf16[512,1024]{1,0:T(8,128)(2,1)S(1)} %get-tuple-element.303), channel_id=1, source_target_pairs={{0,4},{1,5},{2,6},{3,7},{4,8},{5,9},{6,10},{7,11},{8,12},{9,13},{1... | collective-permute-start | bytes 3145736 | tf_op jit(solution)/shard_map/ppermute | solution.py:17
  336.8 136.9 %collective-permute-start.39 = (bf16[512,1024]{1,0:T(8,128)(2,1)S(1)}, bf16[512,1024]{1,0:T(8,128)(2,1)S(1)}, u32[]{:S(2)}, u32[]{:S(2)}) collective-permute-start(bf16[512,1024]{1,0:T(8,128)(2,1)S(1)} %get-tuple-element.302), channel_id=1, source_target_pairs={{0,5},{1,6},{2,7},{3,8},{4,9},{5,10},{6,11},{7,12},{8,13},{9,14},{... | collective-permute-start | bytes 3145736 | tf_op jit(solution)/shard_map/ppermute | solution.py:17
  360.1 118.2 %collective-permute-start.40 = (bf16[512,1024]{1,0:T(8,128)(2,1)S(1)}, bf16[512,1024]{1,0:T(8,128)(2,1)S(1)}, u32[]{:S(2)}, u32[]{:S(2)}) collective-permute-start(bf16[512,1024]{1,0:T(8,128)(2,1)S(1)} %get-tuple-element.301), channel_id=1, source_target_pairs={{0,6},{1,7},{2,8},{3,9},{4,10},{5,11},{6,12},{7,13},{8,14},{9,15},... | collective-permute-start | bytes 3145736 | tf_op jit(solution)/shard_map/ppermute | solution.py:17
  363.1 115.2 %collective-permute-start.41 = (bf16[512,1024]{1,0:T(8,128)(2,1)S(1)}, bf16[512,1024]{1,0:T(8,128)(2,1)S(1)}, u32[]{:S(2)}, u32[]{:S(2)}) collective-permute-start(bf16[512,1024]{1,0:T(8,128)(2,1)S(1)} %get-tuple-element.300), channel_id=1, source_target_pairs={{0,7},{1,8},{2,9},{3,10},{4,11},{5,12},{6,13},{7,14},{8,15},{9,0},... | collective-permute-start | bytes 3145736 | tf_op jit(solution)/shard_map/ppermute | solution.py:17
  594.0 188.3 %collective-permute-start.42 = (bf16[64,512]{1,0:T(8,128)(2,1)S(1)}, bf16[64,512]{1,0:T(8,128)(2,1)S(1)}, u32[]{:S(2)}, u32[]{:S(2)}) collective-permute-start(bf16[64,512]{1,0:T(8,128)(2,1)S(1)} %get-tuple-element.355), channel_id=1, source_target_pairs={{0,1},{1,2},{2,3},{3,4},{4,5},{5,6},{6,7},{7,8},{8,9},{9,10},{10,1... | collective-permute-start | bytes 196616 | tf_op jit(solution)/shard_map/ppermute | solution.py:17
  707.5 74.9 %collective-permute-start.43 = (bf16[64,512]{1,0:T(8,128)(2,1)S(1)}, bf16[64,512]{1,0:T(8,128)(2,1)S(1)}, u32[]{:S(2)}, u32[]{:S(2)}) collective-permute-start(bf16[64,512]{1,0:T(8,128)(2,1)S(1)} %get-tuple-element.354), channel_id=1, source_target_pairs={{0,2},{1,3},{2,4},{3,5},{4,6},{5,7},{6,8},{7,9},{8,10},{9,11},{10,... | collective-permute-start | bytes 196616 | tf_op jit(solution)/shard_map/ppermute | solution.py:17
  707.5 79.3 %collective-permute-start.44 = (bf16[64,512]{1,0:T(8,128)(2,1)S(1)}, bf16[64,512]{1,0:T(8,128)(2,1)S(1)}, u32[]{:S(2)}, u32[]{:S(2)}) collective-permute-start(bf16[64,512]{1,0:T(8,128)(2,1)S(1)} %get-tuple-element.353), channel_id=1, source_target_pairs={{0,3},{1,4},{2,5},{3,6},{4,7},{5,8},{6,9},{7,10},{8,11},{9,12},{10... | collective-permute-start | bytes 196616 | tf_op jit(solution)/shard_map/ppermute | solution.py:17
  744.0 44.4 %collective-permute-start.45 = (bf16[64,512]{1,0:T(8,128)(2,1)S(1)}, bf16[64,512]{1,0:T(8,128)(2,1)S(1)}, u32[]{:S(2)}, u32[]{:S(2)}) collective-permute-start(bf16[64,512]{1,0:T(8,128)(2,1)S(1)} %get-tuple-element.352), channel_id=1, source_target_pairs={{0,4},{1,5},{2,6},{3,7},{4,8},{5,9},{6,10},{7,11},{8,12},{9,13},{1... | collective-permute-start | bytes 196616 | tf_op jit(solution)/shard_map/ppermute | solution.py:17
  782.4 9.8 collective-permute-start.46
  782.4 9.9 collective-permute-start.47
  782.4 12.8 collective-permute-start.48
  786.9 8.3 collective-permute-start.49
  788.4 8.9 collective-permute-start.50
  792.2 8.6 collective-permute-start.51
  792.3 8.6 collective-permute-start.52
  795.2 6.3 collective-permute-start.54
  883.8 6.3 collective-permute-start.57
  883.9 6.8 collective-permute-start.58
  883.9 7.5 collective-permute-start.59
  884.0 9.8 collective-permute-start.60
  886.3 10.7 collective-permute-start.61
  890.1 8.6 collective-permute-start.62
  890.7 9.3 collective-permute-start.63
  891.5 11.9 collective-permute-start.64
  893.8 13.4 %collective-permute-start.65 = (bf16[64,512]{1,0:T(8,128)(2,1)S(1)}, bf16[64,512]{1,0:T(8,128)(2,1)S(1)}, u32[]{:S(2)}, u32[]{:S(2)}) collective-permute-start(bf16[64,512]{1,0:T(8,128)(2,1)S(1)} %get-tuple-element.332), channel_id=1, source_target_pairs={{0,3},{1,4},{2,5},{3,6},{4,7},{5,8},{6,9},{7,10},{8,11},{9,12},{10... | collective-permute-start | bytes 196616 | tf_op jit(solution)/shard_map/ppermute | solution.py:17
  897.0 10.8 collective-permute-start.66
  898.6 9.8 collective-permute-start.67
  900.0 9.1 collective-permute-start.68
  903.4 6.3 collective-permute-start.69
  1021.1 168.1 %collective-permute-start.70 = (bf16[64,512]{1,0:T(8,128)(2,1)S(1)}, bf16[64,512]{1,0:T(8,128)(2,1)S(1)}, u32[]{:S(2)}, u32[]{:S(2)}) collective-permute-start(bf16[64,512]{1,0:T(8,128)(2,1)S(1)} %get-tuple-element.327), channel_id=1, source_target_pairs={{0,1},{1,2},{2,3},{3,4},{4,5},{5,6},{6,7},{7,8},{8,9},{9,10},{10,1... | collective-permute-start | bytes 196616 | tf_op jit(solution)/shard_map/ppermute | solution.py:17
  1114.3 77.1 %collective-permute-start.71 = (bf16[64,512]{1,0:T(8,128)(2,1)S(1)}, bf16[64,512]{1,0:T(8,128)(2,1)S(1)}, u32[]{:S(2)}, u32[]{:S(2)}) collective-permute-start(bf16[64,512]{1,0:T(8,128)(2,1)S(1)} %get-tuple-element.326), channel_id=1, source_target_pairs={{0,2},{1,3},{2,4},{3,5},{4,6},{5,7},{6,8},{7,9},{8,10},{9,11},{10,... | collective-permute-start | bytes 196616 | tf_op jit(solution)/shard_map/ppermute | solution.py:17
  1114.3 79.3 %collective-permute-start.72 = (bf16[64,512]{1,0:T(8,128)(2,1)S(1)}, bf16[64,512]{1,0:T(8,128)(2,1)S(1)}, u32[]{:S(2)}, u32[]{:S(2)}) collective-permute-start(bf16[64,512]{1,0:T(8,128)(2,1)S(1)} %get-tuple-element.325), channel_id=1, source_target_pairs={{0,3},{1,4},{2,5},{3,6},{4,7},{5,8},{6,9},{7,10},{8,11},{9,12},{10... | collective-permute-start | bytes 196616 | tf_op jit(solution)/shard_map/ppermute | solution.py:17
  1187.3 8.3 collective-permute-start.73
  1189.2 11.1 collective-permute-start.74
  1189.2 11.2 collective-permute-start.75
  1191.4 10.6 collective-permute-start.76
  1193.7 8.6 collective-permute-start.77
  1195.6 9.7 collective-permute-start.78
  1200.3 7.3 collective-permute-start.79
  1200.4 7.3 collective-permute-start.80
  1202.3 6.3 collective-permute-start.82
  (24 other events, 615.3 us)
where the time goes:
time: 1300 us; the launch traced here: 1290 us
  starting transfers between devices  586 us (45%)
  waiting for transfers between devices  251 us (19%)
  blocking collectives  125 us (10%)
  loops' own time  102 us (8%)
  local copies, waits for them, and re-layouts  88.2 us (7%)
  matrix products  82.5 us (6%)
  other arithmetic  52.6 us (4%)
    ppermute x84, starting transfers between devices, from_behind(): return lax.ppermute(value, axis, pairs)  586 us
    ppermute x84, waiting for transfers between devices, from_behind(): return lax.ppermute(value, axis, pairs)  251 us
    psum x2, blocking collectives, on_device(): lax.psum(gram_local, 'rows') / (peer_count * embeddings.shape[0])  125 us
    another operation x2, loops' own time, on_device(): accum_own, outgoing = lax.fori_loop(0, live_pairs, pair_work, initial)  102 us
    dot_general x12, matrix products, affinity_tile(): lax.dot_general(left, right, (((1,), (1,)), ((), ())), preferred_element_...  39.9 us
  transfers between devices with their start and end apart: 84, of which 27 were waited for; matrix products, arithmetic and copies ran while one was open for 2% of the time, Pallas kernels for 0%

commit v1 on v0

v1 whole, which is shorter than its diff:
```python
import functools

import jax
import jax.numpy as jnp
import numpy as np
from jax import lax
from jax.experimental import pallas as pl
from jax.experimental.pallas import tpu as pltpu
from jax.sharding import PartitionSpec as P

BLOCK = 512
ITERS = 2
REACH = 7
SHARPNESS = 24.0
LOG2E = 1.4426950408889634
VMEM_LIMIT = 56 * 1024 * 1024


def make_plan(count):
    if count == 16:
        moves = [[(i, i ^ m) for i in range(count)] for m in (1, 2, 3)]
        moves.append([(i, i - 4) for i in range(4, count)])
        moves.append([(i, i + 8) for i in range(8)] + [(i, i - 12) for i in range(12, 16)])
        late = {5}
    else:
        moves = [[(i, (i - o) % count) for i in range(count)] for o in range(1, REACH + 1)]
        late = {5, 6, 7}
    hold = -np.ones((count, len(moves) + 1), np.int32)
    hold[:, 0] = np.arange(count)
    for m, pairs in enumerate(moves):
        for source, target in pairs:
            hold[target, m + 1] = source
    work = np.zeros((count, count, count), bool)
    load = np.zeros(count, np.int32)
    for row in range(count):
        for col in range(count):
            gap = min((row - col) % count, (col - row) % count)
            if gap > REACH:
                continue
            able = [w for w in range(count) if row in hold[w] and col in hold[w]]
            pick = row if row in able else col if col in able else min(able, key=lambda w: load[w])
            work[pick, row, col] = True
            load[pick] += 1
    place = -np.ones((count, count), np.int32)
    for w in range(count):
        for s, device in enumerate(hold[w]):
            if device >= 0:
                place[w, device] = s
    return moves, place, work, late, int(load.max())


def work_list(lists, place, work, late, slots, blocks_here, top, me):
    count = lists.shape[0]
    pairs = lists[:, : 2 * slots].reshape(count, slots, 2)
    live = jnp.arange(slots, dtype=jnp.int32)[None, :] < lists[:, 2 * slots :]
    col_owner = pairs[:, :, 1] // blocks_here
    my_place = lax.dynamic_index_in_dim(jnp.asarray(place), me, 0, keepdims=False)
    my_work = lax.dynamic_index_in_dim(jnp.asarray(work.astype(np.int32)), me, 0, keepdims=False)
    is_col = col_owner[:, :, None] == jnp.arange(count, dtype=jnp.int32)
    col_place = jnp.sum(jnp.where(is_col, my_place[None, None, :], 0), axis=2)
    mine = jnp.sum(jnp.where(is_col, my_work[:, None, :], 0), axis=2) > 0
    valid = jnp.logical_and(live, mine)
    row_place = jnp.broadcast_to(my_place[:, None], col_place.shape)
    is_late = functools.reduce(
        jnp.logical_or, [jnp.logical_or(row_place == s, col_place == s) for s in sorted(late)]
    )
    row_held = (row_place * blocks_here + pairs[:, :, 0] % blocks_here).reshape(-1)
    col_held = (col_place * blocks_here + pairs[:, :, 1] % blocks_here).reshape(-1)
    first = jnp.logical_and(valid, jnp.logical_not(is_late)).reshape(-1).astype(jnp.int32)
    second = jnp.logical_and(valid, is_late).reshape(-1).astype(jnp.int32)
    total = first.shape[0]
    before = jnp.arange(total)[:, None] < jnp.arange(total)[None, :]
    first_rank = jnp.sum(jnp.where(before, first[:, None], 0), axis=0)
    second_rank = jnp.sum(jnp.where(before, second[:, None], 0), axis=0)
    n_first, n_second = jnp.sum(first), jnp.sum(second)
    rank = jnp.where(first > 0, first_rank, jnp.where(second > 0, n_first + second_rank, total))
    chosen = rank[None, :] == jnp.arange(top, dtype=jnp.int32)[:, None]
    rows = jnp.sum(jnp.where(chosen, row_held[None, :], 0), axis=1)
    cols = jnp.sum(jnp.where(chosen, col_held[None, :], 0), axis=1)
    zero = jnp.zeros((), jnp.int32)
    return jnp.stack([rows, cols]), jnp.stack([zero, n_first]), jnp.stack([n_first, n_first + n_second])


def fill_panel(panel_refs, pan, sem):
    per = panel_refs[0].shape[0]
    copies = [
        pltpu.make_async_copy(ref, pan.at[pl.ds(s * per, per)], sem.at[s]) for s, ref in enumerate(panel_refs)
    ]
    for copy in copies:
        copy.start()
    return copies


def add_products(pan, acc, aff, row, col):
    acc[row] += lax.dot_general(pan[col], aff, (((1,), (1,)), ((), ())), preferred_element_type=jnp.float32)
    acc[col] += lax.dot_general(pan[row], aff, (((1,), (0,)), ((), ())), preferred_element_type=jnp.float32)


def pair_kernel(n_unit, with_init, items, span, *refs):
    units, refs = refs[:n_unit], refs[n_unit:]
    n_panel = n_unit
    panels, refs = refs[:n_panel], refs[n_panel:]
    if with_init:
        acc_in, _, refs = refs[0], refs[1], refs[2:]
    acc, aff_out, ubuf, pan, affbuf, usem, psem, asem = refs
    per = units[0].shape[0]
    begin, end = span[0], span[1]

    def fetch(i, slot):
        for side in range(2):
            held = items[side, i]
            for s, ref in enumerate(units):

                @pl.when(held // per == s)
                def _():
                    pltpu.make_async_copy(ref.at[held % per], ubuf.at[slot, side], usem.at[slot, side]).start()

    def store(i, slot):
        return pltpu.make_async_copy(affbuf.at[slot], aff_out.at[i], asem.at[slot])

    copies = fill_panel(panels, pan, psem)

    @pl.when(begin < end)
    def _():
        fetch(begin, begin % 2)

    if with_init:
        acc[...] = acc_in[...]
    else:
        acc[...] = jnp.zeros_like(acc)
    for copy in copies:
        copy.wait()

    @pl.loop(begin, end)
    def _(i):
        slot = i % 2

        @pl.when(i + 1 < end)
        def _():
            fetch(i + 1, 1 - slot)

        for side in range(2):
            pltpu.make_async_copy(units[0].at[0], ubuf.at[slot, side], usem.at[slot, side]).wait()

        @pl.when(i >= begin + 2)
        def _():
            store(i - 2, slot).wait()

        half = BLOCK // 2
        for part in range(2):
            scores = lax.dot_general(
                ubuf[slot, 0, pl.ds(part * half, half), :],
                ubuf[slot, 1],
                (((1,), (1,)), ((), ())),
                preferred_element_type=jnp.float32,
            )
            power = scores * (SHARPNESS * LOG2E)
            affbuf[slot, pl.ds(part * half, half), :] = (
                jnp.exp2(power - 1.0) - jnp.exp2(-1.0 - power)
            ).astype(jnp.bfloat16)
        store(i, slot).start()
        add_products(pan, acc, affbuf[slot], items[0, i], items[1, i])

    for back in (2, 1):

        @pl.when(end - back >= begin)
        def _():
            store(end - back, (end - back) % 2).wait()


def pair_call(items, span, units, panels, top, init=None):
    blocks = len(units) * units[0].shape[0]
    width = panels[0].shape[1]
    depth = units[0].shape[2]
    smem = pl.BlockSpec(memory_space=pltpu.SMEM)
    anywhere = pl.BlockSpec(memory_space=pl.ANY)
    vmem = pl.BlockSpec(memory_space=pltpu.VMEM)
    operands = [items, span, *units, *panels]
    in_specs = [smem, smem] + [anywhere] * (2 * len(units))
    aliases = {}
    if init is not None:
        aliases = {len(operands): 0, len(operands) + 1: 1}
        operands += list(init)
        in_specs += [vmem, anywhere]
    return pl.pallas_call(
        functools.partial(pair_kernel, len(units), init is not None),
        out_shape=(
            jax.ShapeDtypeStruct((blocks, width, BLOCK), jnp.float32),
            jax.ShapeDtypeStruct((top, BLOCK, BLOCK), jnp.bfloat16),
        ),
        in_specs=in_specs,
        out_specs=(vmem, anywhere),
        scratch_shapes=[
            pltpu.VMEM((2, 2, BLOCK, depth), jnp.bfloat16),
            pltpu.VMEM((blocks, width, BLOCK), jnp.bfloat16),
            pltpu.VMEM((2, BLOCK, BLOCK), jnp.bfloat16),
            pltpu.SemaphoreType.DMA((2, 2)),
            pltpu.SemaphoreType.DMA((len(panels),)),
            pltpu.SemaphoreType.DMA((2,)),
        ],
        input_output_aliases=aliases,
        compiler_params=pltpu.CompilerParams(vmem_limit_bytes=VMEM_LIMIT),
        name="pairs",
    )(*operands)


def apply_kernel(n_panel, items, span, *refs):
    panels, refs = refs[:n_panel], refs[n_panel:]
    aff_in, acc, pan, affbuf, psem, asem = refs
    end = span[1]

    def load(i, slot):
        return pltpu.make_async_copy(aff_in.at[i], affbuf.at[slot], asem.at[slot])

    copies = fill_panel(panels, pan, psem)
    for ahead in range(3):

        @pl.when(ahead < end)
        def _():
            load(ahead, ahead).start()

    acc[...] = jnp.zeros_like(acc)
    for copy in copies:
        copy.wait()

    @pl.loop(0, end)
    def _(i):
        slot = i % 4

        @pl.when(i + 3 < end)
        def _():
            load(i + 3, (i + 3) % 4).start()

        load(i, slot).wait()
        add_products(pan, acc, affbuf[slot], items[0, i], items[1, i])


def apply_call(items, span, panels, aff):
    blocks = len(panels) * panels[0].shape[0]
    width = panels[0].shape[1]
    smem = pl.BlockSpec(memory_space=pltpu.SMEM)
    anywhere = pl.BlockSpec(memory_space=pl.ANY)
    return pl.pallas_call(
        functools.partial(apply_kernel, len(panels)),
        out_shape=jax.ShapeDtypeStruct((blocks, width, BLOCK), jnp.float32),
        in_specs=[smem, smem] + [anywhere] * (len(panels) + 1),
        out_specs=pl.BlockSpec(memory_space=pltpu.VMEM),
        scratch_shapes=[
            pltpu.VMEM((blocks, width, BLOCK), jnp.bfloat16),
            pltpu.VMEM((4, BLOCK, BLOCK), jnp.bfloat16),
            pltpu.SemaphoreType.DMA((len(panels),)),
            pltpu.SemaphoreType.DMA((4,)),
        ],
        compiler_params=pltpu.CompilerParams(vmem_limit_bytes=VMEM_LIMIT),
        name="apply",
    )(items, span, *panels, aff)


def gram_kernel(n_back, own, *refs):
    backs, (y_out, gram_out) = refs[:n_back], refs[n_back:]
    gram = None
    for b in range(own.shape[0]):
        total = own[b]
        for back in backs:
            total = total + back[b].astype(jnp.float32)
        y_out[b] = total
        part = lax.dot_general(
            total,
            total,
            (((1,), (1,)), ((), ())),
            preferred_element_type=jnp.float32,
            precision=lax.Precision.HIGHEST,
        )
        gram = part if gram is None else gram + part
    gram_out[...] = gram


def gram_call(own, backs):
    width = own.shape[1]
    return pl.pallas_call(
        functools.partial(gram_kernel, len(backs)),
        out_shape=(
            jax.ShapeDtypeStruct(own.shape, jnp.float32),
            jax.ShapeDtypeStruct((width, width), jnp.float32),
        ),
        compiler_params=pltpu.CompilerParams(vmem_limit_bytes=VMEM_LIMIT),
        name="gram",
    )(own, *backs)


def inverse_factor(gram):
    width = gram.shape[0]
    row_id = lax.broadcasted_iota(jnp.int32, (width, width), 0)
    col_id = lax.broadcasted_iota(jnp.int32, (width, width), 1)
    table = jnp.concatenate([gram, (row_id == col_id).astype(jnp.float32)], axis=1)
    below = lax.broadcasted_iota(jnp.int32, (width, 1), 0)
    scale = jnp.zeros((width, 1), jnp.float32)
    for k in range(width):
        line = table[k : k + 1, :]
        pivot = table[k : k + 1, k : k + 1]
        scale = jnp.where(below == k, pivot, scale)
        factor = jnp.where(below > k, table[:, k : k + 1] / pivot, 0.0)
        table = table - factor * line
    return table[:, width:] / jnp.sqrt(scale)


def panel_kernel(rows_all, last, gram, y, out):
    inverse = inverse_factor(gram[...] * (1.0 / rows_all))
    for b in range(y.shape[0]):
        block = lax.dot_general(
            inverse,
            y[b],
            (((1,), (0,)), ((), ())),
            preferred_element_type=jnp.float32,
            precision=lax.Precision.HIGHEST,
        )
        if last:
            out[:, b * BLOCK : (b + 1) * BLOCK] = block
        else:
            out[b] = block.astype(jnp.bfloat16)


def panel_call(gram, y, rows_all, last):
    blocks, width, _ = y.shape
    shape = (
        jax.ShapeDtypeStruct((width, blocks * BLOCK), jnp.float32)
        if last
        else jax.ShapeDtypeStruct(y.shape, jnp.bfloat16)
    )
    return pl.pallas_call(
        functools.partial(panel_kernel, rows_all, last),
        out_shape=shape,
        compiler_params=pltpu.CompilerParams(vmem_limit_bytes=VMEM_LIMIT),
        name="panel",
    )(gram, y)


def normalize_rows(rows_in):
    values = rows_in.astype(jnp.float32)
    factor = lax.rsqrt(jnp.mean(values * values, axis=-1, keepdims=True) + 1e-06) * values.shape[-1] ** (-0.5)
    return (values * factor).astype(jnp.bfloat16)


def sum_over_rows(value):
    count = lax.axis_size("rows")
    step = 1
    while step < count:
        value = value + lax.ppermute(value, "rows", [(i, i ^ step) for i in range(count)])
        step *= 2
    return value


def on_device(embeddings, block_pairs, pair_count, start_panel):
    count = lax.axis_size("rows")
    me = lax.axis_index("rows")
    blocks_here = embeddings.shape[0] // BLOCK
    width = start_panel.shape[0]
    slots = block_pairs.shape[0]
    moves, place, work, late, top = make_plan(count)

    unit = normalize_rows(embeddings).reshape(blocks_here, BLOCK, embeddings.shape[1])
    panel = start_panel.astype(jnp.bfloat16).reshape(width, blocks_here, BLOCK).transpose(1, 0, 2)

    lists = lax.all_gather(jnp.concatenate([block_pairs.reshape(-1), pair_count]), "rows")
    items, span_first, span_second = work_list(lists, place, work, late, slots, blocks_here, top, me)
    span_all = jnp.stack([span_first[0], span_second[1]])

    def spread(value):
        return [value] + [lax.ppermute(value, "rows", pairs) for pairs in moves]

    units = spread(unit)
    panels = spread(panel)
    early = [0] + [m for m in range(1, len(moves) + 1) if m not in late]
    first_units = [units[s] if s in early else unit for s in range(len(units))]
    first_panels = [panels[s] if s in early else panel for s in range(len(units))]
    state = pair_call(items, span_first, first_units, first_panels, top)
    acc, aff = pair_call(items, span_second, units, panels, top, state)

    for sweep in range(ITERS):
        if sweep > 0:
            panels = spread(panel)
            acc = apply_call(items, span_all, panels, aff)
        acc = acc.reshape(len(moves) + 1, blocks_here, width, BLOCK)
        backs = [
            lax.ppermute(acc[m + 1].astype(jnp.bfloat16), "rows", [(t, s) for s, t in pairs])
            for m, pairs in enumerate(moves)
        ]
        y, gram = gram_call(acc[0], backs)
        gram = sum_over_rows(gram)
        panel = panel_call(gram, y, count * embeddings.shape[0], sweep == ITERS - 1)
    return panel


def solution(mesh):
    in_specs = (
        P(("groups", "rows"), None),
        P(("groups", "rows"), None),
        P(("groups", "rows")),
        P(None, ("groups", "rows")),
    )
    out_specs = P(None, ("groups", "rows"))
    return jax.shard_map(on_device, mesh=mesh, in_specs=in_specs, out_specs=out_specs, check_vma=False)
```

time: 1300 us -> 467 us (0.36)
  the two profiles are of different devices: /device:TPU:2 before, /device:TPU:0 now
where the time goes in v1:
time: 467 us; the launch traced here: 460 us
  blocking collectives  179 us (38%)
  waiting for transfers between devices  144 us (31%)
  Pallas kernels  54.2 us (12%)
  starting transfers between devices  47 us (10%)
  other arithmetic  20.8 us (4%)
  local copies, waits for them, and re-layouts  12 us (3%)
    unnamed x1, blocking collectives  179 us
    ppermute x15, waiting for transfers between devices, spread(): return [value] + [lax.ppermute(value, 'rows', pairs) for pairs in moves]  107 us
    pallas_call x2, Pallas kernels, pair_call(): pl.pallas_call(functools.partial(pair_kernel, len(units), init is not Non...  24.2 us
    ppermute x15, starting transfers between devices, spread(): return [value] + [lax.ppermute(value, 'rows', pairs) for pairs in moves]  24.2 us
    ppermute x10, waiting for transfers between devices, on_device(): lax.ppermute(acc[m + 1].astype(jnp.bfloat16), 'rows', [(t, s) for s, t in...  19.2 us
    ppermute x8, waiting for transfers between devices, sum_over_rows(): lax.ppermute(value, 'rows', [(i, i ^ step) for i in range(count)])  17.6 us
    pallas_call x2, Pallas kernels, panel_call(): pl.pallas_call(functools.partial(panel_kernel, rows_all, last), out_shape...  16.7 us
    ppermute x10, starting transfers between devices, on_device(): lax.ppermute(acc[m + 1].astype(jnp.bfloat16), 'rows', [(t, s) for s, t in...  11.6 us
  transfers between devices with their start and end apart: 33, of which 18 were waited for; matrix products, arithmetic and copies ran while one was open for 3% of the time, Pallas kernels for 3%

profile of v1, /device:TPU:0, one launch (start us, length us, event | category | flops | bytes accessed | tf_op | source)
XLA Modules:
  0.0 460.1 jit_solution(16391280381571576217)
XLA Ops:
  0.0 3.2 fusion
  3.5 2.8 fusion.1
  6.3 1.3 collective-permute-start.3
  7.6 1.3 collective-permute-start.8
  8.9 2.5 collective-permute-start.7
  12.1 95.5 %collective-permute-done.8.refs_10_ = bf16[4,64,512]{2,1,0:T(8,128)(2,1)S(1)} collective-permute-done((bf16[4,64,512]{2,1,0:T(8,128)(2,1)S(1)}, bf16[4,64,512]{2,1,0:T(8,128)(2,1)S(1)}, u32[]{:S(2)}, u32[]{:S(2)}) %collective-permute-start.8) | collective-permute-done | bytes 262176 | tf_op jit(solution)/shard_map/ppermute | solution.py:369
  107.8 1.5 collective-permute-start.1
  109.5 4.6 %collective-permute-start.4 = (bf16[4,512,1024]{2,1,0:T(8,128)(2,1)}, bf16[4,512,1024]{2,1,0:T(8,128)(2,1)}, u32[]{:S(2)}, u32[]{:S(2)}) collective-permute-start(bf16[4,512,1024]{2,1,0:T(8,128)(2,1)} %bitcast.7.refs_0_.refs_5_), channel_id=1, source_target_pairs={{0,8},{1,9},{2,10},{3,11},{4,12},{5,13},{6,14},{7,15},{12,0},{13,1... | collective-permute-start | bytes 12582920 | tf_op jit(solution)/shard_map/ppermute | solution.py:369
  114.8 0.7 broadcast_multiply_fusion.1
  117.2 178.9 %all-reduce = s32[496]{0:T(512)S(1)} all-reduce(s32[496]{0:T(512)S(1)} %add_dynamic-update-slice_fusion), channel_id=2, replica_groups=mesh['groups'=2,'rows'=16] {'rows'}, use_global_device_ids=true, to_apply=%add | all-reduce | flops 496 | bytes 3968
  296.6 0.7 broadcast_compare_fusion
  297.3 0.7 dynamic-slice_bitcast_fusion.1
  298.0 0.7 dynamic-slice_bitcast_fusion
  299.5 0.7 convert_reduce_fusion
  302.3 1.3 pad_add_fusion.3.span
  304.5 4.3 collective-permute-start.9
  308.8 1.3 pad_add_fusion.1.span
  310.8 12.9 %pairs.2 = (f32[24,64,512]{2,1,0:T(8,128)}, bf16[20,512,512]{2,1,0:T(8,128)(2,1)}) custom-call(s32[2,20]{1,0:T(2,128)} %pad_add_fusion.items, s32[2]{0:T(128)} %pad_add_fusion.1.span, bf16[4,512,1024]{2,1,0:T(8,128)(2,1)} %bitcast.7.refs_0_.refs_5_, bf16[4,512,1024]{2,1,0:T(8,128)(2,1)} %collective-permute-done.refs_1_, ...), custom_call_target="tpu_custom_call" | custom-call | tf_op jit(solution)/shard_map/pairs/pallas_call | solution.py:185
  324.5 11.3 %pairs.3 = (f32[24,64,512]{2,1,0:T(8,128)}, bf16[20,512,512]{2,1,0:T(8,128)(2,1)}) custom-call(s32[2,20]{1,0:T(2,128)} %pad_add_fusion.items, s32[2]{0:T(128)} %pad_add_fusion.3.span, bf16[4,512,1024]{2,1,0:T(8,128)(2,1)} %bitcast.7.refs_0_.refs_5_, ...), custom_call_target="tpu_custom_call", output_to_operand_aliasing={{0}: (14, {}), {1}: (15, {})} | custom-call | tf_op jit(solution)/shard_map/pairs/pallas_call | solution.py:185
  335.8 2.1 convert.14
  338.0 1.9 collective-permute-start.14
  340.0 1.3 collective-permute-start.13
  341.4 0.9 collective-permute-start.11
  342.2 1.0 collective-permute-start.10
  343.2 1.9 slice.75.own
  345.1 2.1 collective-permute-done.14.refs_4_
  347.2 0.8 collective-permute-done.13.refs_3_
  348.0 1.9 collective-permute-done.12.refs_2_
  349.9 4.5 collective-permute-done.11.refs_1_
  355.1 0.7 copy-done.21
  355.8 2.7 gram.2
  358.8 1.1 collective-permute-done.15
  359.9 0.8 add.98
  360.7 1.5 collective-permute-start.16
  362.2 2.4 collective-permute-done.16
  364.6 1.9 collective-permute-start.17
  366.5 2.0 collective-permute-done.17
  368.5 2.3 collective-permute-start.18
  370.8 2.5 collective-permute-done.18
  373.9 8.3 %panel.2.refs_0_ = bf16[4,64,512]{2,1,0:T(8,128)(2,1)} custom-call(f32[64,64]{1,0:T(8,128)} %add.101.gram, f32[4,64,512]{2,1,0:T(8,128)} %get-tuple-element.17.y), custom_call_target="tpu_custom_call" | custom-call | tf_op jit(solution)/shard_map/panel/pallas_call | solution.py:330
  382.2 4.2 collective-permute-start.23
  386.5 1.3 collective-permute-start.22
  387.9 2.0 collective-permute-start.20
  390.5 3.8 collective-permute-done.23.refs_5_
  394.4 2.7 collective-permute-done.22.refs_4_
  397.1 5.2 %collective-permute-done.20.refs_2_ = bf16[4,64,512]{2,1,0:T(8,128)(2,1)S(1)} collective-permute-done((bf16[4,64,512]{2,1,0:T(8,128)(2,1)}, bf16[4,64,512]{2,1,0:T(8,128)(2,1)S(1)}, u32[]{:S(2)}, u32[]{:S(2)}) %collective-permute-start.20) | collective-permute-done | bytes 262176 | tf_op jit(solution)/shard_map/ppermute | solution.py:369
  403.0 8.0 %apply.1 = f32[24,64,512]{2,1,0:T(8,128)} custom-call(s32[2,20]{1,0:T(2,128)} %pad_add_fusion.items, s32[2]{0:T(128)} %pad_add_fusion.2.span, bf16[4,64,512]{2,1,0:T(8,128)(2,1)} %panel.2.refs_0_, bf16[4,64,512]{2,1,0:T(8,128)(2,1)} %copy-done.12, bf16[4,64,512]{2,1,0:T(8,128)(2,1)} %copy-done.11, bf16[4,64,512]{2,1,0:T(8,128)(2,1)} %copy-done.10, ...), custom_call_target="tpu_custom_call" | custom-call | tf_op jit(solution)/shard_map/apply/pallas_call | solution.py:243
  411.0 2.1 convert.15
  413.3 1.9 collective-permute-start.28
  415.2 2.6 collective-permute-start.27
  417.9 1.2 collective-permute-start.25
  419.7 1.9 slice.96.own
  421.6 6.4 %collective-permute-done.28.refs_4_ = bf16[4,64,512]{2,1,0:T(8,128)(2,1)S(1)} collective-permute-done((bf16[4,64,512]{2,1,0:T(8,128)(2,1)S(1)}, bf16[4,64,512]{2,1,0:T(8,128)(2,1)S(1)}, u32[]{:S(2)}, u32[]{:S(2)}) %collective-permute-start.28) | collective-permute-done | bytes 262176 | tf_op jit(solution)/shard_map/ppermute | solution.py:385
  428.1 3.5 collective-permute-done.25.refs_1_
  432.2 0.7 copy-done.22
  432.9 2.7 gram.3
  435.7 1.3 collective-permute-done.29
  437.0 0.8 add.102
  438.4 3.3 collective-permute-done.30
  441.7 0.8 collective-permute-start.31
  442.6 3.1 collective-permute-done.31
  445.6 3.5 collective-permute-start.32
  449.2 1.9 collective-permute-done.32
  451.7 8.4 %panel.3 = f32[64,2048]{1,0:T(8,128)} custom-call(f32[64,64]{1,0:T(8,128)} %add.105.gram, f32[4,64,512]{2,1,0:T(8,128)} %get-tuple-element.20.y), custom_call_target="tpu_custom_call" | custom-call | tf_op jit(solution)/shard_map/panel/pallas_call | solution.py:330
  (117 shorter events, 12.9 us)
Async XLA Ops:
  0.0 3.4 copy-start
  3.5 4.1 copy-start.6
  3.5 112.2 %copy-start.23 = (s32[15,2]{0,1:T(2,128)S(1)}, s32[15,2]{0,1:T(2,128)}, u32[]{:S(2)}) copy-start(s32[15,2]{0,1:T(2,128)} %param.7) | copy-start | bytes 364
  3.5 112.4 %copy-start.24 = (u32[32]{0:T(128)S(1)}, u32[32]{0:T(128)}, u32[]{:S(2)}) copy-start(u32[32]{0:T(128)} %constant.75) | copy-start | bytes 388
  6.3 298.2 %collective-permute-start.3 = (bf16[4,512,1024]{2,1,0:T(8,128)(2,1)}, bf16[4,512,1024]{2,1,0:T(8,128)(2,1)}, u32[]{:S(2)}, u32[]{:S(2)}) collective-permute-start(bf16[4,512,1024]{2,1,0:T(8,128)(2,1)} %bitcast.7.refs_0_.refs_5_), channel_id=1, source_target_pairs={{4,0},{5,1},{6,2},{7,3},{8,4},{9,5},{10,6},{11,7},{12,8},{13,9},{1... | collective-permute-start | bytes 12582920 | tf_op jit(solution)/shard_map/ppermute | solution.py:369
  7.6 303.1 %copy-start.1 = (bf16[8,4,8,512]{3,2,0,1:T(8,128)(2,1)}, bf16[8,4,8,512]{3,2,0,1:T(8,128)(2,1)S(1)}, u32[]{:S(2)}) copy-start(bf16[8,4,8,512]{3,2,0,1:T(8,128)(2,1)S(1)} %copy.46) | copy-start | bytes 786436
  7.6 99.9 %collective-permute-start.8 = (bf16[4,64,512]{2,1,0:T(8,128)(2,1)S(1)}, bf16[4,64,512]{2,1,0:T(8,128)(2,1)S(1)}, u32[]{:S(2)}, u32[]{:S(2)}) collective-permute-start(bf16[4,64,512]{2,1,0:T(8,128)(2,1)S(1)} %bitcast.31), channel_id=1, source_target_pairs={{4,0},{5,1},{6,2},{7,3},{8,4},{9,5},{10,6},{11,7},{12,8},{13,9},{1... | collective-permute-start | bytes 786440 | tf_op jit(solution)/shard_map/ppermute | solution.py:369
  8.9 98.9 %collective-permute-start.7 = (bf16[4,64,512]{2,1,0:T(8,128)(2,1)S(1)}, bf16[4,64,512]{2,1,0:T(8,128)(2,1)S(1)}, u32[]{:S(2)}, u32[]{:S(2)}) collective-permute-start(bf16[4,64,512]{2,1,0:T(8,128)(2,1)S(1)} %bitcast.32), channel_id=1, source_target_pairs={{0,3},{1,2},{2,1},{3,0},{4,7},{5,6},{6,5},{7,4},{8,11},{9,10},{10,... | collective-permute-start | bytes 786440 | tf_op jit(solution)/shard_map/ppermute | solution.py:369
  11.4 98.0 %collective-permute-start.6 = (bf16[4,64,512]{2,1,0:T(8,128)(2,1)S(1)}, bf16[4,64,512]{2,1,0:T(8,128)(2,1)S(1)}, u32[]{:S(2)}, u32[]{:S(2)}) collective-permute-start(bf16[4,64,512]{2,1,0:T(8,128)(2,1)S(1)} %bitcast.33), channel_id=1, source_target_pairs={{0,2},{1,3},{2,0},{3,1},{4,6},{5,7},{6,4},{7,5},{8,10},{9,11},{10,... | collective-permute-start | bytes 786440 | tf_op jit(solution)/shard_map/ppermute | solution.py:369
  12.0 97.4 %collective-permute-start.5 = (bf16[4,64,512]{2,1,0:T(8,128)(2,1)S(1)}, bf16[4,64,512]{2,1,0:T(8,128)(2,1)S(1)}, u32[]{:S(2)}, u32[]{:S(2)}) collective-permute-start(bf16[4,64,512]{2,1,0:T(8,128)(2,1)S(1)} %bitcast.34), channel_id=1, source_target_pairs={{0,1},{1,0},{2,3},{3,2},{4,5},{5,4},{6,7},{7,6},{8,9},{9,8},{10,11... | collective-permute-start | bytes 786440 | tf_op jit(solution)/shard_map/ppermute | solution.py:369
  107.6 203.2 %copy-start.2 = (bf16[4,64,512]{2,1,0:T(8,128)(2,1)}, bf16[4,64,512]{2,1,0:T(8,128)(2,1)S(1)}, u32[]{:S(2)}) copy-start(bf16[4,64,512]{2,1,0:T(8,128)(2,1)S(1)} %collective-permute-done.8.refs_10_) | copy-start | bytes 786436
  107.6 203.2 %collective-permute-start.2 = (bf16[4,512,1024]{2,1,0:T(8,128)(2,1)}, bf16[4,512,1024]{2,1,0:T(8,128)(2,1)}, u32[]{:S(2)}, u32[]{:S(2)}) collective-permute-start(bf16[4,512,1024]{2,1,0:T(8,128)(2,1)} %bitcast.7.refs_0_.refs_5_), channel_id=1, source_target_pairs={{0,3},{1,2},{2,1},{3,0},{4,7},{5,6},{6,5},{7,4},{8,11},{9,10},{10,... | collective-permute-start | bytes 12582920 | tf_op jit(solution)/shard_map/ppermute | solution.py:369
  107.8 203.0 %copy-start.3 = (bf16[4,64,512]{2,1,0:T(8,128)(2,1)}, bf16[4,64,512]{2,1,0:T(8,128)(2,1)S(1)}, u32[]{:S(2)}) copy-start(bf16[4,64,512]{2,1,0:T(8,128)(2,1)S(1)} %collective-permute-done.7.refs_9_) | copy-start | bytes 786436
  107.8 202.9 %collective-permute-start.1 = (bf16[4,512,1024]{2,1,0:T(8,128)(2,1)}, bf16[4,512,1024]{2,1,0:T(8,128)(2,1)}, u32[]{:S(2)}, u32[]{:S(2)}) collective-permute-start(bf16[4,512,1024]{2,1,0:T(8,128)(2,1)} %bitcast.7.refs_0_.refs_5_), channel_id=1, source_target_pairs={{0,2},{1,3},{2,0},{3,1},{4,6},{5,7},{6,4},{7,5},{8,10},{9,11},{10,... | collective-permute-start | bytes 12582920 | tf_op jit(solution)/shard_map/ppermute | solution.py:369
  109.4 201.4 %copy-start.4 = (bf16[4,64,512]{2,1,0:T(8,128)(2,1)}, bf16[4,64,512]{2,1,0:T(8,128)(2,1)S(1)}, u32[]{:S(2)}) copy-start(bf16[4,64,512]{2,1,0:T(8,128)(2,1)S(1)} %collective-permute-done.6.refs_8_) | copy-start | bytes 786436
  109.4 201.4 %collective-permute-start = (bf16[4,512,1024]{2,1,0:T(8,128)(2,1)}, bf16[4,512,1024]{2,1,0:T(8,128)(2,1)}, u32[]{:S(2)}, u32[]{:S(2)}) collective-permute-start(bf16[4,512,1024]{2,1,0:T(8,128)(2,1)} %bitcast.7.refs_0_.refs_5_), channel_id=1, source_target_pairs={{0,1},{1,0},{2,3},{3,2},{4,5},{5,4},{6,7},{7,6},{8,9},{9,8},{10,11... | collective-permute-start | bytes 12582920 | tf_op jit(solution)/shard_map/ppermute | solution.py:369
  109.5 201.3 %copy-start.5 = (bf16[4,64,512]{2,1,0:T(8,128)(2,1)}, bf16[4,64,512]{2,1,0:T(8,128)(2,1)S(1)}, u32[]{:S(2)}) copy-start(bf16[4,64,512]{2,1,0:T(8,128)(2,1)S(1)} %collective-permute-done.5.refs_7_) | copy-start | bytes 786436
  109.5 214.3 %collective-permute-start.4 = (bf16[4,512,1024]{2,1,0:T(8,128)(2,1)}, bf16[4,512,1024]{2,1,0:T(8,128)(2,1)}, u32[]{:S(2)}, u32[]{:S(2)}) collective-permute-start(bf16[4,512,1024]{2,1,0:T(8,128)(2,1)} %bitcast.7.refs_0_.refs_5_), channel_id=1, source_target_pairs={{0,8},{1,9},{2,10},{3,11},{4,12},{5,13},{6,14},{7,15},{12,0},{13,1... | collective-permute-start | bytes 12582920 | tf_op jit(solution)/shard_map/ppermute | solution.py:369
  304.5 19.3 %collective-permute-start.9 = (bf16[4,64,512]{2,1,0:T(8,128)(2,1)S(1)}, bf16[4,64,512]{2,1,0:T(8,128)(2,1)S(1)}, u32[]{:S(2)}, u32[]{:S(2)}) collective-permute-start(bf16[4,64,512]{2,1,0:T(8,128)(2,1)S(1)} %bitcast.35), channel_id=1, source_target_pairs={{0,8},{1,9},{2,10},{3,11},{4,12},{5,13},{6,14},{7,15},{12,0},{13,1... | collective-permute-start | bytes 786440 | tf_op jit(solution)/shard_map/ppermute | solution.py:369
  323.8 0.7 copy-start.7
  338.0 9.2 %collective-permute-start.14 = (bf16[4,64,512]{2,1,0:T(8,128)(2,1)S(1)}, bf16[4,64,512]{2,1,0:T(8,128)(2,1)S(1)}, u32[]{:S(2)}, u32[]{:S(2)}) collective-permute-start(bf16[4,64,512]{2,1,0:T(8,128)(2,1)S(1)} %get-tuple-element.34), channel_id=1, source_target_pairs={{8,0},{9,1},{10,2},{11,3},{12,4},{13,5},{14,6},{15,7},{0,12},{1,13... | collective-permute-start | bytes 786440 | tf_op jit(solution)/shard_map/ppermute | solution.py:385
  340.0 8.0 %collective-permute-start.13 = (bf16[4,64,512]{2,1,0:T(8,128)(2,1)S(1)}, bf16[4,64,512]{2,1,0:T(8,128)(2,1)S(1)}, u32[]{:S(2)}, u32[]{:S(2)}) collective-permute-start(bf16[4,64,512]{2,1,0:T(8,128)(2,1)S(1)} %get-tuple-element.35), channel_id=1, source_target_pairs={{0,4},{1,5},{2,6},{3,7},{4,8},{5,9},{6,10},{7,11},{8,12},{9,13},{1... | collective-permute-start | bytes 786440 | tf_op jit(solution)/shard_map/ppermute | solution.py:385
  341.3 8.6 %collective-permute-start.12 = (bf16[4,64,512]{2,1,0:T(8,128)(2,1)S(1)}, bf16[4,64,512]{2,1,0:T(8,128)(2,1)S(1)}, u32[]{:S(2)}, u32[]{:S(2)}) collective-permute-start(bf16[4,64,512]{2,1,0:T(8,128)(2,1)S(1)} %get-tuple-element.36), channel_id=1, source_target_pairs={{3,0},{2,1},{1,2},{0,3},{7,4},{6,5},{5,6},{4,7},{11,8},{10,9},{9,1... | collective-permute-start | bytes 786440 | tf_op jit(solution)/shard_map/ppermute | solution.py:385
  341.4 13.0 %collective-permute-start.11 = (bf16[4,64,512]{2,1,0:T(8,128)(2,1)S(1)}, bf16[4,64,512]{2,1,0:T(8,128)(2,1)S(1)}, u32[]{:S(2)}, u32[]{:S(2)}) collective-permute-start(bf16[4,64,512]{2,1,0:T(8,128)(2,1)S(1)} %get-tuple-element.37), channel_id=1, source_target_pairs={{2,0},{3,1},{0,2},{1,3},{6,4},{7,5},{4,6},{5,7},{10,8},{11,9},{8,1... | collective-permute-start | bytes 786440 | tf_op jit(solution)/shard_map/ppermute | solution.py:385
  342.2 12.1 %collective-permute-start.10 = (bf16[4,64,512]{2,1,0:T(8,128)(2,1)S(1)}, bf16[4,64,512]{2,1,0:T(8,128)(2,1)S(1)}, u32[]{:S(2)}, u32[]{:S(2)}) collective-permute-start(bf16[4,64,512]{2,1,0:T(8,128)(2,1)S(1)} %get-tuple-element.38), channel_id=1, source_target_pairs={{1,0},{0,1},{3,2},{2,3},{5,4},{4,5},{7,6},{6,7},{9,8},{8,9},{11,10... | collective-permute-start | bytes 786440 | tf_op jit(solution)/shard_map/ppermute | solution.py:385
  347.2 7.2 %copy-start.13 = (bf16[4,64,512]{2,1,0:T(8,128)(2,1)}, bf16[4,64,512]{2,1,0:T(8,128)(2,1)S(1)}, u32[]{:S(2)}) copy-start(bf16[4,64,512]{2,1,0:T(8,128)(2,1)S(1)} %collective-permute-done.14.refs_4_) | copy-start | bytes 786436
  348.0 6.4 %copy-start.15 = (bf16[4,64,512]{2,1,0:T(8,128)(2,1)}, bf16[4,64,512]{2,1,0:T(8,128)(2,1)S(1)}, u32[]{:S(2)}) copy-start(bf16[4,64,512]{2,1,0:T(8,128)(2,1)S(1)} %collective-permute-done.13.refs_3_) | copy-start | bytes 786436
  349.9 4.5 copy-start.17
  354.4 0.7 copy-start.19
  355.1 0.7 copy-start.21
  358.4 1.5 collective-permute-start.15
  360.7 3.9 collective-permute-start.16
  364.6 3.9 collective-permute-start.17
  368.5 4.8 %collective-permute-start.18 = (f32[64,64]{1,0:T(8,128)S(1)}, f32[64,64]{1,0:T(8,128)S(1)}, u32[]{:S(2)}, u32[]{:S(2)}) collective-permute-start(f32[64,64]{1,0:T(8,128)S(1)} %add.100), channel_id=1, source_target_pairs={{0,8},{1,9},{2,10},{3,11},{4,12},{5,13},{6,14},{7,15},{8,0},{9,1},... | collective-permute-start | bytes 49160 | tf_op jit(solution)/shard_map/ppermute | solution.py:348
  382.2 12.1 %collective-permute-start.23 = (bf16[4,64,512]{2,1,0:T(8,128)(2,1)}, bf16[4,64,512]{2,1,0:T(8,128)(2,1)S(1)}, u32[]{:S(2)}, u32[]{:S(2)}) collective-permute-start(bf16[4,64,512]{2,1,0:T(8,128)(2,1)} %panel.2.refs_0_), channel_id=1, source_target_pairs={{0,8},{1,9},{2,10},{3,11},{4,12},{5,13},{6,14},{7,15},{12,0},{13,1... | collective-permute-start | bytes 786440 | tf_op jit(solution)/shard_map/ppermute | solution.py:369
  386.5 10.6 %collective-permute-start.22 = (bf16[4,64,512]{2,1,0:T(8,128)(2,1)}, bf16[4,64,512]{2,1,0:T(8,128)(2,1)S(1)}, u32[]{:S(2)}, u32[]{:S(2)}) collective-permute-start(bf16[4,64,512]{2,1,0:T(8,128)(2,1)} %panel.2.refs_0_), channel_id=1, source_target_pairs={{4,0},{5,1},{6,2},{7,3},{8,4},{9,5},{10,6},{11,7},{12,8},{13,9},{1... | collective-permute-start | bytes 786440 | tf_op jit(solution)/shard_map/ppermute | solution.py:369
  387.8 9.3 %collective-permute-start.21 = (bf16[4,64,512]{2,1,0:T(8,128)(2,1)}, bf16[4,64,512]{2,1,0:T(8,128)(2,1)S(1)}, u32[]{:S(2)}, u32[]{:S(2)}) collective-permute-start(bf16[4,64,512]{2,1,0:T(8,128)(2,1)} %panel.2.refs_0_), channel_id=1, source_target_pairs={{0,3},{1,2},{2,1},{3,0},{4,7},{5,6},{6,5},{7,4},{8,11},{9,10},{10,... | collective-permute-start | bytes 786440 | tf_op jit(solution)/shard_map/ppermute | solution.py:369
  387.9 14.4 %collective-permute-start.20 = (bf16[4,64,512]{2,1,0:T(8,128)(2,1)}, bf16[4,64,512]{2,1,0:T(8,128)(2,1)S(1)}, u32[]{:S(2)}, u32[]{:S(2)}) collective-permute-start(bf16[4,64,512]{2,1,0:T(8,128)(2,1)} %panel.2.refs_0_), channel_id=1, source_target_pairs={{0,2},{1,3},{2,0},{3,1},{4,6},{5,7},{6,4},{7,5},{8,10},{9,11},{10,... | collective-permute-start | bytes 786440 | tf_op jit(solution)/shard_map/ppermute | solution.py:369
  389.9 12.4 %collective-permute-start.19 = (bf16[4,64,512]{2,1,0:T(8,128)(2,1)}, bf16[4,64,512]{2,1,0:T(8,128)(2,1)S(1)}, u32[]{:S(2)}, u32[]{:S(2)}) collective-permute-start(bf16[4,64,512]{2,1,0:T(8,128)(2,1)} %panel.2.refs_0_), channel_id=1, source_target_pairs={{0,1},{1,0},{2,3},{3,2},{4,5},{5,4},{6,7},{7,6},{8,9},{9,8},{10,11... | collective-permute-start | bytes 786440 | tf_op jit(solution)/shard_map/ppermute | solution.py:369
  394.4 7.9 %copy-start.8 = (bf16[4,64,512]{2,1,0:T(8,128)(2,1)}, bf16[4,64,512]{2,1,0:T(8,128)(2,1)S(1)}, u32[]{:S(2)}) copy-start(bf16[4,64,512]{2,1,0:T(8,128)(2,1)S(1)} %collective-permute-done.23.refs_5_) | copy-start | bytes 786436
  397.0 5.2 %copy-start.9 = (bf16[4,64,512]{2,1,0:T(8,128)(2,1)}, bf16[4,64,512]{2,1,0:T(8,128)(2,1)S(1)}, u32[]{:S(2)}) copy-start(bf16[4,64,512]{2,1,0:T(8,128)(2,1)S(1)} %collective-permute-done.22.refs_4_) | copy-start | bytes 786436
  397.1 5.2 %copy-start.10 = (bf16[4,64,512]{2,1,0:T(8,128)(2,1)}, bf16[4,64,512]{2,1,0:T(8,128)(2,1)S(1)}, u32[]{:S(2)}) copy-start(bf16[4,64,512]{2,1,0:T(8,128)(2,1)S(1)} %collective-permute-done.21.refs_3_) | copy-start | bytes 786436
  402.3 0.7 copy-start.11
  402.3 0.8 copy-start.12
  413.3 14.8 %collective-permute-start.28 = (bf16[4,64,512]{2,1,0:T(8,128)(2,1)S(1)}, bf16[4,64,512]{2,1,0:T(8,128)(2,1)S(1)}, u32[]{:S(2)}, u32[]{:S(2)}) collective-permute-start(bf16[4,64,512]{2,1,0:T(8,128)(2,1)S(1)} %get-tuple-element.29), channel_id=1, source_target_pairs={{8,0},{9,1},{10,2},{11,3},{12,4},{13,5},{14,6},{15,7},{0,12},{1,13... | collective-permute-start | bytes 786440 | tf_op jit(solution)/shard_map/ppermute | solution.py:385
  415.2 12.8 %collective-permute-start.27 = (bf16[4,64,512]{2,1,0:T(8,128)(2,1)S(1)}, bf16[4,64,512]{2,1,0:T(8,128)(2,1)S(1)}, u32[]{:S(2)}, u32[]{:S(2)}) collective-permute-start(bf16[4,64,512]{2,1,0:T(8,128)(2,1)S(1)} %get-tuple-element.30), channel_id=1, source_target_pairs={{0,4},{1,5},{2,6},{3,7},{4,8},{5,9},{6,10},{7,11},{8,12},{9,13},{1... | collective-permute-start | bytes 786440 | tf_op jit(solution)/shard_map/ppermute | solution.py:385
  417.8 10.2 %collective-permute-start.26 = (bf16[4,64,512]{2,1,0:T(8,128)(2,1)S(1)}, bf16[4,64,512]{2,1,0:T(8,128)(2,1)S(1)}, u32[]{:S(2)}, u32[]{:S(2)}) collective-permute-start(bf16[4,64,512]{2,1,0:T(8,128)(2,1)S(1)} %get-tuple-element.31), channel_id=1, source_target_pairs={{3,0},{2,1},{1,2},{0,3},{7,4},{6,5},{5,6},{4,7},{11,8},{10,9},{9,1... | collective-permute-start | bytes 786440 | tf_op jit(solution)/shard_map/ppermute | solution.py:385
  417.9 13.6 %collective-permute-start.25 = (bf16[4,64,512]{2,1,0:T(8,128)(2,1)S(1)}, bf16[4,64,512]{2,1,0:T(8,128)(2,1)S(1)}, u32[]{:S(2)}, u32[]{:S(2)}) collective-permute-start(bf16[4,64,512]{2,1,0:T(8,128)(2,1)S(1)} %get-tuple-element.32), channel_id=1, source_target_pairs={{2,0},{3,1},{0,2},{1,3},{6,4},{7,5},{4,6},{5,7},{10,8},{11,9},{8,1... | collective-permute-start | bytes 786440 | tf_op jit(solution)/shard_map/ppermute | solution.py:385
  419.1 12.4 %collective-permute-start.24 = (bf16[4,64,512]{2,1,0:T(8,128)(2,1)S(1)}, bf16[4,64,512]{2,1,0:T(8,128)(2,1)S(1)}, u32[]{:S(2)}, u32[]{:S(2)}) collective-permute-start(bf16[4,64,512]{2,1,0:T(8,128)(2,1)S(1)} %get-tuple-element.33), channel_id=1, source_target_pairs={{1,0},{0,1},{3,2},{2,3},{5,4},{4,5},{7,6},{6,7},{9,8},{8,9},{11,10... | collective-permute-start | bytes 786440 | tf_op jit(solution)/shard_map/ppermute | solution.py:385
  428.1 3.5 copy-start.14
  428.1 3.5 copy-start.16
  428.1 3.5 copy-start.18
  431.5 0.7 copy-start.20
  432.2 0.7 copy-start.22
  435.6 1.4 collective-permute-start.29
  437.8 3.9 collective-permute-start.30
  441.7 3.9 collective-permute-start.31
  445.6 5.4 %collective-permute-start.32 = (f32[64,64]{1,0:T(8,128)S(1)}, f32[64,64]{1,0:T(8,128)S(1)}, u32[]{:S(2)}, u32[]{:S(2)}) collective-permute-start(f32[64,64]{1,0:T(8,128)S(1)} %add.104), channel_id=1, source_target_pairs={{0,8},{1,9},{2,10},{3,11},{4,12},{5,13},{6,14},{7,15},{8,0},{9,1},... | collective-permute-start | bytes 49160 | tf_op jit(solution)/shard_map/ppermute | solution.py:348

commit v2 on v1

v2 whole, which is shorter than its diff:
```python
import functools

import jax
import jax.numpy as jnp
import numpy as np
from jax import lax
from jax.experimental import pallas as pl
from jax.experimental.pallas import tpu as pltpu
from jax.sharding import PartitionSpec as P

BLOCK = 512
ITERS = 2
REACH = 7
SHARPNESS = 24.0
LOG2E = 1.4426950408889634
VMEM_LIMIT = 32 * 1024 * 1024


def make_plan(count):
    if count == 16:
        moves = [[(i, i ^ m) for i in range(count)] for m in (1, 2, 3)]
        moves.append([(i, i - 4) for i in range(4, count)])
        moves.append([(i, i + 8) for i in range(8)])
        moves.append([(i, i - 12) for i in range(12, 16)])
        late = {5, 6}
        after = {6: 4}
        joint = [[1], [2], [3], [4], [5, 6]]
    else:
        moves = [[(i, (i - o) % count) for i in range(count)] for o in range(1, REACH + 1)]
        late = {5, 6, 7}
        after = {6: 1, 7: 2}
        joint = [[m] for m in range(1, REACH + 1)]
    hold = -np.ones((count, len(moves) + 1), np.int32)
    hold[:, 0] = np.arange(count)
    for m, pairs in enumerate(moves):
        for source, target in pairs:
            hold[target, m + 1] = source
    work = np.zeros((count, count, count), bool)
    load = np.zeros(count, np.int32)
    for row in range(count):
        for col in range(count):
            gap = min((row - col) % count, (col - row) % count)
            if gap > REACH:
                continue
            able = [w for w in range(count) if row in hold[w] and col in hold[w]]
            pick = row if row in able else col if col in able else min(able, key=lambda w: load[w])
            work[pick, row, col] = True
            load[pick] += 1
    place = -np.ones((count, count), np.int32)
    for w in range(count):
        for s, device in enumerate(hold[w]):
            if device >= 0:
                place[w, device] = s
    return moves, joint, hold, place, work, late, after, int(load.max())


def work_list(lists, hold, place, work, late, slots, blocks_here, top, me):
    count, held = hold.shape
    allowed = np.zeros((count, held, count), np.int32)
    for w in range(count):
        for s in range(held):
            if hold[w, s] >= 0 and place[w, hold[w, s]] == s:
                allowed[w, s] = np.where(work[w, hold[w, s]], place[w] + 1, 0)
    mine = lax.dynamic_index_in_dim(jnp.asarray(allowed), me, 0, keepdims=False)
    pairs = lists[:, : 2 * slots].reshape(held, slots, 2)
    live = jnp.arange(slots, dtype=jnp.int32)[None, :] < lists[:, 2 * slots :]
    col_owner = pairs[:, :, 1] // blocks_here
    is_col = col_owner[:, :, None] == jnp.arange(count, dtype=jnp.int32)
    col_place = jnp.sum(jnp.where(is_col, mine[:, None, :], 0), axis=2) - 1
    valid = jnp.logical_and(live, col_place >= 0)
    row_place = jnp.broadcast_to(jnp.arange(held, dtype=jnp.int32)[:, None], col_place.shape)
    is_late = functools.reduce(
        jnp.logical_or, [jnp.logical_or(row_place == s, col_place == s) for s in sorted(late)]
    )
    row_held = (row_place * blocks_here + pairs[:, :, 0] % blocks_here).reshape(-1)
    col_held = (col_place * blocks_here + pairs[:, :, 1] % blocks_here).reshape(-1)
    first = jnp.logical_and(valid, jnp.logical_not(is_late)).reshape(-1).astype(jnp.int32)
    second = jnp.logical_and(valid, is_late).reshape(-1).astype(jnp.int32)
    total = first.shape[0]
    before = jnp.arange(total)[:, None] < jnp.arange(total)[None, :]
    first_rank = jnp.sum(jnp.where(before, first[:, None], 0), axis=0)
    second_rank = jnp.sum(jnp.where(before, second[:, None], 0), axis=0)
    n_first, n_second = jnp.sum(first), jnp.sum(second)
    rank = jnp.where(first > 0, first_rank, jnp.where(second > 0, n_first + second_rank, total))
    chosen = rank[None, :] == jnp.arange(top, dtype=jnp.int32)[:, None]
    rows = jnp.sum(jnp.where(chosen, row_held[None, :], 0), axis=1)
    cols = jnp.sum(jnp.where(chosen, col_held[None, :], 0), axis=1)
    zero = jnp.zeros((), jnp.int32)
    return jnp.stack([rows, cols]), jnp.stack([zero, n_first]), jnp.stack([n_first, n_first + n_second])


def pack_kernel(rows, panel, out, buf, in_sem, out_sem):
    count, depth = rows.shape
    blocks = count // BLOCK
    per_row = depth // BLOCK
    high = panel.shape[0] // per_row
    step = 64
    loads = [
        pltpu.make_async_copy(rows.at[pl.ds(b * BLOCK, BLOCK)], buf.at[pl.ds(b * BLOCK, BLOCK)], in_sem.at[b])
        for b in range(blocks)
    ]
    for load in loads:
        load.start()
    for b in range(blocks):
        for q in range(per_row):
            buf[pl.ds(count + b * high, high), q * BLOCK : (q + 1) * BLOCK] = panel[
                q * high : (q + 1) * high, b * BLOCK : (b + 1) * BLOCK
            ].astype(jnp.bfloat16)
    stores = [(count, blocks * high)] + [(b * BLOCK, BLOCK) for b in range(blocks)]
    stores = [
        pltpu.make_async_copy(buf.at[pl.ds(at, size)], out.at[pl.ds(at, size)], out_sem.at[n])
        for n, (at, size) in enumerate(stores)
    ]
    stores[0].start()
    for b in range(blocks):
        loads[b].wait()

        @pl.loop(0, BLOCK // step, unroll=2)
        def _(i):
            at = pl.ds(pl.multiple_of(b * BLOCK + i * step, step), step)
            values = buf[at, :].astype(jnp.float32)
            mean = jnp.sum(values * values, axis=-1, keepdims=True) * (1.0 / depth)
            factor = lax.rsqrt(mean + 1e-06) * depth ** (-0.5)
            buf[at, :] = (values * factor).astype(jnp.bfloat16)

        stores[b + 1].start()
    for store in stores:
        store.wait()


def pack_call(embeddings, panel):
    rows, depth = embeddings.shape
    blocks = rows // BLOCK
    tall = rows + panel.shape[0] * panel.shape[1] // depth
    return pl.pallas_call(
        pack_kernel,
        out_shape=jax.ShapeDtypeStruct((tall, depth), jnp.bfloat16),
        in_specs=[pl.BlockSpec(memory_space=pltpu.HBM), pl.BlockSpec(memory_space=pltpu.VMEM)],
        out_specs=pl.BlockSpec(memory_space=pltpu.HBM),
        scratch_shapes=[
            pltpu.VMEM((tall, depth), jnp.bfloat16),
            pltpu.SemaphoreType.DMA((blocks,)),
            pltpu.SemaphoreType.DMA((blocks + 1,)),
        ],
        compiler_params=pltpu.CompilerParams(vmem_limit_bytes=VMEM_LIMIT),
        name="pack",
    )(embeddings, panel)


def fill_panel(refs, columns, at, pan, sem):
    per_row = pan.shape[0]
    copies = []
    for ref, s in zip(refs, columns):
        size = ref.shape[0] - at
        for q in range(per_row):
            source = ref.at[pl.ds(at, size), pl.ds(q * BLOCK, BLOCK)]
            copies.append(
                pltpu.make_async_copy(source, pan.at[q, pl.ds(s * size, size)], sem.at[len(copies)])
            )
    for copy in copies:
        copy.start()
    return copies


def panel_of(pan, block, high):
    at = pl.ds(pl.multiple_of(block * high, high), high)
    return jnp.concatenate([pan[q, at] for q in range(pan.shape[0])], axis=0)


def add_products(pan, acc, aff, row, col):
    high = acc.shape[1] // pan.shape[0]
    forward = lax.dot_general(
        panel_of(pan, col, high), aff, (((1,), (1,)), ((), ())), preferred_element_type=jnp.float32
    )
    mirror = lax.dot_general(
        panel_of(pan, row, high), aff, (((1,), (0,)), ((), ())), preferred_element_type=jnp.float32
    )
    acc[row] += forward
    acc[col] += mirror


def write_sums(acc, joint, own, backs):
    per = own.shape[0]
    own[...] = acc[pl.ds(0, per)]
    for columns, back in zip(joint, backs):
        back[...] = sum(acc[pl.ds(s * per, per)] for s in columns).astype(jnp.bfloat16)


def pair_kernel(columns, fresh, joint, per, first, final, items, span, *refs):
    n_unit = len(columns)
    units, refs = refs[:n_unit], refs[n_unit:]
    if not first:
        acc_in, pan_in, _, refs = refs[0], refs[1], refs[2], refs[3:]
    if final:
        own, refs = refs[0], refs[1:]
        backs, refs = refs[: len(joint)], refs[len(joint) :]
        aff_out, acc, pan, refs = refs[0], refs[1], refs[2], refs[3:]
    else:
        acc, pan, aff_out, refs = refs[0], refs[1], refs[2], refs[3:]
    ubuf, affbuf, usem, psem, asem = refs
    begin, end = span[0], span[1]

    def rows_of(ref, block):
        return ref.at[pl.ds(pl.multiple_of(block * BLOCK, BLOCK), BLOCK)]

    def fetch(i, slot):
        for side in range(2):
            held = items[side, i]
            for s, ref in zip(columns, units):

                @pl.when(held // per == s)
                def _():
                    pltpu.make_async_copy(rows_of(ref, held % per), ubuf.at[slot, side], usem.at[slot, side]).start()

    def store(i, slot):
        return pltpu.make_async_copy(affbuf.at[slot], aff_out.at[i], asem.at[slot])

    @pl.when(begin < end)
    def _():
        fetch(begin, begin % 2)

    if first:
        acc[...] = jnp.zeros_like(acc)
    else:
        acc[...] = acc_in[...]
        pan[...] = pan_in[...]
    for copy in fill_panel(units[fresh:], columns[fresh:], per * BLOCK, pan, psem):
        copy.wait()

    @pl.loop(begin, end)
    def _(i):
        slot = i % 2

        @pl.when(i + 1 < end)
        def _():
            fetch(i + 1, 1 - slot)

        for side in range(2):
            pltpu.make_async_copy(rows_of(units[0], 0), ubuf.at[slot, side], usem.at[slot, side]).wait()

        @pl.when(i >= begin + 2)
        def _():
            store(i - 2, slot).wait()

        half = BLOCK // 2
        halves = []
        for part in range(2):
            scores = lax.dot_general(
                ubuf[slot, 0, pl.ds(part * half, half), :],
                ubuf[slot, 1],
                (((1,), (1,)), ((), ())),
                preferred_element_type=jnp.float32,
            )
            power = scores * (SHARPNESS * LOG2E)
            halves.append((jnp.exp2(power - 1.0) - jnp.exp2(-1.0 - power)).astype(jnp.bfloat16))
        aff = jnp.concatenate(halves, axis=0)
        affbuf[slot] = aff
        store(i, slot).start()
        add_products(pan, acc, aff, items[0, i], items[1, i])

    for back in (2, 1):

        @pl.when(end - back >= begin)
        def _():
            store(end - back, (end - back) % 2).wait()

    if final:
        write_sums(acc, joint, own, backs)


def sum_shapes(sends, per, width):
    return [jax.ShapeDtypeStruct((per, width, BLOCK), jnp.float32)] + [
        jax.ShapeDtypeStruct((per, width, BLOCK), jnp.bfloat16)
    ] * sends


def pair_call(items, span, units, columns, fresh, joint, per, width, top, state, final):
    blocks = (1 + sum(len(group) for group in joint)) * per
    depth = units[0].shape[1]
    per_row = depth // BLOCK
    smem = pl.BlockSpec(memory_space=pltpu.SMEM)
    anywhere = pl.BlockSpec(memory_space=pltpu.HBM)
    vmem = pl.BlockSpec(memory_space=pltpu.VMEM)
    operands = [items, span, *units]
    in_specs = [smem, smem] + [anywhere] * len(units)
    acc_shape = (blocks, width, BLOCK)
    pan_shape = (per_row, blocks * width // per_row, BLOCK)
    aff_shape = jax.ShapeDtypeStruct((top, BLOCK, BLOCK), jnp.bfloat16)
    scratch = [
        pltpu.VMEM((2, 2, BLOCK, depth), jnp.bfloat16),
        pltpu.VMEM((2, BLOCK, BLOCK), jnp.bfloat16),
        pltpu.SemaphoreType.DMA((2, 2)),
        pltpu.SemaphoreType.DMA((len(units) * per_row,)),
        pltpu.SemaphoreType.DMA((2,)),
    ]
    if final:
        out_shape = sum_shapes(len(joint), per, width) + [aff_shape]
        out_specs = [vmem] * (1 + len(joint)) + [anywhere]
        scratch = [pltpu.VMEM(acc_shape, jnp.float32), pltpu.VMEM(pan_shape, jnp.bfloat16)] + scratch
    else:
        out_shape = [
            jax.ShapeDtypeStruct(acc_shape, jnp.float32),
            jax.ShapeDtypeStruct(pan_shape, jnp.bfloat16),
            aff_shape,
        ]
        out_specs = [vmem, vmem, anywhere]
    aliases = {}
    if state is not None:
        aliases = {len(operands) + 2: len(out_shape) - 1}
        operands += list(state)
        in_specs += [vmem, vmem, anywhere]
    return pl.pallas_call(
        functools.partial(pair_kernel, columns, fresh, joint, per, state is None, final),
        out_shape=out_shape,
        in_specs=in_specs,
        out_specs=out_specs,
        scratch_shapes=scratch,
        input_output_aliases=aliases,
        compiler_params=pltpu.CompilerParams(vmem_limit_bytes=VMEM_LIMIT),
        name="pairs",
    )(*operands)


def apply_kernel(joint, items, span, *refs):
    n_panel = len(joint) + 1
    panels, refs = refs[:n_panel], refs[n_panel:]
    aff_in, own, backs, refs = refs[0], refs[1], refs[2 : n_panel + 1], refs[n_panel + 1 :]
    acc, pan, affbuf, psem, asem = refs
    end = span[1]

    def load(i, slot):
        return pltpu.make_async_copy(aff_in.at[i], affbuf.at[slot], asem.at[slot])

    for ahead in range(3):

        @pl.when(ahead < end)
        def _():
            load(ahead, ahead).start()

    spots = [(panels[0], 0)] + [(ref, s) for ref, group in zip(panels[1:], joint) for s in group]
    copies = fill_panel([ref for ref, _ in spots], [s for _, s in spots], 0, pan, psem)
    acc[...] = jnp.zeros_like(acc)
    for copy in copies:
        copy.wait()

    @pl.loop(0, end)
    def _(i):
        slot = i % 4

        @pl.when(i + 3 < end)
        def _():
            load(i + 3, (i + 3) % 4).start()

        load(i, slot).wait()
        add_products(pan, acc, affbuf[slot], items[0, i], items[1, i])

    write_sums(acc, joint, own, backs)


def apply_call(items, span, panels, joint, aff, per, width):
    held = 1 + sum(len(group) for group in joint)
    blocks = held * per
    per_row = panels[0].shape[1] // BLOCK
    smem = pl.BlockSpec(memory_space=pltpu.SMEM)
    anywhere = pl.BlockSpec(memory_space=pl.ANY)
    return pl.pallas_call(
        functools.partial(apply_kernel, joint),
        out_shape=sum_shapes(len(joint), per, width),
        in_specs=[smem, smem] + [anywhere] * len(panels) + [pl.BlockSpec(memory_space=pltpu.HBM)],
        out_specs=[pl.BlockSpec(memory_space=pltpu.VMEM)] * len(panels),
        scratch_shapes=[
            pltpu.VMEM((blocks, width, BLOCK), jnp.float32),
            pltpu.VMEM((per_row, blocks * width // per_row, BLOCK), jnp.bfloat16),
            pltpu.VMEM((4, BLOCK, BLOCK), jnp.bfloat16),
            pltpu.SemaphoreType.DMA((held * per_row,)),
            pltpu.SemaphoreType.DMA((4,)),
        ],
        compiler_params=pltpu.CompilerParams(vmem_limit_bytes=VMEM_LIMIT),
        name="apply",
    )(items, span, *panels, aff)


def gram_kernel(n_back, own, *refs):
    backs, (y_out, gram_out) = refs[:n_back], refs[n_back:]
    gram = None
    for b in range(own.shape[0]):
        total = own[b]
        for back in backs:
            total = total + back[b].astype(jnp.float32)
        y_out[b] = total
        part = lax.dot_general(
            total,
            total,
            (((1,), (1,)), ((), ())),
            preferred_element_type=jnp.float32,
            precision=lax.Precision.HIGHEST,
        )
        gram = part if gram is None else gram + part
    gram_out[...] = gram


def gram_call(own, backs):
    width = own.shape[1]
    return pl.pallas_call(
        functools.partial(gram_kernel, len(backs)),
        out_shape=(
            jax.ShapeDtypeStruct(own.shape, jnp.float32),
            jax.ShapeDtypeStruct((width, width), jnp.float32),
        ),
        compiler_params=pltpu.CompilerParams(vmem_limit_bytes=VMEM_LIMIT),
        name="gram",
    )(own, *backs)


def inverse_factor(gram):
    width = gram.shape[0]
    row_id = lax.broadcasted_iota(jnp.int32, (width, width), 0)
    col_id = lax.broadcasted_iota(jnp.int32, (width, width), 1)
    table = jnp.concatenate([gram, (row_id == col_id).astype(jnp.float32)], axis=1)
    below = lax.broadcasted_iota(jnp.int32, (width, 1), 0)
    scale = jnp.zeros((width, 1), jnp.float32)
    for k in range(width):
        line = table[k : k + 1, :]
        pivot = table[k : k + 1, k : k + 1]
        scale = jnp.where(below == k, pivot, scale)
        factor = jnp.where(below > k, table[:, k : k + 1] / pivot, 0.0)
        table = table - factor * line
    return table[:, width:] / jnp.sqrt(scale)


def panel_kernel(rows_all, last, n_gram, *refs):
    grams, (y, out) = refs[:n_gram], refs[n_gram:]
    gram = grams[0][...]
    for other in grams[1:]:
        gram = gram + other[...]
    inverse = inverse_factor(gram * (1.0 / rows_all))
    for b in range(y.shape[0]):
        block = lax.dot_general(
            inverse,
            y[b],
            (((1,), (0,)), ((), ())),
            preferred_element_type=jnp.float32,
            precision=lax.Precision.HIGHEST,
        )
        if last:
            out[:, b * BLOCK : (b + 1) * BLOCK] = block
        else:
            per_row = out.shape[1] // BLOCK
            high = block.shape[0] // per_row
            for q in range(per_row):
                out[b * high : (b + 1) * high, q * BLOCK : (q + 1) * BLOCK] = block[
                    q * high : (q + 1) * high
                ].astype(jnp.bfloat16)


def panel_call(grams, y, rows_all, depth, last):
    blocks, width, _ = y.shape
    shape = (
        jax.ShapeDtypeStruct((width, blocks * BLOCK), jnp.float32)
        if last
        else jax.ShapeDtypeStruct((width * blocks * BLOCK // depth, depth), jnp.bfloat16)
    )
    return pl.pallas_call(
        functools.partial(panel_kernel, rows_all, last, len(grams)),
        out_shape=shape,
        compiler_params=pltpu.CompilerParams(vmem_limit_bytes=VMEM_LIMIT),
        name="panel",
    )(*grams, y)


def sum_over_rows(value):
    count = lax.axis_size("rows")
    terms, step = [value], 1
    while step < count:
        value = functools.reduce(jnp.add, terms)
        radix = min(4, count // step)
        terms = [value] + [
            lax.ppermute(value, "rows", [(i, i ^ (step * m)) for i in range(count)]) for m in range(1, radix)
        ]
        step *= radix
    return terms


def on_device(embeddings, block_pairs, pair_count, start_panel):
    count = lax.axis_size("rows")
    me = lax.axis_index("rows")
    depth = embeddings.shape[1]
    per = embeddings.shape[0] // BLOCK
    width = start_panel.shape[0]
    slots = block_pairs.shape[0]
    moves, joint, hold, place, work, late, after, top = make_plan(count)
    held = len(moves) + 1

    own_list = jnp.concatenate([block_pairs.reshape(-1), pair_count])
    merged = [functools.reduce(list.__add__, [moves[s - 1] for s in group]) for group in joint]
    lists = [own_list]
    for group, pairs in zip(joint, merged):
        lists += [lax.ppermute(own_list, "rows", pairs)] * len(group)
    lists = jnp.stack(lists)
    packed = pack_call(embeddings, start_panel)
    packed, lists = lax.optimization_barrier((packed, lists))
    units = {0: packed}
    for m, pairs in enumerate(moves, 1):
        outgoing = packed
        if m in after:
            outgoing, _ = lax.optimization_barrier((packed, units[after[m]]))
        units[m] = lax.ppermute(outgoing, "rows", pairs)
    items, span_first, span_second = work_list(lists, hold, place, work, late, slots, per, top, me)
    span_all = jnp.stack([span_first[0], span_second[1]])

    early = [s for s in range(held) if s not in late]
    order = early + sorted(late)
    state = pair_call(items, span_first, [units[s] for s in early], early, 0, joint, per, width, top, None, False)
    *sums, aff = pair_call(
        items, span_second, [units[s] for s in order], order, len(early), joint, per, width, top, state, True
    )

    for sweep in range(ITERS):
        if sweep > 0:
            panels = [panel] + [lax.ppermute(panel, "rows", pairs) for pairs in merged]
            sums = apply_call(items, span_all, panels, joint, aff, per, width)
        backs = [
            lax.ppermute(sums[m], "rows", [(target, source) for source, target in pairs])
            for m, pairs in enumerate(merged, 1)
        ]
        y, gram = gram_call(sums[0], backs)
        grams = sum_over_rows(gram)
        panel = panel_call(grams, y, count * embeddings.shape[0], depth, sweep == ITERS - 1)
    return panel


def solution(mesh):
    in_specs = (
        P(("groups", "rows"), None),
        P(("groups", "rows"), None),
        P(("groups", "rows")),
        P(None, ("groups", "rows")),
    )
    out_specs = P(None, ("groups", "rows"))
    return jax.shard_map(on_device, mesh=mesh, in_specs=in_specs, out_specs=out_specs, check_vma=False)
```

time: 467 us -> 361 us (0.77)
  blocking collectives: 179 us -> 0 us
  waiting for transfers between devices: 144 us -> 234 us
  other arithmetic: 20.8 us -> 3.72 us
  Pallas kernels: 54.2 us -> 46.4 us
  starting transfers between devices: 47 us -> 54 us
    unnamed x1 -> x0, blocking collectives: 179 us -> none
    ppermute x33 -> x38, waiting for transfers between devices: 144 us -> 234 us  [the longest x6 185 us: on_device(): units[m] = lax.ppermute(outgoing, 'rows', pairs)]
    unnamed x54 -> x11, local copies, waits for them, and re-layouts: 5.16 us -> 12.3 us
    ppermute x33 -> x38, starting transfers between devices: 47 us -> 54 us  [the longest x12 12.8 us: sum_over_rows(): lax.ppermute(value, 'rows', [(i, i ^ step * m) for i in range(count)])]
    pallas_call x5 -> x6, Pallas kernels: 48.9 us -> 45.2 us  [the longest x2 20.9 us: pair_call(): pl.pallas_call(functools.partial(pair_kernel, columns, fresh, joint, per,...]
  transfers between devices with their start and end apart: 33 -> 38, of which waited for: 18 -> 19; matrix products, arithmetic and copies ran while one was open for 3% -> 2% of each run, Pallas kernels for 3% -> 4%
where the time goes in v2:
time: 361 us; the launch traced here: 355 us
  waiting for transfers between devices  234 us (65%)
  starting transfers between devices  54 us (15%)
  Pallas kernels  46.4 us (13%)
  local copies, waits for them, and re-layouts  14.2 us (4%)
  other arithmetic  3.72 us (1%)
    ppermute x6, waiting for transfers between devices, on_device(): units[m] = lax.ppermute(outgoing, 'rows', pairs)  185 us
    ppermute x10, waiting for transfers between devices, on_device(): lax.ppermute(sums[m], 'rows', [(target, source) for source, target in pai...  28.1 us
    pallas_call x2, Pallas kernels, pair_call(): pl.pallas_call(functools.partial(pair_kernel, columns, fresh, joint, per,...  20.9 us
    pallas_call x2, Pallas kernels, panel_call(): pl.pallas_call(functools.partial(panel_kernel, rows_all, last, len(grams)...  13.9 us
    ppermute x12, starting transfers between devices, sum_over_rows(): lax.ppermute(value, 'rows', [(i, i ^ step * m) for i in range(count)])  12.8 us
    ppermute x10, starting transfers between devices, on_device(): lax.ppermute(sums[m], 'rows', [(target, source) for source, target in pai...  12.4 us
    unnamed x11, local copies, waits for them, and re-layouts  12.3 us
    ppermute x6, starting transfers between devices, on_device(): units[m] = lax.ppermute(outgoing, 'rows', pairs)  12 us
  transfers between devices with their start and end apart: 38, of which 19 were waited for; matrix products, arithmetic and copies ran while one was open for 2% of the time, Pallas kernels for 4%

profile of v2, /device:TPU:0, one launch (start us, length us, event | category | flops | bytes accessed | tf_op | source)
XLA Modules:
  0.0 354.7 jit_solution(18356508258414384951)
XLA Ops:
  0.7 0.8 copy.15
  1.6 1.3 collective-permute-start.3
  2.9 2.5 collective-permute-start.2
  5.4 0.6 collective-permute-start.1
  6.0 5.8 %collective-permute-start.4 = (s32[31]{0:T(128)S(1)}, s32[31]{0:T(128)S(1)}, u32[]{:S(2)}, u32[]{:S(2)}) collective-permute-start(s32[31]{0:T(128)S(1)} %pad_add_fusion.3), channel_id=1, source_target_pairs={{0,8},{1,9},{2,10},{3,11},{4,12},{5,13},{6,14},{7,15},{12,0},{13,1... | collective-permute-start | bytes 380 | tf_op jit(solution)/shard_map/ppermute | solution.py:498
  11.9 2.2 copy-done.3
  14.1 1.0 copy-done.4
  15.1 4.5 %pack.1.refs_0_ = bf16[2176,1024]{1,0:T(8,128)(2,1)S(1)} custom-call(bf16[2048,1024]{1,0:T(8,128)(2,1)S(1)} %copy-done.3, f32[64,2048]{1,0:T(8,128)S(1)} %copy-done.4), custom_call_target="tpu_custom_call" | custom-call | tf_op jit(solution)/shard_map/pack/pallas_call | solution.py:135
  19.6 2.0 copy-done.1
  21.7 1.3 collective-permute-start.8
  23.0 7.6 %collective-permute-start.9 = (bf16[2176,1024]{1,0:T(8,128)(2,1)}, bf16[2176,1024]{1,0:T(8,128)(2,1)}, u32[]{:S(2)}, u32[]{:S(2)}) collective-permute-start(bf16[2176,1024]{1,0:T(8,128)(2,1)} %copy-done.1), channel_id=1, source_target_pairs={{0,8},{1,9},{2,10},{3,11},{4,12},{5,13},{6,14},{7,15},{16,24},{17,... | collective-permute-start | bytes 13369352 | tf_op jit(solution)/shard_map/ppermute | solution.py:507
  30.9 1.3 collective-permute-start.6
  32.4 89.5 %collective-permute-done.8.refs_4_ = bf16[2176,1024]{1,0:T(8,128)(2,1)} collective-permute-done((bf16[2176,1024]{1,0:T(8,128)(2,1)}, bf16[2176,1024]{1,0:T(8,128)(2,1)}, u32[]{:S(2)}, u32[]{:S(2)}) %collective-permute-start.8) | collective-permute-done | bytes 4456480 | tf_op jit(solution)/shard_map/ppermute | solution.py:507
  122.0 1.3 collective-permute-start.10
  123.4 0.7 dynamic-slice_bitcast_fusion
  125.0 0.7 convert_reduce_fusion
  127.5 0.7 pad_add_fusion.4.span
  128.2 0.7 pad_add_fusion.1.span
  129.1 0.6 compare_select_fusion.8
  129.9 95.0 %collective-permute-done.6.refs_2_ = bf16[2176,1024]{1,0:T(8,128)(2,1)} collective-permute-done((bf16[2176,1024]{1,0:T(8,128)(2,1)}, bf16[2176,1024]{1,0:T(8,128)(2,1)}, u32[]{:S(2)}, u32[]{:S(2)}) %collective-permute-start.6) | collective-permute-done | bytes 4456480 | tf_op jit(solution)/shard_map/ppermute | solution.py:507
  224.9 2.3 copy-done.2
  227.2 11.0 %pairs.2 = (f32[28,64,512]{2,1,0:T(8,128)S(1)}, bf16[2,896,512]{2,1,0:T(8,128)(2,1)S(1)}, bf16[20,512,512]{2,1,0:T(8,128)(2,1)}) custom-call(s32[2,20]{1,0:T(2,128)S(1)} %pad_add_fusion.items, s32[2]{0:T(128)S(1)} %pad_add_fusion.1.span, bf16[2176,1024]{1,0:T(8,128)(2,1)S(1)} %copy-done.2, bf16[2176,1024]{1,0:T(8,128)(2,1)} %collective-permute-done.5.refs_1_, ...), custom_call_target="tpu_custom_call" | custom-call | tf_op jit(solution)/shard_map/pairs/pallas_call | solution.py:312
  238.2 9.9 %pairs.3 = (f32[4,64,512]{2,1,0:T(8,128)S(1)}, bf16[4,64,512]{2,1,0:T(8,128)(2,1)S(1)}, bf16[4,64,512]{2,1,0:T(8,128)(2,1)S(1)}, bf16[4,64,512]{2,1,0:T(8,128)(2...) custom-call(s32[2,20]{1,0:T(2,128)S(1)} %pad_add_fusion.items, ...), custom_call_target="tpu_custom_call", output_to_operand_aliasing={{6}: (11, {})} | custom-call | tf_op jit(solution)/shard_map/pairs/pallas_call | solution.py:312
  248.1 0.9 collective-permute-start.11
  248.9 1.0 collective-permute-start.12
  250.3 1.3 collective-permute-start.14
  251.6 1.9 collective-permute-start.15
  253.6 4.5 %collective-permute-done.12.refs_1_ = bf16[4,64,512]{2,1,0:T(8,128)(2,1)S(1)} collective-permute-done((bf16[4,64,512]{2,1,0:T(8,128)(2,1)S(1)}, bf16[4,64,512]{2,1,0:T(8,128)(2,1)S(1)}, u32[]{:S(2)}, u32[]{:S(2)}) %collective-permute-start.12) | collective-permute-done | bytes 262176 | tf_op jit(solution)/shard_map/ppermute | solution.py:523
  258.1 3.9 %collective-permute-done.13.refs_2_ = bf16[4,64,512]{2,1,0:T(8,128)(2,1)S(1)} collective-permute-done((bf16[4,64,512]{2,1,0:T(8,128)(2,1)S(1)}, bf16[4,64,512]{2,1,0:T(8,128)(2,1)S(1)}, u32[]{:S(2)}, u32[]{:S(2)}) %collective-permute-start.13) | collective-permute-done | bytes 262176 | tf_op jit(solution)/shard_map/ppermute | solution.py:523
  261.9 5.2 %collective-permute-done.15.refs_4_ = bf16[4,64,512]{2,1,0:T(8,128)(2,1)S(1)} collective-permute-done((bf16[4,64,512]{2,1,0:T(8,128)(2,1)S(1)}, bf16[4,64,512]{2,1,0:T(8,128)(2,1)S(1)}, u32[]{:S(2)}, u32[]{:S(2)}) %collective-permute-start.15) | collective-permute-done | bytes 262176 | tf_op jit(solution)/shard_map/ppermute | solution.py:523
  267.1 0.6 gram.2
  267.8 1.7 collective-permute-start.17
  269.7 1.5 collective-permute-done.18
  271.2 1.0 collective-permute-done.17
  272.2 1.1 collective-permute-start.21
  273.4 3.3 collective-permute-start.19
  276.7 1.7 collective-permute-done.21.refs_3_
  278.8 6.5 %panel.4.refs_0_ = bf16[128,1024]{1,0:T(8,128)(2,1)S(1)} custom-call(f32[64,64]{1,0:T(8,128)S(1)} %add_add_fusion.1.refs_0_, f32[64,64]{1,0:T(8,128)S(1)} %collective-permute-done.19.refs_1_, f32[64,64]{1,0:T(8,128)S(1)} %collective-permute-done.20.refs_2_, f32[64,64]{1,0:T(8,128)S(1)} %collective-permute-done.21.refs_3_, ...), custom_call_target="tpu_custom_call" | custom-call | tf_op jit(solution)/shard_map/panel/pallas_call | solution.py:463
  285.3 3.3 collective-permute-start.26
  288.7 1.3 collective-permute-start.25
  290.0 1.3 collective-permute-start.23
  291.3 0.5 collective-permute-start.22
  292.0 6.3 %collective-permute-done.26.refs_5_ = bf16[128,1024]{1,0:T(8,128)(2,1)S(1)} collective-permute-done((bf16[128,1024]{1,0:T(8,128)(2,1)S(1)}, bf16[128,1024]{1,0:T(8,128)(2,1)S(1)}, u32[]{:S(2)}, u32[]{:S(2)}) %collective-permute-start.26) | collective-permute-done | bytes 262176 | tf_op jit(solution)/shard_map/ppermute | solution.py:520
  298.3 3.1 collective-permute-done.25.refs_4_
  301.4 2.5 collective-permute-done.23.refs_2_
  303.8 4.0 %copy-done = bf16[20,512,512]{2,1,0:T(8,128)(2,1)S(1)} copy-done((bf16[20,512,512]{2,1,0:T(8,128)(2,1)S(1)}, bf16[20,512,512]{2,1,0:T(8,128)(2,1)}, u32[]{:S(2)}) %copy-start) | copy-done | bytes 10485784
  307.8 6.0 %apply.1 = (f32[4,64,512]{2,1,0:T(8,128)S(1)}, bf16[4,64,512]{2,1,0:T(8,128)(2,1)S(1)}, bf16[4,64,512]{2,1,0:T(8,128)(2,1)S(1)}, bf16[4,64,512]{2,1,0:T(8,128)(2...) custom-call(s32[2,20]{1,0:T(2,128)S(1)} %pad_add_fusion.items, s32[2]{0:T(128)S(1)} %pad_add_fusion.2.span, ...), custom_call_target="tpu_custom_call" | custom-call | tf_op jit(solution)/shard_map/apply/pallas_call | solution.py:366
  313.8 0.6 collective-permute-start.27
  314.4 0.7 collective-permute-start.28
  315.1 0.7 collective-permute-start.29
  315.8 2.8 collective-permute-start.30
  318.7 2.1 collective-permute-start.31
  320.8 2.8 collective-permute-done.28.refs_1_
  323.6 3.9 %collective-permute-done.29.refs_2_ = bf16[4,64,512]{2,1,0:T(8,128)(2,1)S(1)} collective-permute-done((bf16[4,64,512]{2,1,0:T(8,128)(2,1)S(1)}, bf16[4,64,512]{2,1,0:T(8,128)(2,1)S(1)}, u32[]{:S(2)}, u32[]{:S(2)}) %collective-permute-start.29) | collective-permute-done | bytes 262176 | tf_op jit(solution)/shard_map/ppermute | solution.py:523
  327.4 7.9 %collective-permute-done.31.refs_4_ = bf16[4,64,512]{2,1,0:T(8,128)(2,1)S(1)} collective-permute-done((bf16[4,64,512]{2,1,0:T(8,128)(2,1)S(1)}, bf16[4,64,512]{2,1,0:T(8,128)(2,1)S(1)}, u32[]{:S(2)}, u32[]{:S(2)}) %collective-permute-start.31) | collective-permute-done | bytes 262176 | tf_op jit(solution)/shard_map/ppermute | solution.py:523
  335.3 0.6 gram.3
  335.9 0.9 collective-permute-start.34
  336.8 0.8 collective-permute-start.33
  337.9 1.7 collective-permute-done.34
  339.6 1.4 collective-permute-done.33
  341.2 4.3 %collective-permute-start.35 = (f32[64,64]{1,0:T(8,128)S(1)}, f32[64,64]{1,0:T(8,128)S(1)}, u32[]{:S(2)}, u32[]{:S(2)}) collective-permute-start(f32[64,64]{1,0:T(8,128)S(1)} %add_add_fusion.refs_0_), channel_id=1, source_target_pairs={{0,4},{1,5},{2,6},{3,7},{4,0},{5,1},{6,2},{7,3},{8,12},{9,13},{10,... | collective-permute-start | bytes 49160 | tf_op jit(solution)/shard_map/ppermute | solution.py:478
  345.5 1.4 collective-permute-done.37.refs_3_
  346.9 0.5 collective-permute-done.35.refs_1_
  347.4 7.3 %panel.5 = f32[64,2048]{1,0:T(8,128)} custom-call(f32[64,64]{1,0:T(8,128)S(1)} %add_add_fusion.refs_0_, f32[64,64]{1,0:T(8,128)S(1)} %collective-permute-done.35.refs_1_, f32[64,64]{1,0:T(8,128)S(1)} %collective-permute-done.36.refs_2_, f32[64,64]{1,0:T(8,128)S(1)} %collective-permute-done.37.refs_3_, f32[4,64,512]{2,1,0:T(8,128)S(1)} %get-tuple-element.50.refs_4_), custom_call_target="tpu_custom_call" | custom-call | tf_op jit(solution)/shard_map/panel/pallas_call | solution.py:463
  (67 shorter events, 4.4 us)
Async XLA Ops:
  1.6 20.1 %collective-permute-start.3 = (s32[31]{0:T(128)S(1)}, s32[31]{0:T(128)S(1)}, u32[]{:S(2)}, u32[]{:S(2)}) collective-permute-start(s32[31]{0:T(128)S(1)} %pad_add_fusion.3), channel_id=1, source_target_pairs={{4,0},{5,1},{6,2},{7,3},{8,4},{9,5},{10,6},{11,7},{12,8},{13,9},{1... | collective-permute-start | bytes 380 | tf_op jit(solution)/shard_map/ppermute | solution.py:498
  2.9 18.8 %collective-permute-start.2 = (s32[31]{0:T(128)S(1)}, s32[31]{0:T(128)S(1)}, u32[]{:S(2)}, u32[]{:S(2)}) collective-permute-start(s32[31]{0:T(128)S(1)} %pad_add_fusion.3), channel_id=1, source_target_pairs={{0,3},{1,2},{2,1},{3,0},{4,7},{5,6},{6,5},{7,4},{8,11},{9,10},{10,... | collective-permute-start | bytes 380 | tf_op jit(solution)/shard_map/ppermute | solution.py:498
  5.4 16.3 %collective-permute-start.1 = (s32[31]{0:T(128)S(1)}, s32[31]{0:T(128)S(1)}, u32[]{:S(2)}, u32[]{:S(2)}) collective-permute-start(s32[31]{0:T(128)S(1)} %pad_add_fusion.3), channel_id=1, source_target_pairs={{0,2},{1,3},{2,0},{3,1},{4,6},{5,7},{6,4},{7,5},{8,10},{9,11},{10,... | collective-permute-start | bytes 380 | tf_op jit(solution)/shard_map/ppermute | solution.py:498
  6.0 15.7 %collective-permute-start = (s32[31]{0:T(128)S(1)}, s32[31]{0:T(128)S(1)}, u32[]{:S(2)}, u32[]{:S(2)}) collective-permute-start(s32[31]{0:T(128)S(1)} %pad_add_fusion.3), channel_id=1, source_target_pairs={{0,1},{1,0},{2,3},{3,2},{4,5},{5,4},{6,7},{7,6},{8,9},{9,8},{10,11... | collective-permute-start | bytes 380 | tf_op jit(solution)/shard_map/ppermute | solution.py:498
  6.0 15.6 %collective-permute-start.4 = (s32[31]{0:T(128)S(1)}, s32[31]{0:T(128)S(1)}, u32[]{:S(2)}, u32[]{:S(2)}) collective-permute-start(s32[31]{0:T(128)S(1)} %pad_add_fusion.3), channel_id=1, source_target_pairs={{0,8},{1,9},{2,10},{3,11},{4,12},{5,13},{6,14},{7,15},{12,0},{13,1... | collective-permute-start | bytes 380 | tf_op jit(solution)/shard_map/ppermute | solution.py:498
  11.9 2.2 copy-start.3
  14.1 1.0 copy-start.4
  19.6 2.0 copy-start.1
  21.7 100.3 %collective-permute-start.8 = (bf16[2176,1024]{1,0:T(8,128)(2,1)}, bf16[2176,1024]{1,0:T(8,128)(2,1)}, u32[]{:S(2)}, u32[]{:S(2)}) collective-permute-start(bf16[2176,1024]{1,0:T(8,128)(2,1)} %copy-done.1), channel_id=1, source_target_pairs={{4,0},{5,1},{6,2},{7,3},{8,4},{9,5},{10,6},{11,7},{12,8},{13,9},{1... | collective-permute-start | bytes 13369352 | tf_op jit(solution)/shard_map/ppermute | solution.py:507
  23.0 215.2 %collective-permute-start.9 = (bf16[2176,1024]{1,0:T(8,128)(2,1)}, bf16[2176,1024]{1,0:T(8,128)(2,1)}, u32[]{:S(2)}, u32[]{:S(2)}) collective-permute-start(bf16[2176,1024]{1,0:T(8,128)(2,1)} %copy-done.1), channel_id=1, source_target_pairs={{0,8},{1,9},{2,10},{3,11},{4,12},{5,13},{6,14},{7,15},{16,24},{17,... | collective-permute-start | bytes 13369352 | tf_op jit(solution)/shard_map/ppermute | solution.py:507
  30.6 99.3 %collective-permute-start.7 = (bf16[2176,1024]{1,0:T(8,128)(2,1)}, bf16[2176,1024]{1,0:T(8,128)(2,1)}, u32[]{:S(2)}, u32[]{:S(2)}) collective-permute-start(bf16[2176,1024]{1,0:T(8,128)(2,1)} %copy-done.1), channel_id=1, source_target_pairs={{0,3},{1,2},{2,1},{3,0},{4,7},{5,6},{6,5},{7,4},{8,11},{9,10},{10,... | collective-permute-start | bytes 13369352 | tf_op jit(solution)/shard_map/ppermute | solution.py:507
  30.9 194.0 %collective-permute-start.6 = (bf16[2176,1024]{1,0:T(8,128)(2,1)}, bf16[2176,1024]{1,0:T(8,128)(2,1)}, u32[]{:S(2)}, u32[]{:S(2)}) collective-permute-start(bf16[2176,1024]{1,0:T(8,128)(2,1)} %copy-done.1), channel_id=1, source_target_pairs={{0,2},{1,3},{2,0},{3,1},{4,6},{5,7},{6,4},{7,5},{8,10},{9,11},{10,... | collective-permute-start | bytes 13369352 | tf_op jit(solution)/shard_map/ppermute | solution.py:507
  32.1 192.8 %collective-permute-start.5 = (bf16[2176,1024]{1,0:T(8,128)(2,1)}, bf16[2176,1024]{1,0:T(8,128)(2,1)}, u32[]{:S(2)}, u32[]{:S(2)}) collective-permute-start(bf16[2176,1024]{1,0:T(8,128)(2,1)} %copy-done.1), channel_id=1, source_target_pairs={{0,1},{1,0},{2,3},{3,2},{4,5},{5,4},{6,7},{7,6},{8,9},{9,8},{10,11... | collective-permute-start | bytes 13369352 | tf_op jit(solution)/shard_map/ppermute | solution.py:507
  122.0 116.2 %collective-permute-start.10 = (bf16[2176,1024]{1,0:T(8,128)(2,1)}, bf16[2176,1024]{1,0:T(8,128)(2,1)}, u32[]{:S(2)}, u32[]{:S(2)}) collective-permute-start(bf16[2176,1024]{1,0:T(8,128)(2,1)} %copy-done.1), channel_id=1, source_target_pairs={{12,0},{13,1},{14,2},{15,3},{28,16},{29,17},{30,18},{31,19}} | collective-permute-start | bytes 13369352 | tf_op jit(solution)/shard_map/ppermute | solution.py:507
  224.9 2.3 copy-start.2
  248.1 5.5 %collective-permute-start.11 = (bf16[4,64,512]{2,1,0:T(8,128)(2,1)S(1)}, bf16[4,64,512]{2,1,0:T(8,128)(2,1)S(1)}, u32[]{:S(2)}, u32[]{:S(2)}) collective-permute-start(bf16[4,64,512]{2,1,0:T(8,128)(2,1)S(1)} %get-tuple-element.35), channel_id=1, source_target_pairs={{1,0},{0,1},{3,2},{2,3},{5,4},{4,5},{7,6},{6,7},{9,8},{8,9},{11,10... | collective-permute-start | bytes 786440 | tf_op jit(solution)/shard_map/ppermute | solution.py:523
  248.9 9.2 %collective-permute-start.12 = (bf16[4,64,512]{2,1,0:T(8,128)(2,1)S(1)}, bf16[4,64,512]{2,1,0:T(8,128)(2,1)S(1)}, u32[]{:S(2)}, u32[]{:S(2)}) collective-permute-start(bf16[4,64,512]{2,1,0:T(8,128)(2,1)S(1)} %get-tuple-element.36), channel_id=1, source_target_pairs={{2,0},{3,1},{0,2},{1,3},{6,4},{7,5},{4,6},{5,7},{10,8},{11,9},{8,1... | collective-permute-start | bytes 786440 | tf_op jit(solution)/shard_map/ppermute | solution.py:523
  249.9 12.1 %collective-permute-start.13 = (bf16[4,64,512]{2,1,0:T(8,128)(2,1)S(1)}, bf16[4,64,512]{2,1,0:T(8,128)(2,1)S(1)}, u32[]{:S(2)}, u32[]{:S(2)}) collective-permute-start(bf16[4,64,512]{2,1,0:T(8,128)(2,1)S(1)} %get-tuple-element.37), channel_id=1, source_target_pairs={{3,0},{2,1},{1,2},{0,3},{7,4},{6,5},{5,6},{4,7},{11,8},{10,9},{9,1... | collective-permute-start | bytes 786440 | tf_op jit(solution)/shard_map/ppermute | solution.py:523
  250.3 11.6 %collective-permute-start.14 = (bf16[4,64,512]{2,1,0:T(8,128)(2,1)S(1)}, bf16[4,64,512]{2,1,0:T(8,128)(2,1)S(1)}, u32[]{:S(2)}, u32[]{:S(2)}) collective-permute-start(bf16[4,64,512]{2,1,0:T(8,128)(2,1)S(1)} %get-tuple-element.38), channel_id=1, source_target_pairs={{0,4},{1,5},{2,6},{3,7},{4,8},{5,9},{6,10},{7,11},{8,12},{9,13},{1... | collective-permute-start | bytes 786440 | tf_op jit(solution)/shard_map/ppermute | solution.py:523
  251.6 15.5 %collective-permute-start.15 = (bf16[4,64,512]{2,1,0:T(8,128)(2,1)S(1)}, bf16[4,64,512]{2,1,0:T(8,128)(2,1)S(1)}, u32[]{:S(2)}, u32[]{:S(2)}) collective-permute-start(bf16[4,64,512]{2,1,0:T(8,128)(2,1)S(1)} %get-tuple-element.39), channel_id=1, source_target_pairs={{8,0},{9,1},{10,2},{11,3},{12,4},{13,5},{14,6},{15,7},{0,12},{1,13... | collective-permute-start | bytes 786440 | tf_op jit(solution)/shard_map/ppermute | solution.py:523
  267.7 3.5 collective-permute-start.18
  267.8 4.4 %collective-permute-start.17 = (f32[64,64]{1,0:T(8,128)S(1)}, f32[64,64]{1,0:T(8,128)S(1)}, u32[]{:S(2)}, u32[]{:S(2)}) collective-permute-start(f32[64,64]{1,0:T(8,128)S(1)} %get-tuple-element.40), channel_id=1, source_target_pairs={{0,2},{1,3},{2,0},{3,1},{4,6},{5,7},{6,4},{7,5},{8,10},{9,11},{10,... | collective-permute-start | bytes 49160 | tf_op jit(solution)/shard_map/ppermute | solution.py:478
  269.5 2.7 collective-permute-start.16
  272.2 6.1 %collective-permute-start.21 = (f32[64,64]{1,0:T(8,128)S(1)}, f32[64,64]{1,0:T(8,128)S(1)}, u32[]{:S(2)}, u32[]{:S(2)}) collective-permute-start(f32[64,64]{1,0:T(8,128)S(1)} %add_add_fusion.1.refs_0_), channel_id=1, source_target_pairs={{0,12},{1,13},{2,14},{3,15},{4,8},{5,9},{6,10},{7,11},{8,4},{9,5},... | collective-permute-start | bytes 49160 | tf_op jit(solution)/shard_map/ppermute | solution.py:478
  273.4 5.4 %collective-permute-start.20 = (f32[64,64]{1,0:T(8,128)S(1)}, f32[64,64]{1,0:T(8,128)S(1)}, u32[]{:S(2)}, u32[]{:S(2)}) collective-permute-start(f32[64,64]{1,0:T(8,128)S(1)} %add_add_fusion.1.refs_0_), channel_id=1, source_target_pairs={{0,8},{1,9},{2,10},{3,11},{4,12},{5,13},{6,14},{7,15},{8,0},{9,1},... | collective-permute-start | bytes 49160 | tf_op jit(solution)/shard_map/ppermute | solution.py:478
  273.4 5.4 %collective-permute-start.19 = (f32[64,64]{1,0:T(8,128)S(1)}, f32[64,64]{1,0:T(8,128)S(1)}, u32[]{:S(2)}, u32[]{:S(2)}) collective-permute-start(f32[64,64]{1,0:T(8,128)S(1)} %add_add_fusion.1.refs_0_), channel_id=1, source_target_pairs={{0,4},{1,5},{2,6},{3,7},{4,0},{5,1},{6,2},{7,3},{8,12},{9,13},{10,... | collective-permute-start | bytes 49160 | tf_op jit(solution)/shard_map/ppermute | solution.py:478
  285.3 12.9 %collective-permute-start.26 = (bf16[128,1024]{1,0:T(8,128)(2,1)S(1)}, bf16[128,1024]{1,0:T(8,128)(2,1)S(1)}, u32[]{:S(2)}, u32[]{:S(2)}) collective-permute-start(bf16[128,1024]{1,0:T(8,128)(2,1)S(1)} %panel.4.refs_0_), channel_id=1, source_target_pairs={{0,8},{1,9},{2,10},{3,11},{4,12},{5,13},{6,14},{7,15},{12,0},{13,1... | collective-permute-start | bytes 786440 | tf_op jit(solution)/shard_map/ppermute | solution.py:520
  288.7 12.7 %collective-permute-start.25 = (bf16[128,1024]{1,0:T(8,128)(2,1)S(1)}, bf16[128,1024]{1,0:T(8,128)(2,1)S(1)}, u32[]{:S(2)}, u32[]{:S(2)}) collective-permute-start(bf16[128,1024]{1,0:T(8,128)(2,1)S(1)} %panel.4.refs_0_), channel_id=1, source_target_pairs={{4,0},{5,1},{6,2},{7,3},{8,4},{9,5},{10,6},{11,7},{12,8},{13,9},{1... | collective-permute-start | bytes 786440 | tf_op jit(solution)/shard_map/ppermute | solution.py:520
  290.0 11.4 %collective-permute-start.24 = (bf16[128,1024]{1,0:T(8,128)(2,1)S(1)}, bf16[128,1024]{1,0:T(8,128)(2,1)S(1)}, u32[]{:S(2)}, u32[]{:S(2)}) collective-permute-start(bf16[128,1024]{1,0:T(8,128)(2,1)S(1)} %panel.4.refs_0_), channel_id=1, source_target_pairs={{0,3},{1,2},{2,1},{3,0},{4,7},{5,6},{6,5},{7,4},{8,11},{9,10},{10,... | collective-permute-start | bytes 786440 | tf_op jit(solution)/shard_map/ppermute | solution.py:520
  290.0 13.8 %collective-permute-start.23 = (bf16[128,1024]{1,0:T(8,128)(2,1)S(1)}, bf16[128,1024]{1,0:T(8,128)(2,1)S(1)}, u32[]{:S(2)}, u32[]{:S(2)}) collective-permute-start(bf16[128,1024]{1,0:T(8,128)(2,1)S(1)} %panel.4.refs_0_), channel_id=1, source_target_pairs={{0,2},{1,3},{2,0},{3,1},{4,6},{5,7},{6,4},{7,5},{8,10},{9,11},{10,... | collective-permute-start | bytes 786440 | tf_op jit(solution)/shard_map/ppermute | solution.py:520
  291.3 12.5 %collective-permute-start.22 = (bf16[128,1024]{1,0:T(8,128)(2,1)S(1)}, bf16[128,1024]{1,0:T(8,128)(2,1)S(1)}, u32[]{:S(2)}, u32[]{:S(2)}) collective-permute-start(bf16[128,1024]{1,0:T(8,128)(2,1)S(1)} %panel.4.refs_0_), channel_id=1, source_target_pairs={{0,1},{1,0},{2,3},{3,2},{4,5},{5,4},{6,7},{7,6},{8,9},{9,8},{10,11... | collective-permute-start | bytes 786440 | tf_op jit(solution)/shard_map/ppermute | solution.py:520
  303.8 4.0 %copy-start = (bf16[20,512,512]{2,1,0:T(8,128)(2,1)S(1)}, bf16[20,512,512]{2,1,0:T(8,128)(2,1)}, u32[]{:S(2)}) copy-start(bf16[20,512,512]{2,1,0:T(8,128)(2,1)} %get-tuple-element.42.refs_6_) | copy-start | bytes 31457284
  313.8 7.0 %collective-permute-start.27 = (bf16[4,64,512]{2,1,0:T(8,128)(2,1)S(1)}, bf16[4,64,512]{2,1,0:T(8,128)(2,1)S(1)}, u32[]{:S(2)}, u32[]{:S(2)}) collective-permute-start(bf16[4,64,512]{2,1,0:T(8,128)(2,1)S(1)} %get-tuple-element.44), channel_id=1, source_target_pairs={{1,0},{0,1},{3,2},{2,3},{5,4},{4,5},{7,6},{6,7},{9,8},{8,9},{11,10... | collective-permute-start | bytes 786440 | tf_op jit(solution)/shard_map/ppermute | solution.py:523
  314.4 9.2 %collective-permute-start.28 = (bf16[4,64,512]{2,1,0:T(8,128)(2,1)S(1)}, bf16[4,64,512]{2,1,0:T(8,128)(2,1)S(1)}, u32[]{:S(2)}, u32[]{:S(2)}) collective-permute-start(bf16[4,64,512]{2,1,0:T(8,128)(2,1)S(1)} %get-tuple-element.45), channel_id=1, source_target_pairs={{2,0},{3,1},{0,2},{1,3},{6,4},{7,5},{4,6},{5,7},{10,8},{11,9},{8,1... | collective-permute-start | bytes 786440 | tf_op jit(solution)/shard_map/ppermute | solution.py:523
  315.1 12.3 %collective-permute-start.29 = (bf16[4,64,512]{2,1,0:T(8,128)(2,1)S(1)}, bf16[4,64,512]{2,1,0:T(8,128)(2,1)S(1)}, u32[]{:S(2)}, u32[]{:S(2)}) collective-permute-start(bf16[4,64,512]{2,1,0:T(8,128)(2,1)S(1)} %get-tuple-element.46), channel_id=1, source_target_pairs={{3,0},{2,1},{1,2},{0,3},{7,4},{6,5},{5,6},{4,7},{11,8},{10,9},{9,1... | collective-permute-start | bytes 786440 | tf_op jit(solution)/shard_map/ppermute | solution.py:523
  315.8 11.6 %collective-permute-start.30 = (bf16[4,64,512]{2,1,0:T(8,128)(2,1)S(1)}, bf16[4,64,512]{2,1,0:T(8,128)(2,1)S(1)}, u32[]{:S(2)}, u32[]{:S(2)}) collective-permute-start(bf16[4,64,512]{2,1,0:T(8,128)(2,1)S(1)} %get-tuple-element.47), channel_id=1, source_target_pairs={{0,4},{1,5},{2,6},{3,7},{4,8},{5,9},{6,10},{7,11},{8,12},{9,13},{1... | collective-permute-start | bytes 786440 | tf_op jit(solution)/shard_map/ppermute | solution.py:523
  318.7 16.7 %collective-permute-start.31 = (bf16[4,64,512]{2,1,0:T(8,128)(2,1)S(1)}, bf16[4,64,512]{2,1,0:T(8,128)(2,1)S(1)}, u32[]{:S(2)}, u32[]{:S(2)}) collective-permute-start(bf16[4,64,512]{2,1,0:T(8,128)(2,1)S(1)} %get-tuple-element.48), channel_id=1, source_target_pairs={{8,0},{9,1},{10,2},{11,3},{12,4},{13,5},{14,6},{15,7},{0,12},{1,13... | collective-permute-start | bytes 786440 | tf_op jit(solution)/shard_map/ppermute | solution.py:523
  335.9 3.6 %collective-permute-start.34 = (f32[64,64]{1,0:T(8,128)S(1)}, f32[64,64]{1,0:T(8,128)S(1)}, u32[]{:S(2)}, u32[]{:S(2)}) collective-permute-start(f32[64,64]{1,0:T(8,128)S(1)} %get-tuple-element.49), channel_id=1, source_target_pairs={{0,3},{1,2},{2,1},{3,0},{4,7},{5,6},{6,5},{7,4},{8,11},{9,10},{10,... | collective-permute-start | bytes 49160 | tf_op jit(solution)/shard_map/ppermute | solution.py:478
  336.8 4.1 %collective-permute-start.33 = (f32[64,64]{1,0:T(8,128)S(1)}, f32[64,64]{1,0:T(8,128)S(1)}, u32[]{:S(2)}, u32[]{:S(2)}) collective-permute-start(f32[64,64]{1,0:T(8,128)S(1)} %get-tuple-element.49), channel_id=1, source_target_pairs={{0,2},{1,3},{2,0},{3,1},{4,6},{5,7},{6,4},{7,5},{8,10},{9,11},{10,... | collective-permute-start | bytes 49160 | tf_op jit(solution)/shard_map/ppermute | solution.py:478
  337.7 3.3 collective-permute-start.32
  341.0 5.9 %collective-permute-start.37 = (f32[64,64]{1,0:T(8,128)S(1)}, f32[64,64]{1,0:T(8,128)S(1)}, u32[]{:S(2)}, u32[]{:S(2)}) collective-permute-start(f32[64,64]{1,0:T(8,128)S(1)} %add_add_fusion.refs_0_), channel_id=1, source_target_pairs={{0,12},{1,13},{2,14},{3,15},{4,8},{5,9},{6,10},{7,11},{8,4},{9,5},... | collective-permute-start | bytes 49160 | tf_op jit(solution)/shard_map/ppermute | solution.py:478
  341.1 5.8 %collective-permute-start.36 = (f32[64,64]{1,0:T(8,128)S(1)}, f32[64,64]{1,0:T(8,128)S(1)}, u32[]{:S(2)}, u32[]{:S(2)}) collective-permute-start(f32[64,64]{1,0:T(8,128)S(1)} %add_add_fusion.refs_0_), channel_id=1, source_target_pairs={{0,8},{1,9},{2,10},{3,11},{4,12},{5,13},{6,14},{7,15},{8,0},{9,1},... | collective-permute-start | bytes 49160 | tf_op jit(solution)/shard_map/ppermute | solution.py:478
  341.2 6.2 %collective-permute-start.35 = (f32[64,64]{1,0:T(8,128)S(1)}, f32[64,64]{1,0:T(8,128)S(1)}, u32[]{:S(2)}, u32[]{:S(2)}) collective-permute-start(f32[64,64]{1,0:T(8,128)S(1)} %add_add_fusion.refs_0_), channel_id=1, source_target_pairs={{0,4},{1,5},{2,6},{3,7},{4,0},{5,1},{6,2},{7,3},{8,12},{9,13},{10,... | collective-permute-start | bytes 49160 | tf_op jit(solution)/shard_map/ppermute | solution.py:478

commit v3 on v2

--- a/solution.py
+++ b/solution.py
@@ -13,28 +13,35 @@
 REACH = 7
 SHARPNESS = 24.0
 LOG2E = 1.4426950408889634
+LIST_ROWS = 16
+LANES = 128
 VMEM_LIMIT = 32 * 1024 * 1024
+VMEM_MOST = 55 * 1024 * 1024
 
 
 def make_plan(count):
     if count == 16:
-        moves = [[(i, i ^ m) for i in range(count)] for m in (1, 2, 3)]
+        moves = [[(i, i ^ 1) for i in range(count)], [(i, i ^ 2) for i in range(count)], [(i, i ^ 1) for i in range(count)]]
         moves.append([(i, i - 4) for i in range(4, count)])
         moves.append([(i, i + 8) for i in range(8)])
         moves.append([(i, i - 12) for i in range(12, 16)])
         late = {5, 6}
         after = {6: 4}
+        via = {3: 2}
+        hops = {5: [[(i, i + 4) for i in range(8)], [(i, i + 4) for i in range(4, 12)]]}
         joint = [[1], [2], [3], [4], [5, 6]]
     else:
         moves = [[(i, (i - o) % count) for i in range(count)] for o in range(1, REACH + 1)]
         late = {5, 6, 7}
         after = {6: 1, 7: 2}
+        via = {}
+        hops = {}
         joint = [[m] for m in range(1, REACH + 1)]
     hold = -np.ones((count, len(moves) + 1), np.int32)
     hold[:, 0] = np.arange(count)
     for m, pairs in enumerate(moves):
         for source, target in pairs:
-            hold[target, m + 1] = source
+            hold[target, m + 1] = hold[source, via.get(m + 1, 0)]
     work = np.zeros((count, count, count), bool)
     load = np.zeros(count, np.int32)
     for row in range(count):
@@ -51,7 +58,7 @@
         for s, device in enumerate(hold[w]):
             if device >= 0:
                 place[w, device] = s
-    return moves, joint, hold, place, work, late, after, int(load.max())
+    return moves, via, hops, joint, hold, place, work, late, after, int(load.max())
 
 
 def work_list(lists, hold, place, work, late, slots, blocks_here, top, me):
@@ -89,14 +96,14 @@
     return jnp.stack([rows, cols]), jnp.stack([zero, n_first]), jnp.stack([n_first, n_first + n_second])
 
 
-def pack_kernel(rows, panel, out, buf, in_sem, out_sem):
+def pack_kernel(rows, pairs, live, panel, out, raw, buf, in_sem, out_sem):
     count, depth = rows.shape
     blocks = count // BLOCK
     per_row = depth // BLOCK
     high = panel.shape[0] // per_row
-    step = 64
+    step = 32
     loads = [
-        pltpu.make_async_copy(rows.at[pl.ds(b * BLOCK, BLOCK)], buf.at[pl.ds(b * BLOCK, BLOCK)], in_sem.at[b])
+        pltpu.make_async_copy(rows.at[pl.ds(b * BLOCK, BLOCK)], raw.at[pl.ds(b * BLOCK, BLOCK)], in_sem.at[b])
         for b in range(blocks)
     ]
     for load in loads:
@@ -106,7 +113,15 @@
             buf[pl.ds(count + b * high, high), q * BLOCK : (q + 1) * BLOCK] = panel[
                 q * high : (q + 1) * high, b * BLOCK : (b + 1) * BLOCK
             ].astype(jnp.bfloat16)
-    stores = [(count, blocks * high)] + [(b * BLOCK, BLOCK) for b in range(blocks)]
+    lane = lax.broadcasted_iota(jnp.int32, (LIST_ROWS, LANES), 1)
+    values = jnp.where(lane == 2 * pairs.shape[0], live[0], 0)
+    for slot in range(pairs.shape[0]):
+        for side in range(2):
+            values = jnp.where(lane == 2 * slot + side, pairs[slot, side], values)
+    list_at = count + blocks * high
+    buf[pl.ds(list_at, LIST_ROWS), :LANES] = values.astype(jnp.float32).astype(jnp.bfloat16)
+    buf[pl.ds(list_at, LIST_ROWS), LANES:] = jnp.zeros((LIST_ROWS, depth - LANES), jnp.bfloat16)
+    stores = [(count, blocks * high + LIST_ROWS)] + [(b * BLOCK, BLOCK) for b in range(blocks)]
     stores = [
         pltpu.make_async_copy(buf.at[pl.ds(at, size)], out.at[pl.ds(at, size)], out_sem.at[n])
         for n, (at, size) in enumerate(stores)
@@ -115,10 +130,10 @@
     for b in range(blocks):
         loads[b].wait()
 
-        @pl.loop(0, BLOCK // step, unroll=2)
+        @pl.loop(0, BLOCK // step, unroll=4)
         def _(i):
             at = pl.ds(pl.multiple_of(b * BLOCK + i * step, step), step)
-            values = buf[at, :].astype(jnp.float32)
+            values = raw[at, :].astype(jnp.float32)
             mean = jnp.sum(values * values, axis=-1, keepdims=True) * (1.0 / depth)
             factor = lax.rsqrt(mean + 1e-06) * depth ** (-0.5)
             buf[at, :] = (values * factor).astype(jnp.bfloat16)
@@ -128,30 +143,31 @@
         store.wait()
 
 
-def pack_call(embeddings, panel):
+def pack_call(embeddings, pairs, live, panel):
     rows, depth = embeddings.shape
     blocks = rows // BLOCK
-    tall = rows + panel.shape[0] * panel.shape[1] // depth
+    tall = rows + panel.shape[0] * panel.shape[1] // depth + LIST_ROWS
+    smem = pl.BlockSpec(memory_space=pltpu.SMEM)
     return pl.pallas_call(
         pack_kernel,
         out_shape=jax.ShapeDtypeStruct((tall, depth), jnp.bfloat16),
-        in_specs=[pl.BlockSpec(memory_space=pltpu.HBM), pl.BlockSpec(memory_space=pltpu.VMEM)],
+        in_specs=[pl.BlockSpec(memory_space=pltpu.HBM), smem, smem, pl.BlockSpec(memory_space=pltpu.VMEM)],
         out_specs=pl.BlockSpec(memory_space=pltpu.HBM),
         scratch_shapes=[
+            pltpu.VMEM((rows, depth), jnp.bfloat16),
             pltpu.VMEM((tall, depth), jnp.bfloat16),
             pltpu.SemaphoreType.DMA((blocks,)),
             pltpu.SemaphoreType.DMA((blocks + 1,)),
         ],
-        compiler_params=pltpu.CompilerParams(vmem_limit_bytes=VMEM_LIMIT),
+        compiler_params=pltpu.CompilerParams(vmem_limit_bytes=VMEM_MOST),
         name="pack",
-    )(embeddings, panel)
-
-
-def fill_panel(refs, columns, at, pan, sem):
+    )(embeddings, pairs, live, panel)
+
+
+def fill_panel(refs, columns, at, size, pan, sem):
     per_row = pan.shape[0]
     copies = []
     for ref, s in zip(refs, columns):
-        size = ref.shape[0] - at
         for q in range(per_row):
             source = ref.at[pl.ds(at, size), pl.ds(q * BLOCK, BLOCK)]
             copies.append(
@@ -224,7 +240,8 @@
     else:
         acc[...] = acc_in[...]
         pan[...] = pan_in[...]
-    for copy in fill_panel(units[fresh:], columns[fresh:], per * BLOCK, pan, psem):
+    size = units[0].shape[0] - per * BLOCK - LIST_ROWS
+    for copy in fill_panel(units[fresh:], columns[fresh:], per * BLOCK, size, pan, psem):
         copy.wait()
 
     @pl.loop(begin, end)
@@ -338,7 +355,7 @@
             load(ahead, ahead).start()
 
     spots = [(panels[0], 0)] + [(ref, s) for ref, group in zip(panels[1:], joint) for s in group]
-    copies = fill_panel([ref for ref, _ in spots], [s for _, s in spots], 0, pan, psem)
+    copies = fill_panel([ref for ref, _ in spots], [s for _, s in spots], 0, panels[0].shape[0], pan, psem)
     acc[...] = jnp.zeros_like(acc)
     for copy in copies:
         copy.wait()
@@ -375,7 +392,7 @@
             pltpu.SemaphoreType.DMA((held * per_row,)),
             pltpu.SemaphoreType.DMA((4,)),
         ],
-        compiler_params=pltpu.CompilerParams(vmem_limit_bytes=VMEM_LIMIT),
+        compiler_params=pltpu.CompilerParams(vmem_limit_bytes=50 * 1024 * 1024),
         name="apply",
     )(items, span, *panels, aff)
 
@@ -488,23 +505,38 @@
     per = embeddings.shape[0] // BLOCK
     width = start_panel.shape[0]
     slots = block_pairs.shape[0]
-    moves, joint, hold, place, work, late, after, top = make_plan(count)
+    moves, via, hops, joint, hold, place, work, late, after, top = make_plan(count)
     held = len(moves) + 1
 
+    merged = [functools.reduce(list.__add__, [moves[s - 1] for s in group]) for group in joint]
+
+    def spread(value):
+        got = [value]
+        for group, pairs in zip(joint, merged):
+            got.append(lax.ppermute(got[via.get(group[0], 0)], "rows", pairs))
+        return got
+
+    assert count * per <= 256
     own_list = jnp.concatenate([block_pairs.reshape(-1), pair_count])
-    merged = [functools.reduce(list.__add__, [moves[s - 1] for s in group]) for group in joint]
-    lists = [own_list]
+    lists = {}
     for group, pairs in zip(joint, merged):
-        lists += [lax.ppermute(own_list, "rows", pairs)] * len(group)
-    lists = jnp.stack(lists)
-    packed = pack_call(embeddings, start_panel)
+        if group[0] in late:
+            part = lax.ppermute(own_list, "rows", pairs)
+            lists.update({m: part for m in group})
+    packed = pack_call(embeddings, block_pairs, pair_count, start_panel)
     packed, lists = lax.optimization_barrier((packed, lists))
     units = {0: packed}
-    for m, pairs in enumerate(moves, 1):
-        outgoing = packed
+    for m in range(1, len(moves) + 1):
+        outgoing = units[via.get(m, 0)]
         if m in after:
-            outgoing, _ = lax.optimization_barrier((packed, units[after[m]]))
-        units[m] = lax.ppermute(outgoing, "rows", pairs)
+            outgoing, _ = lax.optimization_barrier((outgoing, units[after[m]]))
+        for pairs in hops.get(m, [moves[m - 1]]):
+            outgoing = lax.ppermute(outgoing, "rows", pairs)
+        units[m] = outgoing
+    for m, unit in units.items():
+        if m not in lists:
+            lists[m] = unit[unit.shape[0] - 1, : own_list.shape[0]].astype(jnp.int32)
+    lists = jnp.stack([lists[m] for m in range(held)])
     items, span_first, span_second = work_list(lists, hold, place, work, late, slots, per, top, me)
     span_all = jnp.stack([span_first[0], span_second[1]])
 
@@ -517,12 +549,14 @@
 
     for sweep in range(ITERS):
         if sweep > 0:
-            panels = [panel] + [lax.ppermute(panel, "rows", pairs) for pairs in merged]
-            sums = apply_call(items, span_all, panels, joint, aff, per, width)
-        backs = [
-            lax.ppermute(sums[m], "rows", [(target, source) for source, target in pairs])
-            for m, pairs in enumerate(merged, 1)
-        ]
+            sums = apply_call(items, span_all, spread(panel), joint, aff, per, width)
+        sums, backs = list(sums), []
+        for m in sorted(range(1, len(joint) + 1), key=lambda m: m not in via):
+            back = lax.ppermute(sums[m], "rows", [(target, source) for source, target in merged[m - 1]])
+            if m in via:
+                sums[via[m]] = sums[via[m]] + back
+            else:
+                backs.append(back)
         y, gram = gram_call(sums[0], backs)
         grams = sum_over_rows(gram)
         panel = panel_call(grams, y, count * embeddings.shape[0], depth, sweep == ITERS - 1)

time: 361 us -> 330 us (0.914); the launches traced: 355 us -> 328 us
  waiting for transfers between devices: 234 us -> 211 us
  local copies, waits for them, and re-layouts: 14.2 us -> 4.98 us
  Pallas kernels: 46.4 us -> 52.5 us
  starting transfers between devices: 54 us -> 49.8 us
    ppermute x26 -> x23, waiting for transfers between devices: 225 us -> 199 us  [the longest x7 169 us: on_device(): outgoing = lax.ppermute(outgoing, 'rows', pairs)]
    unnamed x11 -> x5, local copies, waits for them, and re-layouts: 12.3 us -> 3.04 us
    ppermute x26 -> x23, starting transfers between devices: 41.2 us -> 36.8 us  [the longest x7 13.6 us: on_device(): outgoing = lax.ppermute(outgoing, 'rows', pairs)]
    pallas_call x2, Pallas kernels: 20.9 us -> 24.5 us  [pair_call(): pl.pallas_call(functools.partial(pair_kernel, columns, fresh, joint, per,...]
  transfers between devices with their start and end apart: 38 -> 35, of which waited for: 19 -> 19; matrix products, arithmetic and copies ran while one was open for 2% -> 3% of each run, Pallas kernels for 4% -> 5%
where the time goes in v3:
time: 330 us; the launch traced here: 328 us
  waiting for transfers between devices  211 us (64%)
  Pallas kernels  52.5 us (16%)
  starting transfers between devices  49.8 us (15%)
  other arithmetic  7.1 us (2%)
  local copies, waits for them, and re-layouts  4.98 us (2%)
    ppermute x7, waiting for transfers between devices, on_device(): outgoing = lax.ppermute(outgoing, 'rows', pairs)  169 us
    pallas_call x2, Pallas kernels, pair_call(): pl.pallas_call(functools.partial(pair_kernel, columns, fresh, joint, per,...  24.5 us
    ppermute x10, waiting for transfers between devices, on_device(): lax.ppermute(sums[m], 'rows', [(target, source) for source, target in mer...  20.4 us
    pallas_call x2, Pallas kernels, panel_call(): pl.pallas_call(functools.partial(panel_kernel, rows_all, last, len(grams)...  13.9 us
    ppermute x7, starting transfers between devices, on_device(): outgoing = lax.ppermute(outgoing, 'rows', pairs)  13.6 us
    ppermute x12, starting transfers between devices, sum_over_rows(): lax.ppermute(value, 'rows', [(i, i ^ step * m) for i in range(count)])  13 us
    ppermute x12, waiting for transfers between devices, sum_over_rows(): lax.ppermute(value, 'rows', [(i, i ^ step * m) for i in range(count)])  12.1 us
    ppermute x10, starting transfers between devices, on_device(): lax.ppermute(sums[m], 'rows', [(target, source) for source, target in mer...  10.3 us
  transfers between devices with their start and end apart: 35, of which 19 were waited for; matrix products, arithmetic and copies ran while one was open for 3% of the time, Pallas kernels for 5%

profile of v3, /device:TPU:0, one launch (start us, length us, event | category | flops | bytes accessed | tf_op | source)
XLA Modules:
  0.0 327.9 jit_solution(9842142272010227854)
XLA Ops:
  0.7 0.8 copy.17.pairs
  1.6 5.9 %collective-permute-start = (s32[31]{0:T(128)S(1)}, s32[31]{0:T(128)S(1)}, u32[]{:S(2)}, u32[]{:S(2)}) collective-permute-start(s32[31]{0:T(128)S(1)} %pad_add_fusion.3), channel_id=1, source_target_pairs={{0,8},{1,9},{2,10},{3,11},{4,12},{5,13},{6,14},{7,15},{12,0},{13,1... | collective-permute-start | bytes 380 | tf_op jit(solution)/shard_map/ppermute | solution.py:524
  7.5 5.7 %pack.1.refs_0_ = bf16[2192,1024]{1,0:T(8,128)(2,1)} custom-call(bf16[2048,1024]{1,0:T(8,128)(2,1)} %rows.1, s32[15,2]{1,0:T(8,128)} %copy-done.1, s32[1]{0:T(128)S(6)} %copy.24.live, f32[64,2048]{1,0:T(8,128)} %panel.3), custom_call_target="tpu_custom_call" | custom-call | tf_op jit(solution)/shard_map/pack/pallas_call | solution.py:151
  13.3 1.6 collective-permute-start.2
  14.9 1.3 collective-permute-start.4
  16.2 6.6 %collective-permute-start.5 = (bf16[2192,1024]{1,0:T(8,128)(2,1)}, bf16[2192,1024]{1,0:T(8,128)(2,1)}, u32[]{:S(2)}, u32[]{:S(2)}) collective-permute-start(bf16[2192,1024]{1,0:T(8,128)(2,1)} %pack.1.refs_0_), channel_id=1, source_target_pairs={{0,4},{1,5},{2,6},{3,7},{4,8},{5,9},{6,10},{7,11},{16,20},{17,21},... | collective-permute-start | bytes 13467656 | tf_op jit(solution)/shard_map/ppermute | solution.py:534
  22.8 89.2 %collective-permute-done.2.refs_2_ = bf16[2192,1024]{1,0:T(8,128)(2,1)} collective-permute-done((bf16[2192,1024]{1,0:T(8,128)(2,1)}, bf16[2192,1024]{1,0:T(8,128)(2,1)}, u32[]{:S(2)}, u32[]{:S(2)}) %collective-permute-start.2) | collective-permute-done | bytes 4489248 | tf_op jit(solution)/shard_map/ppermute | solution.py:534
  112.0 3.1 collective-permute-done.4.refs_4_
  115.1 1.2 collective-permute-done.5
  116.3 2.8 collective-permute-start.6
  119.1 1.3 collective-permute-start.7
  120.6 0.7 dynamic-slice_bitcast_fusion
  121.3 0.7 slice_convert_fusion.4
  121.9 0.7 slice_convert_fusion
  122.6 0.6 slice_convert_fusion.2
  123.3 0.7 slice_convert_fusion.3
  124.0 0.6 slice_convert_fusion.1
  125.5 0.7 convert_reduce_fusion
  128.0 0.7 pad_add_fusion.1.span
  128.9 0.6 compare_select_fusion.8
  129.7 2.3 copy-done
  132.0 12.1 %pairs.3 = (f32[28,64,512]{2,1,0:T(8,128)S(1)}, bf16[2,896,512]{2,1,0:T(8,128)(2,1)S(1)}, bf16[20,512,512]{2,1,0:T(8,128)(2,1)}) custom-call(s32[2,20]{1,0:T(2,128)S(1)} %pad_add_fusion.items, s32[2]{0:T(128)S(1)} %pad_add_fusion.1.span, bf16[2192,1024]{1,0:T(8,128)(2,1)S(1)} %copy-done, bf16[2192,1024]{1,0:T(8,128)(2,1)} %collective-permute-done.1.refs_1_, ...), custom_call_target="tpu_custom_call" | custom-call | tf_op jit(solution)/shard_map/pairs/pallas_call | solution.py:329
  144.1 0.7 pad_add_fusion.4.span
  144.8 75.2 %collective-permute-done.7.refs_6_ = bf16[2192,1024]{1,0:T(8,128)(2,1)} collective-permute-done((bf16[2192,1024]{1,0:T(8,128)(2,1)}, bf16[2192,1024]{1,0:T(8,128)(2,1)}, u32[]{:S(2)}, u32[]{:S(2)}) %collective-permute-start.7) | collective-permute-done | bytes 4489248 | tf_op jit(solution)/shard_map/ppermute | solution.py:534
  220.0 12.4 %pairs.4 = (f32[4,64,512]{2,1,0:T(8,128)S(1)}, bf16[4,64,512]{2,1,0:T(8,128)(2,1)S(1)}, bf16[4,64,512]{2,1,0:T(8,128)(2,1)S(1)}, bf16[4,64,512]{2,1,0:T(8,128)(2...) custom-call(s32[2,20]{1,0:T(2,128)S(1)} %pad_add_fusion.items, ...), custom_call_target="tpu_custom_call", output_to_operand_aliasing={{6}: (11, {})} | custom-call | tf_op jit(solution)/shard_map/pairs/pallas_call | solution.py:329
  232.5 0.5 collective-permute-start.8
  233.0 1.3 collective-permute-start.11
  234.3 1.9 collective-permute-start.12
  236.3 0.4 collective-permute-start.10
  236.7 4.2 %collective-permute-done.11.refs_2_ = bf16[4,64,512]{2,1,0:T(8,128)(2,1)S(1)} collective-permute-done((bf16[4,64,512]{2,1,0:T(8,128)(2,1)S(1)}, bf16[4,64,512]{2,1,0:T(8,128)(2,1)S(1)}, u32[]{:S(2)}, u32[]{:S(2)}) %collective-permute-start.11) | collective-permute-done | bytes 262176 | tf_op jit(solution)/shard_map/ppermute | solution.py:555
  240.9 5.1 %collective-permute-done.12.refs_3_ = bf16[4,64,512]{2,1,0:T(8,128)(2,1)S(1)} collective-permute-done((bf16[4,64,512]{2,1,0:T(8,128)(2,1)S(1)}, bf16[4,64,512]{2,1,0:T(8,128)(2,1)S(1)}, u32[]{:S(2)}, u32[]{:S(2)}) %collective-permute-start.12) | collective-permute-done | bytes 262176 | tf_op jit(solution)/shard_map/ppermute | solution.py:555
  246.0 0.6 gram.2
  246.6 0.6 collective-permute-start.15
  247.2 0.6 collective-permute-start.14
  247.8 0.7 collective-permute-start.13
  248.5 1.6 collective-permute-done.15
  250.1 1.0 collective-permute-done.14
  251.1 4.0 %collective-permute-start.18 = (f32[64,64]{1,0:T(8,128)S(1)}, f32[64,64]{1,0:T(8,128)S(1)}, u32[]{:S(2)}, u32[]{:S(2)}) collective-permute-start(f32[64,64]{1,0:T(8,128)S(1)} %add_add_fusion.1.refs_0_), channel_id=1, source_target_pairs={{0,12},{1,13},{2,14},{3,15},{4,8},{5,9},{6,10},{7,11},{8,4},{9,5},... | collective-permute-start | bytes 49160 | tf_op jit(solution)/shard_map/ppermute | solution.py:495
  255.1 0.6 collective-permute-start.16
  255.8 1.3 collective-permute-done.18.refs_3_
  257.0 2.9 collective-permute-done.17.refs_2_
  259.9 6.5 %panel.4.refs_0_ = bf16[128,1024]{1,0:T(8,128)(2,1)S(1)} custom-call(f32[64,64]{1,0:T(8,128)S(1)} %add_add_fusion.1.refs_0_, f32[64,64]{1,0:T(8,128)S(1)} %collective-permute-done.16.refs_1_, f32[64,64]{1,0:T(8,128)S(1)} %collective-permute-done.17.refs_2_, f32[64,64]{1,0:T(8,128)S(1)} %collective-permute-done.18.refs_3_, ...), custom_call_target="tpu_custom_call" | custom-call | tf_op jit(solution)/shard_map/panel/pallas_call | solution.py:480
  266.5 1.4 collective-permute-start.20
  267.9 3.9 %collective-permute-start.23 = (bf16[128,1024]{1,0:T(8,128)(2,1)S(1)}, bf16[128,1024]{1,0:T(8,128)(2,1)S(1)}, u32[]{:S(2)}, u32[]{:S(2)}) collective-permute-start(bf16[128,1024]{1,0:T(8,128)(2,1)S(1)} %panel.4.refs_0_), channel_id=1, source_target_pairs={{0,8},{1,9},{2,10},{3,11},{4,12},{5,13},{6,14},{7,15},{12,0},{13,1... | collective-permute-start | bytes 786440 | tf_op jit(solution)/shard_map/ppermute | solution.py:516
  271.8 1.3 collective-permute-start.22
  273.3 0.4 collective-permute-start.21
  273.7 7.0 %collective-permute-done.23.refs_5_ = bf16[128,1024]{1,0:T(8,128)(2,1)S(1)} collective-permute-done((bf16[128,1024]{1,0:T(8,128)(2,1)S(1)}, bf16[128,1024]{1,0:T(8,128)(2,1)S(1)}, u32[]{:S(2)}, u32[]{:S(2)}) %collective-permute-start.23) | collective-permute-done | bytes 262176 | tf_op jit(solution)/shard_map/ppermute | solution.py:516
  280.8 3.0 collective-permute-done.22.refs_4_
  283.8 7.2 %apply.1 = (f32[4,64,512]{2,1,0:T(8,128)S(1)}, bf16[4,64,512]{2,1,0:T(8,128)(2,1)S(1)}, bf16[4,64,512]{2,1,0:T(8,128)(2,1)S(1)}, bf16[4,64,512]{2,1,0:T(8,128)(2...) custom-call(s32[2,20]{1,0:T(2,128)S(1)} %pad_add_fusion.items, s32[2]{0:T(128)S(1)} %pad_add_fusion.2.span, ...), custom_call_target="tpu_custom_call" | custom-call | tf_op jit(solution)/shard_map/apply/pallas_call | solution.py:383
  291.1 0.5 collective-permute-start.24
  291.6 1.3 collective-permute-start.27
  292.9 2.1 collective-permute-start.28
  295.1 2.1 collective-permute-start.26
  297.2 2.3 collective-permute-done.27.refs_2_
  299.5 8.8 %collective-permute-done.28.refs_3_ = bf16[4,64,512]{2,1,0:T(8,128)(2,1)S(1)} collective-permute-done((bf16[4,64,512]{2,1,0:T(8,128)(2,1)S(1)}, bf16[4,64,512]{2,1,0:T(8,128)(2,1)S(1)}, u32[]{:S(2)}, u32[]{:S(2)}) %collective-permute-start.28) | collective-permute-done | bytes 262176 | tf_op jit(solution)/shard_map/ppermute | solution.py:555
  308.3 0.6 gram.3
  308.9 1.4 collective-permute-start.31
  310.3 0.5 collective-permute-start.30
  310.9 1.6 collective-permute-done.31
  312.4 1.8 collective-permute-done.30
  314.2 0.8 collective-permute-start.34
  315.1 3.6 %collective-permute-start.32 = (f32[64,64]{1,0:T(8,128)S(1)}, f32[64,64]{1,0:T(8,128)S(1)}, u32[]{:S(2)}, u32[]{:S(2)}) collective-permute-start(f32[64,64]{1,0:T(8,128)S(1)} %add_add_fusion.refs_0_), channel_id=1, source_target_pairs={{0,4},{1,5},{2,6},{3,7},{4,0},{5,1},{6,2},{7,3},{8,12},{9,13},{10,... | collective-permute-start | bytes 49160 | tf_op jit(solution)/shard_map/ppermute | solution.py:495
  318.7 1.6 collective-permute-done.34.refs_3_
  320.6 7.3 %panel.5 = f32[64,2048]{1,0:T(8,128)} custom-call(f32[64,64]{1,0:T(8,128)S(1)} %add_add_fusion.refs_0_, f32[64,64]{1,0:T(8,128)S(1)} %collective-permute-done.32.refs_1_, f32[64,64]{1,0:T(8,128)S(1)} %collective-permute-done.33.refs_2_, f32[64,64]{1,0:T(8,128)S(1)} %collective-permute-done.34.refs_3_, f32[4,64,512]{2,1,0:T(8,128)S(1)} %get-tuple-element.52.refs_4_), custom_call_target="tpu_custom_call" | custom-call | tf_op jit(solution)/shard_map/panel/pallas_call | solution.py:480
  (61 shorter events, 3.0 us)
Async XLA Ops:
  1.4 6.1 %copy-start.1 = (s32[15,2]{1,0:T(8,128)}, s32[15,2]{1,0:T(8,128)S(1)}, u32[]{:S(2)}) copy-start(s32[15,2]{1,0:T(8,128)S(1)} %copy.17.pairs) | copy-start | bytes 364
  1.6 11.7 %collective-permute-start = (s32[31]{0:T(128)S(1)}, s32[31]{0:T(128)S(1)}, u32[]{:S(2)}, u32[]{:S(2)}) collective-permute-start(s32[31]{0:T(128)S(1)} %pad_add_fusion.3), channel_id=1, source_target_pairs={{0,8},{1,9},{2,10},{3,11},{4,12},{5,13},{6,14},{7,15},{12,0},{13,1... | collective-permute-start | bytes 380 | tf_op jit(solution)/shard_map/ppermute | solution.py:524
  13.3 98.7 %collective-permute-start.2 = (bf16[2192,1024]{1,0:T(8,128)(2,1)}, bf16[2192,1024]{1,0:T(8,128)(2,1)}, u32[]{:S(2)}, u32[]{:S(2)}) collective-permute-start(bf16[2192,1024]{1,0:T(8,128)(2,1)} %pack.1.refs_0_), channel_id=1, source_target_pairs={{0,2},{1,3},{2,0},{3,1},{4,6},{5,7},{6,4},{7,5},{8,10},{9,11},{10,... | collective-permute-start | bytes 13467656 | tf_op jit(solution)/shard_map/ppermute | solution.py:534
  14.9 100.3 %collective-permute-start.4 = (bf16[2192,1024]{1,0:T(8,128)(2,1)}, bf16[2192,1024]{1,0:T(8,128)(2,1)}, u32[]{:S(2)}, u32[]{:S(2)}) collective-permute-start(bf16[2192,1024]{1,0:T(8,128)(2,1)} %pack.1.refs_0_), channel_id=1, source_target_pairs={{4,0},{5,1},{6,2},{7,3},{8,4},{9,5},{10,6},{11,7},{12,8},{13,9},{1... | collective-permute-start | bytes 13467656 | tf_op jit(solution)/shard_map/ppermute | solution.py:534
  16.2 100.2 %collective-permute-start.5 = (bf16[2192,1024]{1,0:T(8,128)(2,1)}, bf16[2192,1024]{1,0:T(8,128)(2,1)}, u32[]{:S(2)}, u32[]{:S(2)}) collective-permute-start(bf16[2192,1024]{1,0:T(8,128)(2,1)} %pack.1.refs_0_), channel_id=1, source_target_pairs={{0,4},{1,5},{2,6},{3,7},{4,8},{5,9},{6,10},{7,11},{16,20},{17,21},... | collective-permute-start | bytes 13467656 | tf_op jit(solution)/shard_map/ppermute | solution.py:534
  22.8 100.5 %collective-permute-start.1 = (bf16[2192,1024]{1,0:T(8,128)(2,1)}, bf16[2192,1024]{1,0:T(8,128)(2,1)}, u32[]{:S(2)}, u32[]{:S(2)}) collective-permute-start(bf16[2192,1024]{1,0:T(8,128)(2,1)} %pack.1.refs_0_), channel_id=1, source_target_pairs={{0,1},{1,0},{2,3},{3,2},{4,5},{5,4},{6,7},{7,6},{8,9},{9,8},{10,11... | collective-permute-start | bytes 13467656 | tf_op jit(solution)/shard_map/ppermute | solution.py:534
  112.0 11.9 %collective-permute-start.3 = (bf16[2192,1024]{1,0:T(8,128)(2,1)}, bf16[2192,1024]{1,0:T(8,128)(2,1)}, u32[]{:S(2)}, u32[]{:S(2)}) collective-permute-start(bf16[2192,1024]{1,0:T(8,128)(2,1)} %collective-permute-done.2.refs_2_), channel_id=1, source_target_pairs={{0,1},{1,0},{2,3},{3,2},{4,5},{5,4},{6,7},{7,6},{8,9},{9,8},{10,11... | collective-permute-start | bytes 13467656 | tf_op jit(solution)/shard_map/ppermute | solution.py:534
  116.3 28.4 %collective-permute-start.6 = (bf16[2192,1024]{1,0:T(8,128)(2,1)}, bf16[2192,1024]{1,0:T(8,128)(2,1)}, u32[]{:S(2)}, u32[]{:S(2)}) collective-permute-start(bf16[2192,1024]{1,0:T(8,128)(2,1)} %collective-permute-done.5), channel_id=1, source_target_pairs={{4,8},{5,9},{6,10},{7,11},{8,12},{9,13},{10,14},{11,15},{20,24},{2... | collective-permute-start | bytes 13467656 | tf_op jit(solution)/shard_map/ppermute | solution.py:534
  119.1 100.9 %collective-permute-start.7 = (bf16[2192,1024]{1,0:T(8,128)(2,1)}, bf16[2192,1024]{1,0:T(8,128)(2,1)}, u32[]{:S(2)}, u32[]{:S(2)}) collective-permute-start(bf16[2192,1024]{1,0:T(8,128)(2,1)} %pack.1.refs_0_), channel_id=1, source_target_pairs={{12,0},{13,1},{14,2},{15,3},{28,16},{29,17},{30,18},{31,19}} | collective-permute-start | bytes 13467656 | tf_op jit(solution)/shard_map/ppermute | solution.py:534
  129.7 2.3 copy-start
  232.4 3.8 %collective-permute-start.9 = (bf16[4,64,512]{2,1,0:T(8,128)(2,1)S(1)}, bf16[4,64,512]{2,1,0:T(8,128)(2,1)S(1)}, u32[]{:S(2)}, u32[]{:S(2)}) collective-permute-start(bf16[4,64,512]{2,1,0:T(8,128)(2,1)S(1)} %get-tuple-element.39), channel_id=1, source_target_pairs={{1,0},{0,1},{3,2},{2,3},{5,4},{4,5},{7,6},{6,7},{9,8},{8,9},{11,10... | collective-permute-start | bytes 786440 | tf_op jit(solution)/shard_map/ppermute | solution.py:555
  232.5 4.2 %collective-permute-start.8 = (bf16[4,64,512]{2,1,0:T(8,128)(2,1)S(1)}, bf16[4,64,512]{2,1,0:T(8,128)(2,1)S(1)}, u32[]{:S(2)}, u32[]{:S(2)}) collective-permute-start(bf16[4,64,512]{2,1,0:T(8,128)(2,1)S(1)} %get-tuple-element.37), channel_id=1, source_target_pairs={{1,0},{0,1},{3,2},{2,3},{5,4},{4,5},{7,6},{6,7},{9,8},{8,9},{11,10... | collective-permute-start | bytes 786440 | tf_op jit(solution)/shard_map/ppermute | solution.py:555
  233.0 7.9 %collective-permute-start.11 = (bf16[4,64,512]{2,1,0:T(8,128)(2,1)S(1)}, bf16[4,64,512]{2,1,0:T(8,128)(2,1)S(1)}, u32[]{:S(2)}, u32[]{:S(2)}) collective-permute-start(bf16[4,64,512]{2,1,0:T(8,128)(2,1)S(1)} %get-tuple-element.40), channel_id=1, source_target_pairs={{0,4},{1,5},{2,6},{3,7},{4,8},{5,9},{6,10},{7,11},{8,12},{9,13},{1... | collective-permute-start | bytes 786440 | tf_op jit(solution)/shard_map/ppermute | solution.py:555
  234.3 11.7 %collective-permute-start.12 = (bf16[4,64,512]{2,1,0:T(8,128)(2,1)S(1)}, bf16[4,64,512]{2,1,0:T(8,128)(2,1)S(1)}, u32[]{:S(2)}, u32[]{:S(2)}) collective-permute-start(bf16[4,64,512]{2,1,0:T(8,128)(2,1)S(1)} %get-tuple-element.41), channel_id=1, source_target_pairs={{8,0},{9,1},{10,2},{11,3},{12,4},{13,5},{14,6},{15,7},{0,12},{1,13... | collective-permute-start | bytes 786440 | tf_op jit(solution)/shard_map/ppermute | solution.py:555
  236.3 9.7 %collective-permute-start.10 = (bf16[4,64,512]{2,1,0:T(8,128)(2,1)S(1)}, bf16[4,64,512]{2,1,0:T(8,128)(2,1)S(1)}, u32[]{:S(2)}, u32[]{:S(2)}) collective-permute-start(bf16[4,64,512]{2,1,0:T(8,128)(2,1)S(1)} %add.104), channel_id=1, source_target_pairs={{2,0},{3,1},{0,2},{1,3},{6,4},{7,5},{4,6},{5,7},{10,8},{11,9},{8,1... | collective-permute-start | bytes 786440 | tf_op jit(solution)/shard_map/ppermute | solution.py:555
  246.6 3.5 %collective-permute-start.15 = (f32[64,64]{1,0:T(8,128)S(1)}, f32[64,64]{1,0:T(8,128)S(1)}, u32[]{:S(2)}, u32[]{:S(2)}) collective-permute-start(f32[64,64]{1,0:T(8,128)S(1)} %get-tuple-element.42), channel_id=1, source_target_pairs={{0,3},{1,2},{2,1},{3,0},{4,7},{5,6},{6,5},{7,4},{8,11},{9,10},{10,... | collective-permute-start | bytes 49160 | tf_op jit(solution)/shard_map/ppermute | solution.py:495
  247.2 3.9 %collective-permute-start.14 = (f32[64,64]{1,0:T(8,128)S(1)}, f32[64,64]{1,0:T(8,128)S(1)}, u32[]{:S(2)}, u32[]{:S(2)}) collective-permute-start(f32[64,64]{1,0:T(8,128)S(1)} %get-tuple-element.42), channel_id=1, source_target_pairs={{0,2},{1,3},{2,0},{3,1},{4,6},{5,7},{6,4},{7,5},{8,10},{9,11},{10,... | collective-permute-start | bytes 49160 | tf_op jit(solution)/shard_map/ppermute | solution.py:495
  247.8 3.3 collective-permute-start.13
  251.1 5.9 %collective-permute-start.18 = (f32[64,64]{1,0:T(8,128)S(1)}, f32[64,64]{1,0:T(8,128)S(1)}, u32[]{:S(2)}, u32[]{:S(2)}) collective-permute-start(f32[64,64]{1,0:T(8,128)S(1)} %add_add_fusion.1.refs_0_), channel_id=1, source_target_pairs={{0,12},{1,13},{2,14},{3,15},{4,8},{5,9},{6,10},{7,11},{8,4},{9,5},... | collective-permute-start | bytes 49160 | tf_op jit(solution)/shard_map/ppermute | solution.py:495
  255.1 4.8 %collective-permute-start.17 = (f32[64,64]{1,0:T(8,128)S(1)}, f32[64,64]{1,0:T(8,128)S(1)}, u32[]{:S(2)}, u32[]{:S(2)}) collective-permute-start(f32[64,64]{1,0:T(8,128)S(1)} %add_add_fusion.1.refs_0_), channel_id=1, source_target_pairs={{0,8},{1,9},{2,10},{3,11},{4,12},{5,13},{6,14},{7,15},{8,0},{9,1},... | collective-permute-start | bytes 49160 | tf_op jit(solution)/shard_map/ppermute | solution.py:495
  255.1 4.8 %collective-permute-start.16 = (f32[64,64]{1,0:T(8,128)S(1)}, f32[64,64]{1,0:T(8,128)S(1)}, u32[]{:S(2)}, u32[]{:S(2)}) collective-permute-start(f32[64,64]{1,0:T(8,128)S(1)} %add_add_fusion.1.refs_0_), channel_id=1, source_target_pairs={{0,4},{1,5},{2,6},{3,7},{4,0},{5,1},{6,2},{7,3},{8,12},{9,13},{10,... | collective-permute-start | bytes 49160 | tf_op jit(solution)/shard_map/ppermute | solution.py:495
  266.5 6.8 %collective-permute-start.20 = (bf16[128,1024]{1,0:T(8,128)(2,1)S(1)}, bf16[128,1024]{1,0:T(8,128)(2,1)S(1)}, u32[]{:S(2)}, u32[]{:S(2)}) collective-permute-start(bf16[128,1024]{1,0:T(8,128)(2,1)S(1)} %panel.4.refs_0_), channel_id=1, source_target_pairs={{0,2},{1,3},{2,0},{3,1},{4,6},{5,7},{6,4},{7,5},{8,10},{9,11},{10,... | collective-permute-start | bytes 786440 | tf_op jit(solution)/shard_map/ppermute | solution.py:516
  267.9 12.9 %collective-permute-start.23 = (bf16[128,1024]{1,0:T(8,128)(2,1)S(1)}, bf16[128,1024]{1,0:T(8,128)(2,1)S(1)}, u32[]{:S(2)}, u32[]{:S(2)}) collective-permute-start(bf16[128,1024]{1,0:T(8,128)(2,1)S(1)} %panel.4.refs_0_), channel_id=1, source_target_pairs={{0,8},{1,9},{2,10},{3,11},{4,12},{5,13},{6,14},{7,15},{12,0},{13,1... | collective-permute-start | bytes 786440 | tf_op jit(solution)/shard_map/ppermute | solution.py:516
  271.8 12.0 %collective-permute-start.22 = (bf16[128,1024]{1,0:T(8,128)(2,1)S(1)}, bf16[128,1024]{1,0:T(8,128)(2,1)S(1)}, u32[]{:S(2)}, u32[]{:S(2)}) collective-permute-start(bf16[128,1024]{1,0:T(8,128)(2,1)S(1)} %panel.4.refs_0_), channel_id=1, source_target_pairs={{4,0},{5,1},{6,2},{7,3},{8,4},{9,5},{10,6},{11,7},{12,8},{13,9},{1... | collective-permute-start | bytes 786440 | tf_op jit(solution)/shard_map/ppermute | solution.py:516
  273.1 10.7 %collective-permute-start.19 = (bf16[128,1024]{1,0:T(8,128)(2,1)S(1)}, bf16[128,1024]{1,0:T(8,128)(2,1)S(1)}, u32[]{:S(2)}, u32[]{:S(2)}) collective-permute-start(bf16[128,1024]{1,0:T(8,128)(2,1)S(1)} %panel.4.refs_0_), channel_id=1, source_target_pairs={{0,1},{1,0},{2,3},{3,2},{4,5},{5,4},{6,7},{7,6},{8,9},{9,8},{10,11... | collective-permute-start | bytes 786440 | tf_op jit(solution)/shard_map/ppermute | solution.py:516
  273.3 10.5 %collective-permute-start.21 = (bf16[128,1024]{1,0:T(8,128)(2,1)S(1)}, bf16[128,1024]{1,0:T(8,128)(2,1)S(1)}, u32[]{:S(2)}, u32[]{:S(2)}) collective-permute-start(bf16[128,1024]{1,0:T(8,128)(2,1)S(1)} %collective-permute-done.20.refs_2_), channel_id=1, source_target_pairs={{0,1},{1,0},{2,3},{3,2},{4,5},{5,4},{6,7},{7,6},{8,9},{9,8},{10,11... | collective-permute-start | bytes 786440 | tf_op jit(solution)/shard_map/ppermute | solution.py:516
  291.0 4.0 %collective-permute-start.25 = (bf16[4,64,512]{2,1,0:T(8,128)(2,1)S(1)}, bf16[4,64,512]{2,1,0:T(8,128)(2,1)S(1)}, u32[]{:S(2)}, u32[]{:S(2)}) collective-permute-start(bf16[4,64,512]{2,1,0:T(8,128)(2,1)S(1)} %get-tuple-element.48), channel_id=1, source_target_pairs={{1,0},{0,1},{3,2},{2,3},{5,4},{4,5},{7,6},{6,7},{9,8},{8,9},{11,10... | collective-permute-start | bytes 786440 | tf_op jit(solution)/shard_map/ppermute | solution.py:555
  291.1 6.1 %collective-permute-start.24 = (bf16[4,64,512]{2,1,0:T(8,128)(2,1)S(1)}, bf16[4,64,512]{2,1,0:T(8,128)(2,1)S(1)}, u32[]{:S(2)}, u32[]{:S(2)}) collective-permute-start(bf16[4,64,512]{2,1,0:T(8,128)(2,1)S(1)} %get-tuple-element.46), channel_id=1, source_target_pairs={{1,0},{0,1},{3,2},{2,3},{5,4},{4,5},{7,6},{6,7},{9,8},{8,9},{11,10... | collective-permute-start | bytes 786440 | tf_op jit(solution)/shard_map/ppermute | solution.py:555
  291.6 7.9 %collective-permute-start.27 = (bf16[4,64,512]{2,1,0:T(8,128)(2,1)S(1)}, bf16[4,64,512]{2,1,0:T(8,128)(2,1)S(1)}, u32[]{:S(2)}, u32[]{:S(2)}) collective-permute-start(bf16[4,64,512]{2,1,0:T(8,128)(2,1)S(1)} %get-tuple-element.49), channel_id=1, source_target_pairs={{0,4},{1,5},{2,6},{3,7},{4,8},{5,9},{6,10},{7,11},{8,12},{9,13},{1... | collective-permute-start | bytes 786440 | tf_op jit(solution)/shard_map/ppermute | solution.py:555
  292.9 15.4 %collective-permute-start.28 = (bf16[4,64,512]{2,1,0:T(8,128)(2,1)S(1)}, bf16[4,64,512]{2,1,0:T(8,128)(2,1)S(1)}, u32[]{:S(2)}, u32[]{:S(2)}) collective-permute-start(bf16[4,64,512]{2,1,0:T(8,128)(2,1)S(1)} %get-tuple-element.50), channel_id=1, source_target_pairs={{8,0},{9,1},{10,2},{11,3},{12,4},{13,5},{14,6},{15,7},{0,12},{1,13... | collective-permute-start | bytes 786440 | tf_op jit(solution)/shard_map/ppermute | solution.py:555
  295.1 13.2 %collective-permute-start.26 = (bf16[4,64,512]{2,1,0:T(8,128)(2,1)S(1)}, bf16[4,64,512]{2,1,0:T(8,128)(2,1)S(1)}, u32[]{:S(2)}, u32[]{:S(2)}) collective-permute-start(bf16[4,64,512]{2,1,0:T(8,128)(2,1)S(1)} %add.108), channel_id=1, source_target_pairs={{2,0},{3,1},{0,2},{1,3},{6,4},{7,5},{4,6},{5,7},{10,8},{11,9},{8,1... | collective-permute-start | bytes 786440 | tf_op jit(solution)/shard_map/ppermute | solution.py:555
  308.9 3.5 %collective-permute-start.31 = (f32[64,64]{1,0:T(8,128)S(1)}, f32[64,64]{1,0:T(8,128)S(1)}, u32[]{:S(2)}, u32[]{:S(2)}) collective-permute-start(f32[64,64]{1,0:T(8,128)S(1)} %get-tuple-element.51), channel_id=1, source_target_pairs={{0,3},{1,2},{2,1},{3,0},{4,7},{5,6},{6,5},{7,4},{8,11},{9,10},{10,... | collective-permute-start | bytes 49160 | tf_op jit(solution)/shard_map/ppermute | solution.py:495
  310.3 3.9 %collective-permute-start.30 = (f32[64,64]{1,0:T(8,128)S(1)}, f32[64,64]{1,0:T(8,128)S(1)}, u32[]{:S(2)}, u32[]{:S(2)}) collective-permute-start(f32[64,64]{1,0:T(8,128)S(1)} %get-tuple-element.51), channel_id=1, source_target_pairs={{0,2},{1,3},{2,0},{3,1},{4,6},{5,7},{6,4},{7,5},{8,10},{9,11},{10,... | collective-permute-start | bytes 49160 | tf_op jit(solution)/shard_map/ppermute | solution.py:495
  310.8 3.4 %collective-permute-start.29 = (f32[64,64]{1,0:T(8,128)S(1)}, f32[64,64]{1,0:T(8,128)S(1)}, u32[]{:S(2)}, u32[]{:S(2)}) collective-permute-start(f32[64,64]{1,0:T(8,128)S(1)} %get-tuple-element.51), channel_id=1, source_target_pairs={{0,1},{1,0},{2,3},{3,2},{4,5},{5,4},{6,7},{7,6},{8,9},{9,8},{10,11... | collective-permute-start | bytes 49160 | tf_op jit(solution)/shard_map/ppermute | solution.py:495
  314.2 6.0 %collective-permute-start.34 = (f32[64,64]{1,0:T(8,128)S(1)}, f32[64,64]{1,0:T(8,128)S(1)}, u32[]{:S(2)}, u32[]{:S(2)}) collective-permute-start(f32[64,64]{1,0:T(8,128)S(1)} %add_add_fusion.refs_0_), channel_id=1, source_target_pairs={{0,12},{1,13},{2,14},{3,15},{4,8},{5,9},{6,10},{7,11},{8,4},{9,5},... | collective-permute-start | bytes 49160 | tf_op jit(solution)/shard_map/ppermute | solution.py:495
  315.1 5.2 %collective-permute-start.33 = (f32[64,64]{1,0:T(8,128)S(1)}, f32[64,64]{1,0:T(8,128)S(1)}, u32[]{:S(2)}, u32[]{:S(2)}) collective-permute-start(f32[64,64]{1,0:T(8,128)S(1)} %add_add_fusion.refs_0_), channel_id=1, source_target_pairs={{0,8},{1,9},{2,10},{3,11},{4,12},{5,13},{6,14},{7,15},{8,0},{9,1},... | collective-permute-start | bytes 49160 | tf_op jit(solution)/shard_map/ppermute | solution.py:495
  315.1 5.5 %collective-permute-start.32 = (f32[64,64]{1,0:T(8,128)S(1)}, f32[64,64]{1,0:T(8,128)S(1)}, u32[]{:S(2)}, u32[]{:S(2)}) collective-permute-start(f32[64,64]{1,0:T(8,128)S(1)} %add_add_fusion.refs_0_), channel_id=1, source_target_pairs={{0,4},{1,5},{2,6},{3,7},{4,0},{5,1},{6,2},{7,3},{8,12},{9,13},{10,... | collective-permute-start | bytes 49160 | tf_op jit(solution)/shard_map/ppermute | solution.py:495

commit v4 on v3

--- a/solution.py
+++ b/solution.py
@@ -28,6 +28,7 @@
         late = {5, 6}
         after = {6: 4}
         via = {3: 2}
+        after_back = {1: 3, 4: 3}
         hops = {5: [[(i, i + 4) for i in range(8)], [(i, i + 4) for i in range(4, 12)]]}
         joint = [[1], [2], [3], [4], [5, 6]]
     else:
@@ -35,6 +36,7 @@
         late = {5, 6, 7}
         after = {6: 1, 7: 2}
         via = {}
+        after_back = {}
         hops = {}
         joint = [[m] for m in range(1, REACH + 1)]
     hold = -np.ones((count, len(moves) + 1), np.int32)
@@ -58,7 +60,7 @@
         for s, device in enumerate(hold[w]):
             if device >= 0:
                 place[w, device] = s
-    return moves, via, hops, joint, hold, place, work, late, after, int(load.max())
+    return moves, via, after_back, hops, joint, hold, place, work, late, after, int(load.max())
 
 
 def work_list(lists, hold, place, work, late, slots, blocks_here, top, me):
@@ -96,21 +98,14 @@
     return jnp.stack([rows, cols]), jnp.stack([zero, n_first]), jnp.stack([n_first, n_first + n_second])
 
 
-def pack_kernel(rows, pairs, live, panel, out, raw, buf, in_sem, out_sem):
-    count, depth = rows.shape
-    blocks = count // BLOCK
+def extra_kernel(pairs, live, panel, out):
+    depth = out.shape[1]
     per_row = depth // BLOCK
     high = panel.shape[0] // per_row
-    step = 32
-    loads = [
-        pltpu.make_async_copy(rows.at[pl.ds(b * BLOCK, BLOCK)], raw.at[pl.ds(b * BLOCK, BLOCK)], in_sem.at[b])
-        for b in range(blocks)
-    ]
-    for load in loads:
-        load.start()
+    blocks = panel.shape[1] // BLOCK
     for b in range(blocks):
         for q in range(per_row):
-            buf[pl.ds(count + b * high, high), q * BLOCK : (q + 1) * BLOCK] = panel[
+            out[b * high : (b + 1) * high, q * BLOCK : (q + 1) * BLOCK] = panel[
                 q * high : (q + 1) * high, b * BLOCK : (b + 1) * BLOCK
             ].astype(jnp.bfloat16)
     lane = lax.broadcasted_iota(jnp.int32, (LIST_ROWS, LANES), 1)
@@ -118,58 +113,82 @@
     for slot in range(pairs.shape[0]):
         for side in range(2):
             values = jnp.where(lane == 2 * slot + side, pairs[slot, side], values)
-    list_at = count + blocks * high
-    buf[pl.ds(list_at, LIST_ROWS), :LANES] = values.astype(jnp.float32).astype(jnp.bfloat16)
-    buf[pl.ds(list_at, LIST_ROWS), LANES:] = jnp.zeros((LIST_ROWS, depth - LANES), jnp.bfloat16)
-    stores = [(count, blocks * high + LIST_ROWS)] + [(b * BLOCK, BLOCK) for b in range(blocks)]
-    stores = [
-        pltpu.make_async_copy(buf.at[pl.ds(at, size)], out.at[pl.ds(at, size)], out_sem.at[n])
-        for n, (at, size) in enumerate(stores)
-    ]
-    stores[0].start()
+    out[blocks * high :, :LANES] = values.astype(jnp.float32).astype(jnp.bfloat16)
+    out[blocks * high :, LANES:] = jnp.zeros((LIST_ROWS, depth - LANES), jnp.bfloat16)
+
+
+def extra_call(pairs, live, panel, depth):
+    smem = pl.BlockSpec(memory_space=pltpu.SMEM)
+    vmem = pl.BlockSpec(memory_space=pltpu.VMEM)
+    tall = panel.shape[0] * panel.shape[1] // depth + LIST_ROWS
+    return pl.pallas_call(
+        extra_kernel,
+        out_shape=jax.ShapeDtypeStruct((tall, depth), jnp.bfloat16),
+        in_specs=[smem, smem, vmem],
+        out_specs=vmem,
+        compiler_params=pltpu.CompilerParams(vmem_limit_bytes=VMEM_LIMIT),
+        name="extra",
+    )(pairs, live, panel)
+
+
+def unit_kernel(rows, out, raw, buf, scale, in_sem, out_sem):
+    count, depth = rows.shape
+    blocks = count // BLOCK
+    step = 16
+    parts = [pl.ds(b * BLOCK, BLOCK) for b in range(blocks)]
+    loads = [pltpu.make_async_copy(rows.at[at], raw.at[at], in_sem.at[b]) for b, at in enumerate(parts)]
+    stores = [pltpu.make_async_copy(buf.at[at], out.at[at], out_sem.at[b]) for b, at in enumerate(parts)]
+    for load in loads:
+        load.start()
     for b in range(blocks):
         loads[b].wait()
 
-        @pl.loop(0, BLOCK // step, unroll=4)
+        @pl.loop(0, BLOCK // step, unroll=8)
+        def _(i):
+            values = raw[pl.ds(pl.multiple_of(b * BLOCK + i * step, step), step), :].astype(jnp.float32)
+            mean = jnp.sum(values * values, axis=-1, keepdims=True) * (1.0 / depth)
+            factor = lax.rsqrt(mean + 1e-06) * depth ** (-0.5)
+            scale[pl.ds(pl.multiple_of(i * step, step), step), :] = jnp.broadcast_to(factor, (step, LANES))
+
+        @pl.loop(0, BLOCK // step, unroll=8)
         def _(i):
             at = pl.ds(pl.multiple_of(b * BLOCK + i * step, step), step)
-            values = raw[at, :].astype(jnp.float32)
-            mean = jnp.sum(values * values, axis=-1, keepdims=True) * (1.0 / depth)
-            factor = lax.rsqrt(mean + 1e-06) * depth ** (-0.5)
-            buf[at, :] = (values * factor).astype(jnp.bfloat16)
-
-        stores[b + 1].start()
+            factor = scale[pl.ds(pl.multiple_of(i * step, step), step), :]
+            for lane in range(0, depth, LANES):
+                values = raw[at, lane : lane + LANES].astype(jnp.float32)
+                buf[at, lane : lane + LANES] = (values * factor).astype(jnp.bfloat16)
+
+        stores[b].start()
     for store in stores:
         store.wait()
 
 
-def pack_call(embeddings, pairs, live, panel):
-    rows, depth = embeddings.shape
-    blocks = rows // BLOCK
-    tall = rows + panel.shape[0] * panel.shape[1] // depth + LIST_ROWS
-    smem = pl.BlockSpec(memory_space=pltpu.SMEM)
+def unit_call(embeddings):
+    blocks = embeddings.shape[0] // BLOCK
     return pl.pallas_call(
-        pack_kernel,
-        out_shape=jax.ShapeDtypeStruct((tall, depth), jnp.bfloat16),
-        in_specs=[pl.BlockSpec(memory_space=pltpu.HBM), smem, smem, pl.BlockSpec(memory_space=pltpu.VMEM)],
+        unit_kernel,
+        out_shape=jax.ShapeDtypeStruct(embeddings.shape, jnp.bfloat16),
+        in_specs=[pl.BlockSpec(memory_space=pltpu.HBM)],
         out_specs=pl.BlockSpec(memory_space=pltpu.HBM),
         scratch_shapes=[
-            pltpu.VMEM((rows, depth), jnp.bfloat16),
-            pltpu.VMEM((tall, depth), jnp.bfloat16),
+            pltpu.VMEM(embeddings.shape, jnp.bfloat16),
+            pltpu.VMEM(embeddings.shape, jnp.bfloat16),
+            pltpu.VMEM((BLOCK, LANES), jnp.float32),
             pltpu.SemaphoreType.DMA((blocks,)),
-            pltpu.SemaphoreType.DMA((blocks + 1,)),
+            pltpu.SemaphoreType.DMA((blocks,)),
         ],
         compiler_params=pltpu.CompilerParams(vmem_limit_bytes=VMEM_MOST),
-        name="pack",
-    )(embeddings, pairs, live, panel)
-
-
-def fill_panel(refs, columns, at, size, pan, sem):
+        name="unit",
+    )(embeddings)
+
+
+def fill_panel(refs, joint, pan, sem):
     per_row = pan.shape[0]
+    size = pan.shape[1] // (1 + sum(len(group) for group in joint))
     copies = []
-    for ref, s in zip(refs, columns):
+    for ref, s in [(refs[0], 0)] + [(ref, s) for ref, group in zip(refs[1:], joint) for s in group]:
         for q in range(per_row):
-            source = ref.at[pl.ds(at, size), pl.ds(q * BLOCK, BLOCK)]
+            source = ref.at[pl.ds(0, size), pl.ds(q * BLOCK, BLOCK)]
             copies.append(
                 pltpu.make_async_copy(source, pan.at[q, pl.ds(s * size, size)], sem.at[len(copies)])
             )
@@ -202,10 +221,12 @@
         back[...] = sum(acc[pl.ds(s * per, per)] for s in columns).astype(jnp.bfloat16)
 
 
-def pair_kernel(columns, fresh, joint, per, first, final, items, span, *refs):
+def pair_kernel(columns, joint, per, first, final, items, span, *refs):
     n_unit = len(columns)
     units, refs = refs[:n_unit], refs[n_unit:]
-    if not first:
+    if first:
+        panels, refs = refs[: len(joint) + 1], refs[len(joint) + 1 :]
+    else:
         acc_in, pan_in, _, refs = refs[0], refs[1], refs[2], refs[3:]
     if final:
         own, refs = refs[0], refs[1:]
@@ -236,13 +257,13 @@
         fetch(begin, begin % 2)
 
     if first:
+        copies = fill_panel(panels, joint, pan, psem)
         acc[...] = jnp.zeros_like(acc)
+        for copy in copies:
+            copy.wait()
     else:
         acc[...] = acc_in[...]
         pan[...] = pan_in[...]
-    size = units[0].shape[0] - per * BLOCK - LIST_ROWS
-    for copy in fill_panel(units[fresh:], columns[fresh:], per * BLOCK, size, pan, psem):
-        copy.wait()
 
     @pl.loop(begin, end)
     def _(i):
@@ -259,18 +280,11 @@
         def _():
             store(i - 2, slot).wait()
 
-        half = BLOCK // 2
-        halves = []
-        for part in range(2):
-            scores = lax.dot_general(
-                ubuf[slot, 0, pl.ds(part * half, half), :],
-                ubuf[slot, 1],
-                (((1,), (1,)), ((), ())),
-                preferred_element_type=jnp.float32,
-            )
-            power = scores * (SHARPNESS * LOG2E)
-            halves.append((jnp.exp2(power - 1.0) - jnp.exp2(-1.0 - power)).astype(jnp.bfloat16))
-        aff = jnp.concatenate(halves, axis=0)
+        scores = lax.dot_general(
+            ubuf[slot, 0], ubuf[slot, 1], (((1,), (1,)), ((), ())), preferred_element_type=jnp.float32
+        )
+        power = scores * (SHARPNESS * LOG2E)
+        aff = (jnp.exp2(power - 1.0) - jnp.exp2(-1.0 - power)).astype(jnp.bfloat16)
         affbuf[slot] = aff
         store(i, slot).start()
         add_products(pan, acc, aff, items[0, i], items[1, i])
@@ -291,8 +305,9 @@
     ] * sends
 
 
-def pair_call(items, span, units, columns, fresh, joint, per, width, top, state, final):
-    blocks = (1 + sum(len(group) for group in joint)) * per
+def pair_call(items, span, units, columns, panels, joint, per, width, top, state, final):
+    held = 1 + sum(len(group) for group in joint)
+    blocks = held * per
     depth = units[0].shape[1]
     per_row = depth // BLOCK
     smem = pl.BlockSpec(memory_space=pltpu.SMEM)
@@ -307,7 +322,7 @@
         pltpu.VMEM((2, 2, BLOCK, depth), jnp.bfloat16),
         pltpu.VMEM((2, BLOCK, BLOCK), jnp.bfloat16),
         pltpu.SemaphoreType.DMA((2, 2)),
-        pltpu.SemaphoreType.DMA((len(units) * per_row,)),
+        pltpu.SemaphoreType.DMA((held * per_row,)),
         pltpu.SemaphoreType.DMA((2,)),
     ]
     if final:
@@ -322,12 +337,15 @@
         ]
         out_specs = [vmem, vmem, anywhere]
     aliases = {}
-    if state is not None:
+    if state is None:
+        operands += panels
+        in_specs += [pl.BlockSpec(memory_space=pl.ANY)] * len(panels)
+    else:
         aliases = {len(operands) + 2: len(out_shape) - 1}
         operands += list(state)
         in_specs += [vmem, vmem, anywhere]
     return pl.pallas_call(
-        functools.partial(pair_kernel, columns, fresh, joint, per, state is None, final),
+        functools.partial(pair_kernel, columns, joint, per, state is None, final),
         out_shape=out_shape,
         in_specs=in_specs,
         out_specs=out_specs,
@@ -354,8 +372,7 @@
         def _():
             load(ahead, ahead).start()
 
-    spots = [(panels[0], 0)] + [(ref, s) for ref, group in zip(panels[1:], joint) for s in group]
-    copies = fill_panel([ref for ref, _ in spots], [s for _, s in spots], 0, panels[0].shape[0], pan, psem)
+    copies = fill_panel(panels, joint, pan, psem)
     acc[...] = jnp.zeros_like(acc)
     for copy in copies:
         copy.wait()
@@ -434,15 +451,33 @@
     row_id = lax.broadcasted_iota(jnp.int32, (width, width), 0)
     col_id = lax.broadcasted_iota(jnp.int32, (width, width), 1)
     table = jnp.concatenate([gram, (row_id == col_id).astype(jnp.float32)], axis=1)
-    below = lax.broadcasted_iota(jnp.int32, (width, 1), 0)
-    scale = jnp.zeros((width, 1), jnp.float32)
-    for k in range(width):
-        line = table[k : k + 1, :]
-        pivot = table[k : k + 1, k : k + 1]
-        scale = jnp.where(below == k, pivot, scale)
-        factor = jnp.where(below > k, table[:, k : k + 1] / pivot, 0.0)
-        table = table - factor * line
-    return table[:, width:] / jnp.sqrt(scale)
+    tile = 8
+    tiles = [table[at : at + tile] for at in range(0, width, tile)]
+    shape = tiles[0].shape
+    inner = lax.broadcasted_iota(jnp.int32, shape, 0)
+    scales = [None] * len(tiles)
+    for k in range(0, width, 2):
+        home, at = k // tile, k % tile
+        line0, line1 = tiles[home][at : at + 1], tiles[home][at + 1 : at + 2]
+        cols0 = {g: jnp.broadcast_to(tiles[g][:, k : k + 1], shape) for g in range(home, len(tiles))}
+        cols1 = {g: jnp.broadcast_to(tiles[g][:, k + 1 : k + 2], shape) for g in range(home, len(tiles))}
+        a = cols0[home][at : at + 1]
+        b = cols0[home][at + 1 : at + 2]
+        c = cols1[home][at + 1 : at + 2]
+        inv_a = 1.0 / a
+        inv_s = a / (a * c - b * b)
+        line1 = line1 - (b * inv_a) * line0
+        line0 = inv_a * line0
+        for g in range(home, len(tiles)):
+            first = cols0[g] * line0
+            second = ((cols1[g] - cols0[g] * (b * inv_a)) * inv_s) * line1
+            if g == home:
+                first = jnp.where(inner > at, first, 0.0)
+                second = jnp.where(inner > at + 1, second, 0.0)
+                old = scales[g] if at else jnp.zeros(shape, jnp.float32)
+                scales[g] = jnp.where(inner == at, inv_a, jnp.where(inner == at + 1, inv_s, old))
+            tiles[g] = tiles[g] - first - second
+    return jnp.concatenate([t[:, width:] * jnp.sqrt(z[:, :width]) for t, z in zip(tiles, scales)], axis=0)
 
 
 def panel_kernel(rows_all, last, n_gram, *refs):
@@ -505,10 +540,14 @@
     per = embeddings.shape[0] // BLOCK
     width = start_panel.shape[0]
     slots = block_pairs.shape[0]
-    moves, via, hops, joint, hold, place, work, late, after, top = make_plan(count)
+    moves, via, after_back, hops, joint, hold, place, work, late, after, top = make_plan(count)
     held = len(moves) + 1
 
     merged = [functools.reduce(list.__add__, [moves[s - 1] for s in group]) for group in joint]
+
+    direct = [
+        [(int(hold[w, s]), w) for s in group for w in range(count) if hold[w, s] >= 0] for group in joint
+    ]
 
     def spread(value):
         got = [value]
@@ -517,42 +556,40 @@
         return got
 
     assert count * per <= 256
-    own_list = jnp.concatenate([block_pairs.reshape(-1), pair_count])
-    lists = {}
-    for group, pairs in zip(joint, merged):
-        if group[0] in late:
-            part = lax.ppermute(own_list, "rows", pairs)
-            lists.update({m: part for m in group})
-    packed = pack_call(embeddings, block_pairs, pair_count, start_panel)
-    packed, lists = lax.optimization_barrier((packed, lists))
-    units = {0: packed}
+    extra = extra_call(block_pairs, pair_count, start_panel, depth)
+    extras = [extra] + [lax.ppermute(extra, "rows", pairs) for pairs in direct]
+    unit = unit_call(embeddings)
+    settled, extras = lax.optimization_barrier((unit, extras))
+    units = {0: unit}
     for m in range(1, len(moves) + 1):
-        outgoing = units[via.get(m, 0)]
+        outgoing = units[via[m]] if m in via else unit if m in hops or m in after.values() else settled
         if m in after:
             outgoing, _ = lax.optimization_barrier((outgoing, units[after[m]]))
         for pairs in hops.get(m, [moves[m - 1]]):
             outgoing = lax.ppermute(outgoing, "rows", pairs)
         units[m] = outgoing
-    for m, unit in units.items():
-        if m not in lists:
-            lists[m] = unit[unit.shape[0] - 1, : own_list.shape[0]].astype(jnp.int32)
-    lists = jnp.stack([lists[m] for m in range(held)])
+    lists = [part[part.shape[0] - LIST_ROWS, : 2 * slots + 1].astype(jnp.int32) for part in extras]
+    lists = jnp.stack(lists[:1] + [part for part, group in zip(lists[1:], joint) for _ in group])
     items, span_first, span_second = work_list(lists, hold, place, work, late, slots, per, top, me)
     span_all = jnp.stack([span_first[0], span_second[1]])
 
     early = [s for s in range(held) if s not in late]
     order = early + sorted(late)
-    state = pair_call(items, span_first, [units[s] for s in early], early, 0, joint, per, width, top, None, False)
+    state = pair_call(items, span_first, [units[s] for s in early], early, extras, joint, per, width, top, None, False)
     *sums, aff = pair_call(
-        items, span_second, [units[s] for s in order], order, len(early), joint, per, width, top, state, True
+        items, span_second, [units[s] for s in order], order, None, joint, per, width, top, state, True
     )
 
     for sweep in range(ITERS):
         if sweep > 0:
             sums = apply_call(items, span_all, spread(panel), joint, aff, per, width)
-        sums, backs = list(sums), []
+        sums, backs, gone = list(sums), [], {}
         for m in sorted(range(1, len(joint) + 1), key=lambda m: m not in via):
-            back = lax.ppermute(sums[m], "rows", [(target, source) for source, target in merged[m - 1]])
+            outgoing = sums[m]
+            if m in after_back:
+                outgoing, _ = lax.optimization_barrier((outgoing, gone[after_back[m]]))
+            back = lax.ppermute(outgoing, "rows", [(target, source) for source, target in merged[m - 1]])
+            gone[m] = back
             if m in via:
                 sums[via[m]] = sums[via[m]] + back
             else:

time: 330 us -> 321 us (0.973)
  Pallas kernels: 52.5 us -> 41.1 us
    ppermute x11 -> x15, waiting for transfers between devices: 20.4 us -> 27.9 us  [the longest x10 21 us: on_device(): lax.ppermute(outgoing, 'rows', [(target, source) for source, target in me...]
    pallas_call x2, Pallas kernels: 13.9 us -> 8.07 us  [panel_call(): pl.pallas_call(functools.partial(panel_kernel, rows_all, last, len(grams)...]
    pallas_call x3 -> x4, Pallas kernels: 30.2 us -> 25.7 us  [the longest x2 19.4 us: pair_call(): pl.pallas_call(functools.partial(pair_kernel, columns, joint, per, state...]
    ppermute x7, waiting for transfers between devices: 169 us -> 165 us  [on_device(): outgoing = lax.ppermute(outgoing, 'rows', pairs)]
    convert_element_type x5 -> x0, other arithmetic: 3.31 us -> none  [on_device(): lists[m] = unit[unit.shape[0] - 1, :own_list.shape[0]].astype(jnp.int32)]
    ppermute x11 -> x15, starting transfers between devices: 16.2 us -> 18.1 us  [the longest x5 9.16 us: on_device(): extras = [extra] + [lax.ppermute(extra, 'rows', pairs) for pairs in direct]]
  transfers between devices with their start and end apart: 35 -> 39, of which waited for: 19 -> 20; matrix products, arithmetic and copies ran while one was open for 3% -> 2% of each run, Pallas kernels for 5% -> 4%
where the time goes in v4:
time: 321 us; the launch traced here: 318 us
  waiting for transfers between devices  214 us (67%)
  starting transfers between devices  50.5 us (16%)
  Pallas kernels  41.1 us (13%)
  local copies, waits for them, and re-layouts  5.87 us (2%)
  other arithmetic  3.94 us (1%)
    ppermute x7, waiting for transfers between devices, on_device(): outgoing = lax.ppermute(outgoing, 'rows', pairs)  165 us
    ppermute x10, waiting for transfers between devices, on_device(): lax.ppermute(outgoing, 'rows', [(target, source) for source, target in me...  21 us
    pallas_call x2, Pallas kernels, pair_call(): pl.pallas_call(functools.partial(pair_kernel, columns, joint, per, state...  19.4 us
    ppermute x12, starting transfers between devices, sum_over_rows(): lax.ppermute(value, 'rows', [(i, i ^ step * m) for i in range(count)])  13.3 us
    ppermute x7, starting transfers between devices, on_device(): outgoing = lax.ppermute(outgoing, 'rows', pairs)  12.2 us
    ppermute x12, waiting for transfers between devices, sum_over_rows(): lax.ppermute(value, 'rows', [(i, i ^ step * m) for i in range(count)])  12.2 us
    ppermute x5, waiting for transfers between devices, spread(): got.append(lax.ppermute(got[via.get(group[0], 0)], 'rows', pairs))  9.33 us
    ppermute x5, starting transfers between devices, on_device(): extras = [extra] + [lax.ppermute(extra, 'rows', pairs) for pairs in direct]  9.16 us
  transfers between devices with their start and end apart: 39, of which 20 were waited for; matrix products, arithmetic and copies ran while one was open for 2% of the time, Pallas kernels for 4%

profile of v4, /device:TPU:0, one launch (start us, length us, event | category | flops | bytes accessed | tf_op | source)
XLA Modules:
  0.0 318.0 jit_solution(10610647518507925485)
XLA Ops:
  0.7 0.8 copy.15.pairs
  1.4 1.0 copy-done.2
  2.5 0.7 extra.1.refs_5_
  3.2 5.9 %collective-permute-start.4 = (bf16[144,1024]{1,0:T(8,128)(2,1)S(1)}, bf16[144,1024]{1,0:T(8,128)(2,1)S(1)}, u32[]{:S(2)}, u32[]{:S(2)}) collective-permute-start(bf16[144,1024]{1,0:T(8,128)(2,1)S(1)} %extra.1.refs_5_), channel_id=1, source_target_pairs={{0,8},{1,9},{2,10},{3,11},{4,12},{5,13},{6,14},{7,15},{12,0},{13,1... | collective-permute-start | bytes 884744 | tf_op jit(solution)/shard_map/ppermute | solution.py:560
  9.1 1.3 collective-permute-start.3
  10.4 0.7 collective-permute-start.2
  11.2 0.9 collective-permute-start.1
  12.3 5.6 %unit.1.refs_0_ = bf16[2048,1024]{1,0:T(8,128)(2,1)} custom-call(bf16[2048,1024]{1,0:T(8,128)(2,1)} %rows.1), custom_call_target="tpu_custom_call" | custom-call | tf_op jit(solution)/shard_map/unit/pallas_call | solution.py:168
  18.0 1.3 collective-permute-start.8
  19.3 4.2 %collective-permute-done.3.refs_9_ = bf16[144,1024]{1,0:T(8,128)(2,1)S(1)} collective-permute-done((bf16[144,1024]{1,0:T(8,128)(2,1)S(1)}, bf16[144,1024]{1,0:T(8,128)(2,1)S(1)}, u32[]{:S(2)}, u32[]{:S(2)}) %collective-permute-start.3) | collective-permute-done | bytes 294944 | tf_op jit(solution)/shard_map/ppermute | solution.py:560
  23.4 2.7 collective-permute-done.1.refs_7_
  26.1 1.0 collective-permute-start.6
  27.1 6.0 %collective-permute-start.9 = (bf16[2048,1024]{1,0:T(8,128)(2,1)}, bf16[2048,1024]{1,0:T(8,128)(2,1)}, u32[]{:S(2)}, u32[]{:S(2)}) collective-permute-start(bf16[2048,1024]{1,0:T(8,128)(2,1)} %unit.1.refs_0_), channel_id=1, source_target_pairs={{0,4},{1,5},{2,6},{3,7},{4,8},{5,9},{6,10},{7,11},{16,20},{17,21},... | collective-permute-start | bytes 12582920 | tf_op jit(solution)/shard_map/ppermute | solution.py:569
  33.2 83.0 %collective-permute-done.8.refs_4_ = bf16[2048,1024]{1,0:T(8,128)(2,1)} collective-permute-done((bf16[2048,1024]{1,0:T(8,128)(2,1)}, bf16[2048,1024]{1,0:T(8,128)(2,1)}, u32[]{:S(2)}, u32[]{:S(2)}) %collective-permute-start.8) | collective-permute-done | bytes 4194336 | tf_op jit(solution)/shard_map/ppermute | solution.py:569
  116.1 2.8 collective-permute-done.6.refs_2_
  119.0 2.5 collective-permute-done.9
  121.5 2.6 collective-permute-start.10
  124.1 1.3 collective-permute-start.11
  125.5 0.7 dynamic-slice_bitcast_fusion
  127.2 0.8 convert_reduce_fusion
  129.8 0.8 pad_add_fusion.3.span
  130.5 0.8 pad_add_fusion.1.span
  131.5 0.7 compare_select_fusion.8
  132.4 2.2 copy-done
  134.6 8.7 %pairs.3 = (f32[28,64,512]{2,1,0:T(8,128)S(1)}, bf16[2,896,512]{2,1,0:T(8,128)(2,1)S(1)}, bf16[20,512,512]{2,1,0:T(8,128)(2,1)}) custom-call(s32[2,20]{1,0:T(2,128)S(1)} %pad_add_fusion.items, s32[2]{0:T(128)S(1)} %pad_add_fusion.1.span, bf16[2048,1024]{1,0:T(8,128)(2,1)S(1)} %copy-done, bf16[2048,1024]{1,0:T(8,128)(2,1)} %collective-permute-done.5.refs_1_, ...), custom_call_target="tpu_custom_call" | custom-call | tf_op jit(solution)/shard_map/pairs/pallas_call | solution.py:347
  143.2 76.5 %collective-permute-done.11.refs_6_ = bf16[2048,1024]{1,0:T(8,128)(2,1)} collective-permute-done((bf16[2048,1024]{1,0:T(8,128)(2,1)}, bf16[2048,1024]{1,0:T(8,128)(2,1)}, u32[]{:S(2)}, u32[]{:S(2)}) %collective-permute-start.11) | collective-permute-done | bytes 4194336 | tf_op jit(solution)/shard_map/ppermute | solution.py:569
  219.7 10.8 %pairs.4 = (f32[4,64,512]{2,1,0:T(8,128)S(1)}, bf16[4,64,512]{2,1,0:T(8,128)(2,1)S(1)}, bf16[4,64,512]{2,1,0:T(8,128)(2,1)S(1)}, bf16[4,64,512]{2,1,0:T(8,128)(2...) custom-call(s32[2,20]{1,0:T(2,128)S(1)} %pad_add_fusion.items, ...), custom_call_target="tpu_custom_call", output_to_operand_aliasing={{6}: (11, {})} | custom-call | tf_op jit(solution)/shard_map/pairs/pallas_call | solution.py:347
  230.6 1.9 collective-permute-start.16
  232.5 0.6 collective-permute-start.13
  233.1 1.3 collective-permute-start.15
  234.5 7.5 %collective-permute-done.16.refs_3_ = bf16[4,64,512]{2,1,0:T(8,128)(2,1)S(1)} collective-permute-done((bf16[4,64,512]{2,1,0:T(8,128)(2,1)S(1)}, bf16[4,64,512]{2,1,0:T(8,128)(2,1)S(1)}, u32[]{:S(2)}, u32[]{:S(2)}) %collective-permute-start.16) | collective-permute-done | bytes 262176 | tf_op jit(solution)/shard_map/ppermute | solution.py:591
  242.1 2.5 collective-permute-done.15.refs_2_
  244.6 0.6 gram.2
  245.3 1.5 collective-permute-start.18
  246.8 0.3 collective-permute-start.17
  247.1 1.7 collective-permute-done.19
  248.9 0.8 collective-permute-done.18
  249.7 4.3 %collective-permute-start.22 = (f32[64,64]{1,0:T(8,128)S(1)}, f32[64,64]{1,0:T(8,128)S(1)}, u32[]{:S(2)}, u32[]{:S(2)}) collective-permute-start(f32[64,64]{1,0:T(8,128)S(1)} %add_add_fusion.1.refs_0_), channel_id=1, source_target_pairs={{0,12},{1,13},{2,14},{3,15},{4,8},{5,9},{6,10},{7,11},{8,4},{9,5},... | collective-permute-start | bytes 49160 | tf_op jit(solution)/shard_map/ppermute | solution.py:530
  254.0 0.6 collective-permute-start.20
  254.7 1.3 collective-permute-done.22.refs_3_
  255.9 2.9 collective-permute-done.21.refs_2_
  258.8 3.6 %panel.4.refs_0_ = bf16[128,1024]{1,0:T(8,128)(2,1)S(1)} custom-call(f32[64,64]{1,0:T(8,128)S(1)} %add_add_fusion.1.refs_0_, f32[64,64]{1,0:T(8,128)S(1)} %collective-permute-done.20.refs_1_, f32[64,64]{1,0:T(8,128)S(1)} %collective-permute-done.21.refs_2_, f32[64,64]{1,0:T(8,128)S(1)} %collective-permute-done.22.refs_3_, ...), custom_call_target="tpu_custom_call" | custom-call | tf_op jit(solution)/shard_map/panel/pallas_call | solution.py:515
  262.5 1.3 collective-permute-start.24
  263.8 3.9 %collective-permute-start.27 = (bf16[128,1024]{1,0:T(8,128)(2,1)S(1)}, bf16[128,1024]{1,0:T(8,128)(2,1)S(1)}, u32[]{:S(2)}, u32[]{:S(2)}) collective-permute-start(bf16[128,1024]{1,0:T(8,128)(2,1)S(1)} %panel.4.refs_0_), channel_id=1, source_target_pairs={{0,8},{1,9},{2,10},{3,11},{4,12},{5,13},{6,14},{7,15},{12,0},{13,1... | collective-permute-start | bytes 786440 | tf_op jit(solution)/shard_map/ppermute | solution.py:555
  267.7 1.3 collective-permute-start.26
  269.2 0.4 collective-permute-start.25
  269.7 6.6 %collective-permute-done.27.refs_5_ = bf16[128,1024]{1,0:T(8,128)(2,1)S(1)} collective-permute-done((bf16[128,1024]{1,0:T(8,128)(2,1)S(1)}, bf16[128,1024]{1,0:T(8,128)(2,1)S(1)}, u32[]{:S(2)}, u32[]{:S(2)}) %collective-permute-start.27) | collective-permute-done | bytes 262176 | tf_op jit(solution)/shard_map/ppermute | solution.py:555
  276.2 2.7 collective-permute-done.26.refs_4_
  278.9 6.1 %apply.1 = (f32[4,64,512]{2,1,0:T(8,128)S(1)}, bf16[4,64,512]{2,1,0:T(8,128)(2,1)S(1)}, bf16[4,64,512]{2,1,0:T(8,128)(2,1)S(1)}, bf16[4,64,512]{2,1,0:T(8,128)(2...) custom-call(s32[2,20]{1,0:T(2,128)S(1)} %pad_add_fusion.items, s32[2]{0:T(128)S(1)} %pad_add_fusion.2.span, ...), custom_call_target="tpu_custom_call" | custom-call | tf_op jit(solution)/shard_map/apply/pallas_call | solution.py:400
  285.1 1.9 collective-permute-start.32
  287.0 0.6 collective-permute-start.29
  287.6 1.5 collective-permute-start.31
  289.1 1.0 collective-permute-start.30
  290.1 10.9 %collective-permute-done.32.refs_3_ = bf16[4,64,512]{2,1,0:T(8,128)(2,1)S(1)} collective-permute-done((bf16[4,64,512]{2,1,0:T(8,128)(2,1)S(1)}, bf16[4,64,512]{2,1,0:T(8,128)(2,1)S(1)}, u32[]{:S(2)}, u32[]{:S(2)}) %collective-permute-start.32) | collective-permute-done | bytes 262176 | tf_op jit(solution)/shard_map/ppermute | solution.py:591
  301.0 0.6 gram.3
  301.7 0.7 collective-permute-start.35
  302.3 1.1 collective-permute-start.34
  303.6 1.6 collective-permute-done.35
  305.2 1.1 collective-permute-done.34
  306.3 2.4 collective-permute-start.38
  308.7 2.0 collective-permute-start.36
  310.7 1.3 collective-permute-done.38.refs_3_
  312.0 1.5 collective-permute-done.37.refs_2_
  313.5 4.4 %panel.5 = f32[64,2048]{1,0:T(8,128)} custom-call(f32[64,64]{1,0:T(8,128)S(1)} %add_add_fusion.refs_0_, f32[64,64]{1,0:T(8,128)S(1)} %collective-permute-done.36.refs_1_, f32[64,64]{1,0:T(8,128)S(1)} %collective-permute-done.37.refs_2_, f32[64,64]{1,0:T(8,128)S(1)} %collective-permute-done.38.refs_3_, f32[4,64,512]{2,1,0:T(8,128)S(1)} %get-tuple-element.68.refs_4_), custom_call_target="tpu_custom_call" | custom-call | tf_op jit(solution)/shard_map/panel/pallas_call | solution.py:515
  (72 shorter events, 3.1 us)
Async XLA Ops:
  1.4 1.0 copy-start.2
  3.2 14.8 %collective-permute-start.4 = (bf16[144,1024]{1,0:T(8,128)(2,1)S(1)}, bf16[144,1024]{1,0:T(8,128)(2,1)S(1)}, u32[]{:S(2)}, u32[]{:S(2)}) collective-permute-start(bf16[144,1024]{1,0:T(8,128)(2,1)S(1)} %extra.1.refs_5_), channel_id=1, source_target_pairs={{0,8},{1,9},{2,10},{3,11},{4,12},{5,13},{6,14},{7,15},{12,0},{13,1... | collective-permute-start | bytes 884744 | tf_op jit(solution)/shard_map/ppermute | solution.py:560
  9.1 14.3 %collective-permute-start.3 = (bf16[144,1024]{1,0:T(8,128)(2,1)S(1)}, bf16[144,1024]{1,0:T(8,128)(2,1)S(1)}, u32[]{:S(2)}, u32[]{:S(2)}) collective-permute-start(bf16[144,1024]{1,0:T(8,128)(2,1)S(1)} %extra.1.refs_5_), channel_id=1, source_target_pairs={{4,0},{5,1},{6,2},{7,3},{8,4},{9,5},{10,6},{11,7},{12,8},{13,9},{1... | collective-permute-start | bytes 884744 | tf_op jit(solution)/shard_map/ppermute | solution.py:560
  10.4 13.0 %collective-permute-start.2 = (bf16[144,1024]{1,0:T(8,128)(2,1)S(1)}, bf16[144,1024]{1,0:T(8,128)(2,1)S(1)}, u32[]{:S(2)}, u32[]{:S(2)}) collective-permute-start(bf16[144,1024]{1,0:T(8,128)(2,1)S(1)} %extra.1.refs_5_), channel_id=1, source_target_pairs={{3,0},{2,1},{1,2},{0,3},{7,4},{6,5},{5,6},{4,7},{11,8},{10,9},{9,1... | collective-permute-start | bytes 884744 | tf_op jit(solution)/shard_map/ppermute | solution.py:560
  11.2 14.9 %collective-permute-start.1 = (bf16[144,1024]{1,0:T(8,128)(2,1)S(1)}, bf16[144,1024]{1,0:T(8,128)(2,1)S(1)}, u32[]{:S(2)}, u32[]{:S(2)}) collective-permute-start(bf16[144,1024]{1,0:T(8,128)(2,1)S(1)} %extra.1.refs_5_), channel_id=1, source_target_pairs={{2,0},{3,1},{0,2},{1,3},{6,4},{7,5},{4,6},{5,7},{10,8},{11,9},{8,1... | collective-permute-start | bytes 884744 | tf_op jit(solution)/shard_map/ppermute | solution.py:560
  12.1 14.0 %collective-permute-start = (bf16[144,1024]{1,0:T(8,128)(2,1)S(1)}, bf16[144,1024]{1,0:T(8,128)(2,1)S(1)}, u32[]{:S(2)}, u32[]{:S(2)}) collective-permute-start(bf16[144,1024]{1,0:T(8,128)(2,1)S(1)} %extra.1.refs_5_), channel_id=1, source_target_pairs={{1,0},{0,1},{3,2},{2,3},{5,4},{4,5},{7,6},{6,7},{9,8},{8,9},{11,10... | collective-permute-start | bytes 884744 | tf_op jit(solution)/shard_map/ppermute | solution.py:560
  18.0 98.1 %collective-permute-start.8 = (bf16[2048,1024]{1,0:T(8,128)(2,1)}, bf16[2048,1024]{1,0:T(8,128)(2,1)}, u32[]{:S(2)}, u32[]{:S(2)}) collective-permute-start(bf16[2048,1024]{1,0:T(8,128)(2,1)} %unit.1.refs_0_), channel_id=1, source_target_pairs={{4,0},{5,1},{6,2},{7,3},{8,4},{9,5},{10,6},{11,7},{12,8},{13,9},{1... | collective-permute-start | bytes 12582920 | tf_op jit(solution)/shard_map/ppermute | solution.py:569
  26.1 92.8 %collective-permute-start.6 = (bf16[2048,1024]{1,0:T(8,128)(2,1)}, bf16[2048,1024]{1,0:T(8,128)(2,1)}, u32[]{:S(2)}, u32[]{:S(2)}) collective-permute-start(bf16[2048,1024]{1,0:T(8,128)(2,1)} %unit.1.refs_0_), channel_id=1, source_target_pairs={{0,2},{1,3},{2,0},{3,1},{4,6},{5,7},{6,4},{7,5},{8,10},{9,11},{10,... | collective-permute-start | bytes 12582920 | tf_op jit(solution)/shard_map/ppermute | solution.py:569
  27.1 94.4 %collective-permute-start.9 = (bf16[2048,1024]{1,0:T(8,128)(2,1)}, bf16[2048,1024]{1,0:T(8,128)(2,1)}, u32[]{:S(2)}, u32[]{:S(2)}) collective-permute-start(bf16[2048,1024]{1,0:T(8,128)(2,1)} %unit.1.refs_0_), channel_id=1, source_target_pairs={{0,4},{1,5},{2,6},{3,7},{4,8},{5,9},{6,10},{7,11},{16,20},{17,21},... | collective-permute-start | bytes 12582920 | tf_op jit(solution)/shard_map/ppermute | solution.py:569
  33.2 99.2 %collective-permute-start.5 = (bf16[2048,1024]{1,0:T(8,128)(2,1)}, bf16[2048,1024]{1,0:T(8,128)(2,1)}, u32[]{:S(2)}, u32[]{:S(2)}) collective-permute-start(bf16[2048,1024]{1,0:T(8,128)(2,1)} %unit.1.refs_0_), channel_id=1, source_target_pairs={{0,1},{1,0},{2,3},{3,2},{4,5},{5,4},{6,7},{7,6},{8,9},{9,8},{10,11... | collective-permute-start | bytes 12582920 | tf_op jit(solution)/shard_map/ppermute | solution.py:569
  119.0 13.4 %collective-permute-start.7 = (bf16[2048,1024]{1,0:T(8,128)(2,1)}, bf16[2048,1024]{1,0:T(8,128)(2,1)}, u32[]{:S(2)}, u32[]{:S(2)}) collective-permute-start(bf16[2048,1024]{1,0:T(8,128)(2,1)} %collective-permute-done.6.refs_2_), channel_id=1, source_target_pairs={{0,1},{1,0},{2,3},{3,2},{4,5},{5,4},{6,7},{7,6},{8,9},{9,8},{10,11... | collective-permute-start | bytes 12582920 | tf_op jit(solution)/shard_map/ppermute | solution.py:569
  121.5 21.8 %collective-permute-start.10 = (bf16[2048,1024]{1,0:T(8,128)(2,1)}, bf16[2048,1024]{1,0:T(8,128)(2,1)}, u32[]{:S(2)}, u32[]{:S(2)}) collective-permute-start(bf16[2048,1024]{1,0:T(8,128)(2,1)} %collective-permute-done.9), channel_id=1, source_target_pairs={{4,8},{5,9},{6,10},{7,11},{8,12},{9,13},{10,14},{11,15},{20,24},{2... | collective-permute-start | bytes 12582920 | tf_op jit(solution)/shard_map/ppermute | solution.py:569
  124.1 95.7 %collective-permute-start.11 = (bf16[2048,1024]{1,0:T(8,128)(2,1)}, bf16[2048,1024]{1,0:T(8,128)(2,1)}, u32[]{:S(2)}, u32[]{:S(2)}) collective-permute-start(bf16[2048,1024]{1,0:T(8,128)(2,1)} %unit.1.refs_0_), channel_id=1, source_target_pairs={{12,0},{13,1},{14,2},{15,3},{28,16},{29,17},{30,18},{31,19}} | collective-permute-start | bytes 12582920 | tf_op jit(solution)/shard_map/ppermute | solution.py:569
  132.4 2.2 copy-start
  134.6 85.2 %copy-start.1 = (bf16[2048,1024]{1,0:T(8,128)(2,1)S(1)}, bf16[2048,1024]{1,0:T(8,128)(2,1)}, u32[]{:S(2)}) copy-start(bf16[2048,1024]{1,0:T(8,128)(2,1)} %unit.1.refs_0_) | copy-start | bytes 12582916
  230.5 2.0 collective-permute-start.12
  230.6 11.5 %collective-permute-start.16 = (bf16[4,64,512]{2,1,0:T(8,128)(2,1)S(1)}, bf16[4,64,512]{2,1,0:T(8,128)(2,1)S(1)}, u32[]{:S(2)}, u32[]{:S(2)}) collective-permute-start(bf16[4,64,512]{2,1,0:T(8,128)(2,1)S(1)} %get-tuple-element.55), channel_id=1, source_target_pairs={{8,0},{9,1},{10,2},{11,3},{12,4},{13,5},{14,6},{15,7},{0,12},{1,13... | collective-permute-start | bytes 786440 | tf_op jit(solution)/shard_map/ppermute | solution.py:591
  232.5 9.6 %collective-permute-start.13 = (bf16[4,64,512]{2,1,0:T(8,128)(2,1)S(1)}, bf16[4,64,512]{2,1,0:T(8,128)(2,1)S(1)}, u32[]{:S(2)}, u32[]{:S(2)}) collective-permute-start(bf16[4,64,512]{2,1,0:T(8,128)(2,1)S(1)} %get-tuple-element.51), channel_id=1, source_target_pairs={{1,0},{0,1},{3,2},{2,3},{5,4},{4,5},{7,6},{6,7},{9,8},{8,9},{11,10... | collective-permute-start | bytes 786440 | tf_op jit(solution)/shard_map/ppermute | solution.py:591
  233.1 11.6 %collective-permute-start.15 = (bf16[4,64,512]{2,1,0:T(8,128)(2,1)S(1)}, bf16[4,64,512]{2,1,0:T(8,128)(2,1)S(1)}, u32[]{:S(2)}, u32[]{:S(2)}) collective-permute-start(bf16[4,64,512]{2,1,0:T(8,128)(2,1)S(1)} %get-tuple-element.54), channel_id=1, source_target_pairs={{0,4},{1,5},{2,6},{3,7},{4,8},{5,9},{6,10},{7,11},{8,12},{9,13},{1... | collective-permute-start | bytes 786440 | tf_op jit(solution)/shard_map/ppermute | solution.py:591
  234.4 10.2 %collective-permute-start.14 = (bf16[4,64,512]{2,1,0:T(8,128)(2,1)S(1)}, bf16[4,64,512]{2,1,0:T(8,128)(2,1)S(1)}, u32[]{:S(2)}, u32[]{:S(2)}) collective-permute-start(bf16[4,64,512]{2,1,0:T(8,128)(2,1)S(1)} %add.104), channel_id=1, source_target_pairs={{2,0},{3,1},{0,2},{1,3},{6,4},{7,5},{4,6},{5,7},{10,8},{11,9},{8,1... | collective-permute-start | bytes 786440 | tf_op jit(solution)/shard_map/ppermute | solution.py:591
  245.2 3.7 %collective-permute-start.19 = (f32[64,64]{1,0:T(8,128)S(1)}, f32[64,64]{1,0:T(8,128)S(1)}, u32[]{:S(2)}, u32[]{:S(2)}) collective-permute-start(f32[64,64]{1,0:T(8,128)S(1)} %get-tuple-element.56), channel_id=1, source_target_pairs={{0,3},{1,2},{2,1},{3,0},{4,7},{5,6},{6,5},{7,4},{8,11},{9,10},{10,... | collective-permute-start | bytes 49160 | tf_op jit(solution)/shard_map/ppermute | solution.py:530
  245.3 4.4 %collective-permute-start.18 = (f32[64,64]{1,0:T(8,128)S(1)}, f32[64,64]{1,0:T(8,128)S(1)}, u32[]{:S(2)}, u32[]{:S(2)}) collective-permute-start(f32[64,64]{1,0:T(8,128)S(1)} %get-tuple-element.56), channel_id=1, source_target_pairs={{0,2},{1,3},{2,0},{3,1},{4,6},{5,7},{6,4},{7,5},{8,10},{9,11},{10,... | collective-permute-start | bytes 49160 | tf_op jit(solution)/shard_map/ppermute | solution.py:530
  246.8 2.9 collective-permute-start.17
  249.7 6.2 %collective-permute-start.22 = (f32[64,64]{1,0:T(8,128)S(1)}, f32[64,64]{1,0:T(8,128)S(1)}, u32[]{:S(2)}, u32[]{:S(2)}) collective-permute-start(f32[64,64]{1,0:T(8,128)S(1)} %add_add_fusion.1.refs_0_), channel_id=1, source_target_pairs={{0,12},{1,13},{2,14},{3,15},{4,8},{5,9},{6,10},{7,11},{8,4},{9,5},... | collective-permute-start | bytes 49160 | tf_op jit(solution)/shard_map/ppermute | solution.py:530
  254.0 4.8 %collective-permute-start.21 = (f32[64,64]{1,0:T(8,128)S(1)}, f32[64,64]{1,0:T(8,128)S(1)}, u32[]{:S(2)}, u32[]{:S(2)}) collective-permute-start(f32[64,64]{1,0:T(8,128)S(1)} %add_add_fusion.1.refs_0_), channel_id=1, source_target_pairs={{0,8},{1,9},{2,10},{3,11},{4,12},{5,13},{6,14},{7,15},{8,0},{9,1},... | collective-permute-start | bytes 49160 | tf_op jit(solution)/shard_map/ppermute | solution.py:530
  254.0 4.8 %collective-permute-start.20 = (f32[64,64]{1,0:T(8,128)S(1)}, f32[64,64]{1,0:T(8,128)S(1)}, u32[]{:S(2)}, u32[]{:S(2)}) collective-permute-start(f32[64,64]{1,0:T(8,128)S(1)} %add_add_fusion.1.refs_0_), channel_id=1, source_target_pairs={{0,4},{1,5},{2,6},{3,7},{4,0},{5,1},{6,2},{7,3},{8,12},{9,13},{10,... | collective-permute-start | bytes 49160 | tf_op jit(solution)/shard_map/ppermute | solution.py:530
  262.5 6.7 %collective-permute-start.24 = (bf16[128,1024]{1,0:T(8,128)(2,1)S(1)}, bf16[128,1024]{1,0:T(8,128)(2,1)S(1)}, u32[]{:S(2)}, u32[]{:S(2)}) collective-permute-start(bf16[128,1024]{1,0:T(8,128)(2,1)S(1)} %panel.4.refs_0_), channel_id=1, source_target_pairs={{0,2},{1,3},{2,0},{3,1},{4,6},{5,7},{6,4},{7,5},{8,10},{9,11},{10,... | collective-permute-start | bytes 786440 | tf_op jit(solution)/shard_map/ppermute | solution.py:555
  263.8 12.4 %collective-permute-start.27 = (bf16[128,1024]{1,0:T(8,128)(2,1)S(1)}, bf16[128,1024]{1,0:T(8,128)(2,1)S(1)}, u32[]{:S(2)}, u32[]{:S(2)}) collective-permute-start(bf16[128,1024]{1,0:T(8,128)(2,1)S(1)} %panel.4.refs_0_), channel_id=1, source_target_pairs={{0,8},{1,9},{2,10},{3,11},{4,12},{5,13},{6,14},{7,15},{12,0},{13,1... | collective-permute-start | bytes 786440 | tf_op jit(solution)/shard_map/ppermute | solution.py:555
  267.7 11.2 %collective-permute-start.26 = (bf16[128,1024]{1,0:T(8,128)(2,1)S(1)}, bf16[128,1024]{1,0:T(8,128)(2,1)S(1)}, u32[]{:S(2)}, u32[]{:S(2)}) collective-permute-start(bf16[128,1024]{1,0:T(8,128)(2,1)S(1)} %panel.4.refs_0_), channel_id=1, source_target_pairs={{4,0},{5,1},{6,2},{7,3},{8,4},{9,5},{10,6},{11,7},{12,8},{13,9},{1... | collective-permute-start | bytes 786440 | tf_op jit(solution)/shard_map/ppermute | solution.py:555
  269.0 9.9 %collective-permute-start.23 = (bf16[128,1024]{1,0:T(8,128)(2,1)S(1)}, bf16[128,1024]{1,0:T(8,128)(2,1)S(1)}, u32[]{:S(2)}, u32[]{:S(2)}) collective-permute-start(bf16[128,1024]{1,0:T(8,128)(2,1)S(1)} %panel.4.refs_0_), channel_id=1, source_target_pairs={{0,1},{1,0},{2,3},{3,2},{4,5},{5,4},{6,7},{7,6},{8,9},{9,8},{10,11... | collective-permute-start | bytes 786440 | tf_op jit(solution)/shard_map/ppermute | solution.py:555
  269.2 9.7 %collective-permute-start.25 = (bf16[128,1024]{1,0:T(8,128)(2,1)S(1)}, bf16[128,1024]{1,0:T(8,128)(2,1)S(1)}, u32[]{:S(2)}, u32[]{:S(2)}) collective-permute-start(bf16[128,1024]{1,0:T(8,128)(2,1)S(1)} %collective-permute-done.24.refs_2_), channel_id=1, source_target_pairs={{0,1},{1,0},{2,3},{3,2},{4,5},{5,4},{6,7},{7,6},{8,9},{9,8},{10,11... | collective-permute-start | bytes 786440 | tf_op jit(solution)/shard_map/ppermute | solution.py:555
  285.0 2.0 collective-permute-start.28
  285.1 15.9 %collective-permute-start.32 = (bf16[4,64,512]{2,1,0:T(8,128)(2,1)S(1)}, bf16[4,64,512]{2,1,0:T(8,128)(2,1)S(1)}, u32[]{:S(2)}, u32[]{:S(2)}) collective-permute-start(bf16[4,64,512]{2,1,0:T(8,128)(2,1)S(1)} %get-tuple-element.66), channel_id=1, source_target_pairs={{8,0},{9,1},{10,2},{11,3},{12,4},{13,5},{14,6},{15,7},{0,12},{1,13... | collective-permute-start | bytes 786440 | tf_op jit(solution)/shard_map/ppermute | solution.py:591
  287.0 14.0 %collective-permute-start.29 = (bf16[4,64,512]{2,1,0:T(8,128)(2,1)S(1)}, bf16[4,64,512]{2,1,0:T(8,128)(2,1)S(1)}, u32[]{:S(2)}, u32[]{:S(2)}) collective-permute-start(bf16[4,64,512]{2,1,0:T(8,128)(2,1)S(1)} %get-tuple-element.62), channel_id=1, source_target_pairs={{1,0},{0,1},{3,2},{2,3},{5,4},{4,5},{7,6},{6,7},{9,8},{8,9},{11,10... | collective-permute-start | bytes 786440 | tf_op jit(solution)/shard_map/ppermute | solution.py:591
  287.6 13.5 %collective-permute-start.31 = (bf16[4,64,512]{2,1,0:T(8,128)(2,1)S(1)}, bf16[4,64,512]{2,1,0:T(8,128)(2,1)S(1)}, u32[]{:S(2)}, u32[]{:S(2)}) collective-permute-start(bf16[4,64,512]{2,1,0:T(8,128)(2,1)S(1)} %get-tuple-element.65), channel_id=1, source_target_pairs={{0,4},{1,5},{2,6},{3,7},{4,8},{5,9},{6,10},{7,11},{8,12},{9,13},{1... | collective-permute-start | bytes 786440 | tf_op jit(solution)/shard_map/ppermute | solution.py:591
  289.1 11.9 %collective-permute-start.30 = (bf16[4,64,512]{2,1,0:T(8,128)(2,1)S(1)}, bf16[4,64,512]{2,1,0:T(8,128)(2,1)S(1)}, u32[]{:S(2)}, u32[]{:S(2)}) collective-permute-start(bf16[4,64,512]{2,1,0:T(8,128)(2,1)S(1)} %add.108), channel_id=1, source_target_pairs={{2,0},{3,1},{0,2},{1,3},{6,4},{7,5},{4,6},{5,7},{10,8},{11,9},{8,1... | collective-permute-start | bytes 786440 | tf_op jit(solution)/shard_map/ppermute | solution.py:591
  301.7 3.5 %collective-permute-start.35 = (f32[64,64]{1,0:T(8,128)S(1)}, f32[64,64]{1,0:T(8,128)S(1)}, u32[]{:S(2)}, u32[]{:S(2)}) collective-permute-start(f32[64,64]{1,0:T(8,128)S(1)} %get-tuple-element.67), channel_id=1, source_target_pairs={{0,3},{1,2},{2,1},{3,0},{4,7},{5,6},{6,5},{7,4},{8,11},{9,10},{10,... | collective-permute-start | bytes 49160 | tf_op jit(solution)/shard_map/ppermute | solution.py:530
  302.3 3.9 %collective-permute-start.34 = (f32[64,64]{1,0:T(8,128)S(1)}, f32[64,64]{1,0:T(8,128)S(1)}, u32[]{:S(2)}, u32[]{:S(2)}) collective-permute-start(f32[64,64]{1,0:T(8,128)S(1)} %get-tuple-element.67), channel_id=1, source_target_pairs={{0,2},{1,3},{2,0},{3,1},{4,6},{5,7},{6,4},{7,5},{8,10},{9,11},{10,... | collective-permute-start | bytes 49160 | tf_op jit(solution)/shard_map/ppermute | solution.py:530
  303.4 2.8 collective-permute-start.33
  306.3 5.8 %collective-permute-start.38 = (f32[64,64]{1,0:T(8,128)S(1)}, f32[64,64]{1,0:T(8,128)S(1)}, u32[]{:S(2)}, u32[]{:S(2)}) collective-permute-start(f32[64,64]{1,0:T(8,128)S(1)} %add_add_fusion.refs_0_), channel_id=1, source_target_pairs={{0,12},{1,13},{2,14},{3,15},{4,8},{5,9},{6,10},{7,11},{8,4},{9,5},... | collective-permute-start | bytes 49160 | tf_op jit(solution)/shard_map/ppermute | solution.py:530
  308.7 4.8 %collective-permute-start.37 = (f32[64,64]{1,0:T(8,128)S(1)}, f32[64,64]{1,0:T(8,128)S(1)}, u32[]{:S(2)}, u32[]{:S(2)}) collective-permute-start(f32[64,64]{1,0:T(8,128)S(1)} %add_add_fusion.refs_0_), channel_id=1, source_target_pairs={{0,8},{1,9},{2,10},{3,11},{4,12},{5,13},{6,14},{7,15},{8,0},{9,1},... | collective-permute-start | bytes 49160 | tf_op jit(solution)/shard_map/ppermute | solution.py:530
  308.7 4.8 %collective-permute-start.36 = (f32[64,64]{1,0:T(8,128)S(1)}, f32[64,64]{1,0:T(8,128)S(1)}, u32[]{:S(2)}, u32[]{:S(2)}) collective-permute-start(f32[64,64]{1,0:T(8,128)S(1)} %add_add_fusion.refs_0_), channel_id=1, source_target_pairs={{0,4},{1,5},{2,6},{3,7},{4,0},{5,1},{6,2},{7,3},{8,12},{9,13},{10,... | collective-permute-start | bytes 49160 | tf_op jit(solution)/shard_map/ppermute | solution.py:530

commit v5 on v4

--- a/solution.py
+++ b/solution.py
@@ -14,6 +14,7 @@
 SHARPNESS = 24.0
 LOG2E = 1.4426950408889634
 LIST_ROWS = 16
+RING = 4
 LANES = 128
 VMEM_LIMIT = 32 * 1024 * 1024
 VMEM_MOST = 55 * 1024 * 1024
@@ -26,7 +27,10 @@
         moves.append([(i, i + 8) for i in range(8)])
         moves.append([(i, i - 12) for i in range(12, 16)])
         late = {5, 6}
+        light = {5, 6}
         after = {6: 4}
+        settle = {1, 2}
+        bare = True
         via = {3: 2}
         after_back = {1: 3, 4: 3}
         hops = {5: [[(i, i + 4) for i in range(8)], [(i, i + 4) for i in range(4, 12)]]}
@@ -34,7 +38,10 @@
     else:
         moves = [[(i, (i - o) % count) for i in range(count)] for o in range(1, REACH + 1)]
         late = {5, 6, 7}
+        light = late
         after = {6: 1, 7: 2}
+        settle = set(range(1, REACH + 1))
+        bare = False
         via = {}
         after_back = {}
         hops = {}
@@ -60,7 +67,7 @@
         for s, device in enumerate(hold[w]):
             if device >= 0:
                 place[w, device] = s
-    return moves, via, after_back, hops, joint, hold, place, work, late, after, int(load.max())
+    return moves, via, after_back, hops, joint, hold, place, work, late, light, settle, bare, after, int(load.max())
 
 
 def work_list(lists, hold, place, work, late, slots, blocks_here, top, me):
@@ -81,21 +88,22 @@
     is_late = functools.reduce(
         jnp.logical_or, [jnp.logical_or(row_place == s, col_place == s) for s in sorted(late)]
     )
-    row_held = (row_place * blocks_here + pairs[:, :, 0] % blocks_here).reshape(-1)
-    col_held = (col_place * blocks_here + pairs[:, :, 1] % blocks_here).reshape(-1)
-    first = jnp.logical_and(valid, jnp.logical_not(is_late)).reshape(-1).astype(jnp.int32)
-    second = jnp.logical_and(valid, is_late).reshape(-1).astype(jnp.int32)
-    total = first.shape[0]
-    before = jnp.arange(total)[:, None] < jnp.arange(total)[None, :]
-    first_rank = jnp.sum(jnp.where(before, first[:, None], 0), axis=0)
-    second_rank = jnp.sum(jnp.where(before, second[:, None], 0), axis=0)
-    n_first, n_second = jnp.sum(first), jnp.sum(second)
-    rank = jnp.where(first > 0, first_rank, jnp.where(second > 0, n_first + second_rank, total))
+    stage = jnp.where(valid, is_late.astype(jnp.int32), 2).reshape(-1)
+    row_block, col_block = pairs[:, :, 0] % blocks_here, pairs[:, :, 1] % blocks_here
+    row_held = (row_place * blocks_here + row_block).reshape(-1)
+    col_held = (col_place * blocks_here + col_block).reshape(-1)
+    total = stage.shape[0]
+    index = jnp.arange(total, dtype=jnp.int32)
+    ahead = jnp.logical_or(
+        stage[:, None] < stage[None, :],
+        jnp.logical_and(stage[:, None] == stage[None, :], index[:, None] < index[None, :]),
+    )
+    rank = jnp.where(stage < 2, jnp.sum(ahead.astype(jnp.int32), axis=0), total)
     chosen = rank[None, :] == jnp.arange(top, dtype=jnp.int32)[:, None]
     rows = jnp.sum(jnp.where(chosen, row_held[None, :], 0), axis=1)
     cols = jnp.sum(jnp.where(chosen, col_held[None, :], 0), axis=1)
-    zero = jnp.zeros((), jnp.int32)
-    return jnp.stack([rows, cols]), jnp.stack([zero, n_first]), jnp.stack([n_first, n_first + n_second])
+    bounds = jnp.sum((stage[None, :] < jnp.arange(3, dtype=jnp.int32)[:, None]).astype(jnp.int32), axis=1)
+    return jnp.stack([rows, cols]), bounds
 
 
 def extra_kernel(pairs, live, panel, out):
@@ -109,10 +117,10 @@
                 q * high : (q + 1) * high, b * BLOCK : (b + 1) * BLOCK
             ].astype(jnp.bfloat16)
     lane = lax.broadcasted_iota(jnp.int32, (LIST_ROWS, LANES), 1)
-    values = jnp.where(lane == 2 * pairs.shape[0], live[0], 0)
-    for slot in range(pairs.shape[0]):
+    values = jnp.where(lane == 2 * pairs.shape[1], live[0], 0)
+    for slot in range(pairs.shape[1]):
         for side in range(2):
-            values = jnp.where(lane == 2 * slot + side, pairs[slot, side], values)
+            values = jnp.where(lane == 2 * slot + side, pairs[side, slot], values)
     out[blocks * high :, :LANES] = values.astype(jnp.float32).astype(jnp.bfloat16)
     out[blocks * high :, LANES:] = jnp.zeros((LIST_ROWS, depth - LANES), jnp.bfloat16)
 
@@ -131,16 +139,20 @@
     )(pairs, live, panel)
 
 
-def unit_kernel(rows, out, raw, buf, scale, in_sem, out_sem):
+def pack_kernel(bare, rows, extra, *refs):
+    alone, refs = refs[:bare], refs[bare:]
+    out, raw, buf, scale, in_sem, alone_sem, out_sem = refs
     count, depth = rows.shape
     blocks = count // BLOCK
     step = 16
-    parts = [pl.ds(b * BLOCK, BLOCK) for b in range(blocks)]
-    loads = [pltpu.make_async_copy(rows.at[at], raw.at[at], in_sem.at[b]) for b, at in enumerate(parts)]
-    stores = [pltpu.make_async_copy(buf.at[at], out.at[at], out_sem.at[b]) for b, at in enumerate(parts)]
+    spots = [pl.ds(b * BLOCK, BLOCK) for b in range(blocks)]
+    loads = [pltpu.make_async_copy(rows.at[at], raw.at[at], in_sem.at[b]) for b, at in enumerate(spots)]
     for load in loads:
         load.start()
-    for b in range(blocks):
+    tail = pltpu.make_async_copy(extra, out.at[pl.ds(count, extra.shape[0])], out_sem.at[blocks])
+    tail.start()
+    stores = [tail]
+    for b, at in enumerate(spots):
         loads[b].wait()
 
         @pl.loop(0, BLOCK // step, unroll=8)
@@ -152,34 +164,42 @@
 
         @pl.loop(0, BLOCK // step, unroll=8)
         def _(i):
-            at = pl.ds(pl.multiple_of(b * BLOCK + i * step, step), step)
+            here = pl.ds(pl.multiple_of(b * BLOCK + i * step, step), step)
             factor = scale[pl.ds(pl.multiple_of(i * step, step), step), :]
             for lane in range(0, depth, LANES):
-                values = raw[at, lane : lane + LANES].astype(jnp.float32)
-                buf[at, lane : lane + LANES] = (values * factor).astype(jnp.bfloat16)
-
-        stores[b].start()
+                values = raw[here, lane : lane + LANES].astype(jnp.float32)
+                buf[here, lane : lane + LANES] = (values * factor).astype(jnp.bfloat16)
+
+        for ref in alone:
+            stores.append(pltpu.make_async_copy(buf.at[at], ref.at[at], alone_sem.at[b]))
+            stores[-1].start()
+        stores.append(pltpu.make_async_copy(buf.at[at], out.at[at], out_sem.at[b]))
+        stores[-1].start()
     for store in stores:
         store.wait()
 
 
-def unit_call(embeddings):
-    blocks = embeddings.shape[0] // BLOCK
+def pack_call(embeddings, extra, bare):
+    rows, depth = embeddings.shape
+    blocks = rows // BLOCK
+    hbm = pl.BlockSpec(memory_space=pltpu.HBM)
     return pl.pallas_call(
-        unit_kernel,
-        out_shape=jax.ShapeDtypeStruct(embeddings.shape, jnp.bfloat16),
-        in_specs=[pl.BlockSpec(memory_space=pltpu.HBM)],
-        out_specs=pl.BlockSpec(memory_space=pltpu.HBM),
+        functools.partial(pack_kernel, int(bare)),
+        out_shape=[jax.ShapeDtypeStruct((rows, depth), jnp.bfloat16)] * bare
+        + [jax.ShapeDtypeStruct((rows + extra.shape[0], depth), jnp.bfloat16)],
+        in_specs=[hbm, pl.BlockSpec(memory_space=pltpu.VMEM)],
+        out_specs=[hbm] * (bare + 1),
         scratch_shapes=[
-            pltpu.VMEM(embeddings.shape, jnp.bfloat16),
-            pltpu.VMEM(embeddings.shape, jnp.bfloat16),
+            pltpu.VMEM((rows, depth), jnp.bfloat16),
+            pltpu.VMEM((rows, depth), jnp.bfloat16),
             pltpu.VMEM((BLOCK, LANES), jnp.float32),
             pltpu.SemaphoreType.DMA((blocks,)),
             pltpu.SemaphoreType.DMA((blocks,)),
+            pltpu.SemaphoreType.DMA((blocks + 1,)),
         ],
         compiler_params=pltpu.CompilerParams(vmem_limit_bytes=VMEM_MOST),
-        name="unit",
-    )(embeddings)
+        name="pack",
+    )(embeddings, extra)
 
 
 def fill_panel(refs, joint, pan, sem):
@@ -187,8 +207,9 @@
     size = pan.shape[1] // (1 + sum(len(group) for group in joint))
     copies = []
     for ref, s in [(refs[0], 0)] + [(ref, s) for ref, group in zip(refs[1:], joint) for s in group]:
+        at = max(0, ref.shape[0] - size - LIST_ROWS)
         for q in range(per_row):
-            source = ref.at[pl.ds(0, size), pl.ds(q * BLOCK, BLOCK)]
+            source = ref.at[pl.ds(at, size), pl.ds(q * BLOCK, BLOCK)]
             copies.append(
                 pltpu.make_async_copy(source, pan.at[q, pl.ds(s * size, size)], sem.at[len(copies)])
             )
@@ -221,21 +242,22 @@
         back[...] = sum(acc[pl.ds(s * per, per)] for s in columns).astype(jnp.bfloat16)
 
 
-def pair_kernel(columns, joint, per, first, final, items, span, *refs):
-    n_unit = len(columns)
+def pair_kernel(stage, held_at, n_slab, joint, per, final, items, bounds, *refs):
+    n_unit = len(held_at)
     units, refs = refs[:n_unit], refs[n_unit:]
-    if first:
-        panels, refs = refs[: len(joint) + 1], refs[len(joint) + 1 :]
+    if stage == 0:
+        n_ahead = len(joint) + 1 - n_slab
+        panels, refs = [*units[:n_slab], *refs[:n_ahead]], refs[n_ahead:]
+        acc, pan, aff_out, refs = refs[0], refs[1], refs[2], refs[3:]
     else:
-        acc_in, pan_in, _, refs = refs[0], refs[1], refs[2], refs[3:]
-    if final:
-        own, refs = refs[0], refs[1:]
-        backs, refs = refs[: len(joint)], refs[len(joint) :]
-        aff_out, acc, pan, refs = refs[0], refs[1], refs[2], refs[3:]
-    else:
-        acc, pan, aff_out, refs = refs[0], refs[1], refs[2], refs[3:]
+        acc_in, _, pan, refs = refs[0], refs[1], refs[2], refs[3:]
+        if final:
+            own, backs, refs = refs[0], refs[1 : len(joint) + 1], refs[len(joint) + 1 :]
+            aff_out, acc, refs = refs[0], refs[1], refs[2:]
+        else:
+            acc, aff_out, refs = refs[0], refs[1], refs[2:]
     ubuf, affbuf, usem, psem, asem = refs
-    begin, end = span[0], span[1]
+    begin, end = bounds[stage], bounds[stage + 1]
 
     def rows_of(ref, block):
         return ref.at[pl.ds(pl.multiple_of(block * BLOCK, BLOCK), BLOCK)]
@@ -243,48 +265,59 @@
     def fetch(i, slot):
         for side in range(2):
             held = items[side, i]
-            for s, ref in zip(columns, units):
-
-                @pl.when(held // per == s)
+            for (start, size), ref in zip(held_at, units):
+
+                @pl.when(jnp.logical_and(held >= start, held < start + size))
                 def _():
-                    pltpu.make_async_copy(rows_of(ref, held % per), ubuf.at[slot, side], usem.at[slot, side]).start()
+                    copy = pltpu.make_async_copy(
+                        rows_of(ref, held - start), ubuf.at[slot, side], usem.at[slot, side]
+                    )
+                    copy.start()
 
     def store(i, slot):
         return pltpu.make_async_copy(affbuf.at[slot], aff_out.at[i], asem.at[slot])
 
-    @pl.when(begin < end)
-    def _():
-        fetch(begin, begin % 2)
-
-    if first:
+    for ahead in range(RING - 1):
+
+        @pl.when(begin + ahead < end)
+        def _():
+            fetch(begin + ahead, (begin + ahead) % RING)
+
+    if stage == 0:
         copies = fill_panel(panels, joint, pan, psem)
         acc[...] = jnp.zeros_like(acc)
         for copy in copies:
             copy.wait()
     else:
         acc[...] = acc_in[...]
-        pan[...] = pan_in[...]
 
     @pl.loop(begin, end)
     def _(i):
-        slot = i % 2
-
-        @pl.when(i + 1 < end)
+        slot, place = i % 2, i % RING
+
+        @pl.when(i + RING - 1 < end)
         def _():
-            fetch(i + 1, 1 - slot)
+            fetch(i + RING - 1, (i + RING - 1) % RING)
 
         for side in range(2):
-            pltpu.make_async_copy(rows_of(units[0], 0), ubuf.at[slot, side], usem.at[slot, side]).wait()
+            pltpu.make_async_copy(rows_of(units[0], 0), ubuf.at[place, side], usem.at[place, side]).wait()
 
         @pl.when(i >= begin + 2)
         def _():
             store(i - 2, slot).wait()
 
-        scores = lax.dot_general(
-            ubuf[slot, 0], ubuf[slot, 1], (((1,), (1,)), ((), ())), preferred_element_type=jnp.float32
-        )
-        power = scores * (SHARPNESS * LOG2E)
-        aff = (jnp.exp2(power - 1.0) - jnp.exp2(-1.0 - power)).astype(jnp.bfloat16)
+        half = BLOCK // 2
+        halves = []
+        for part in range(2):
+            scores = lax.dot_general(
+                ubuf[place, 0],
+                ubuf[place, 1, pl.ds(part * half, half), :],
+                (((1,), (1,)), ((), ())),
+                preferred_element_type=jnp.float32,
+            )
+            power = scores * (SHARPNESS * LOG2E)
+            halves.append((jnp.exp2(power - 1.0) - jnp.exp2(-1.0 - power)).astype(jnp.bfloat16))
+        aff = jnp.concatenate(halves, axis=1)
         affbuf[slot] = aff
         store(i, slot).start()
         add_products(pan, acc, aff, items[0, i], items[1, i])
@@ -305,63 +338,61 @@
     ] * sends
 
 
-def pair_call(items, span, units, columns, panels, joint, per, width, top, state, final):
+def pair_call(items, bounds, stage, units, held_at, panels, state, n_slab, joint, per, width, top, final):
     held = 1 + sum(len(group) for group in joint)
     blocks = held * per
     depth = units[0].shape[1]
     per_row = depth // BLOCK
     smem = pl.BlockSpec(memory_space=pltpu.SMEM)
-    anywhere = pl.BlockSpec(memory_space=pltpu.HBM)
+    hbm = pl.BlockSpec(memory_space=pltpu.HBM)
     vmem = pl.BlockSpec(memory_space=pltpu.VMEM)
-    operands = [items, span, *units]
-    in_specs = [smem, smem] + [anywhere] * len(units)
-    acc_shape = (blocks, width, BLOCK)
-    pan_shape = (per_row, blocks * width // per_row, BLOCK)
+    acc_shape = jax.ShapeDtypeStruct((blocks, width, BLOCK), jnp.float32)
+    pan_shape = jax.ShapeDtypeStruct((per_row, blocks * width // per_row, BLOCK), jnp.bfloat16)
     aff_shape = jax.ShapeDtypeStruct((top, BLOCK, BLOCK), jnp.bfloat16)
-    scratch = [
-        pltpu.VMEM((2, 2, BLOCK, depth), jnp.bfloat16),
-        pltpu.VMEM((2, BLOCK, BLOCK), jnp.bfloat16),
-        pltpu.SemaphoreType.DMA((2, 2)),
-        pltpu.SemaphoreType.DMA((held * per_row,)),
-        pltpu.SemaphoreType.DMA((2,)),
-    ]
-    if final:
-        out_shape = sum_shapes(len(joint), per, width) + [aff_shape]
-        out_specs = [vmem] * (1 + len(joint)) + [anywhere]
-        scratch = [pltpu.VMEM(acc_shape, jnp.float32), pltpu.VMEM(pan_shape, jnp.bfloat16)] + scratch
-    else:
-        out_shape = [
-            jax.ShapeDtypeStruct(acc_shape, jnp.float32),
-            jax.ShapeDtypeStruct(pan_shape, jnp.bfloat16),
-            aff_shape,
-        ]
-        out_specs = [vmem, vmem, anywhere]
-    aliases = {}
-    if state is None:
+    operands = [items, bounds, *units]
+    in_specs = [smem, smem] + [hbm] * len(units)
+    scratch, aliases = [], {}
+    if stage == 0:
         operands += panels
         in_specs += [pl.BlockSpec(memory_space=pl.ANY)] * len(panels)
+        out_shape, out_specs = [acc_shape, pan_shape, aff_shape], [vmem, vmem, hbm]
     else:
-        aliases = {len(operands) + 2: len(out_shape) - 1}
-        operands += list(state)
-        in_specs += [vmem, vmem, anywhere]
+        acc, aff, pan = state
+        aff_at = len(operands) + 1
+        operands += [acc, aff, pan]
+        in_specs += [vmem, hbm, vmem]
+        if final:
+            out_shape = sum_shapes(len(joint), per, width) + [aff_shape]
+            out_specs = [vmem] * (1 + len(joint)) + [hbm]
+            scratch = [pltpu.VMEM(acc_shape.shape, jnp.float32)]
+        else:
+            out_shape, out_specs = [acc_shape, aff_shape], [vmem, hbm]
+        aliases = {aff_at: len(out_shape) - 1}
     return pl.pallas_call(
-        functools.partial(pair_kernel, columns, joint, per, state is None, final),
+        functools.partial(pair_kernel, stage, held_at, n_slab, joint, per, final),
         out_shape=out_shape,
         in_specs=in_specs,
         out_specs=out_specs,
-        scratch_shapes=scratch,
+        scratch_shapes=scratch
+        + [
+            pltpu.VMEM((RING, 2, BLOCK, depth), jnp.bfloat16),
+            pltpu.VMEM((2, BLOCK, BLOCK), jnp.bfloat16),
+            pltpu.SemaphoreType.DMA((RING, 2)),
+            pltpu.SemaphoreType.DMA((held * per_row,)),
+            pltpu.SemaphoreType.DMA((2,)),
+        ],
         input_output_aliases=aliases,
         compiler_params=pltpu.CompilerParams(vmem_limit_bytes=VMEM_LIMIT),
         name="pairs",
     )(*operands)
 
 
-def apply_kernel(joint, items, span, *refs):
+def apply_kernel(joint, items, bounds, *refs):
     n_panel = len(joint) + 1
     panels, refs = refs[:n_panel], refs[n_panel:]
     aff_in, own, backs, refs = refs[0], refs[1], refs[2 : n_panel + 1], refs[n_panel + 1 :]
     acc, pan, affbuf, psem, asem = refs
-    end = span[1]
+    end = bounds[bounds.shape[0] - 1]
 
     def load(i, slot):
         return pltpu.make_async_copy(aff_in.at[i], affbuf.at[slot], asem.at[slot])
@@ -391,7 +422,7 @@
     write_sums(acc, joint, own, backs)
 
 
-def apply_call(items, span, panels, joint, aff, per, width):
+def apply_call(items, bounds, panels, joint, aff, per, width):
     held = 1 + sum(len(group) for group in joint)
     blocks = held * per
     per_row = panels[0].shape[1] // BLOCK
@@ -411,7 +442,7 @@
         ],
         compiler_params=pltpu.CompilerParams(vmem_limit_bytes=50 * 1024 * 1024),
         name="apply",
-    )(items, span, *panels, aff)
+    )(items, bounds, *panels, aff)
 
 
 def gram_kernel(n_back, own, *refs):
@@ -540,7 +571,7 @@
     per = embeddings.shape[0] // BLOCK
     width = start_panel.shape[0]
     slots = block_pairs.shape[0]
-    moves, via, after_back, hops, joint, hold, place, work, late, after, top = make_plan(count)
+    moves, via, after_back, hops, joint, hold, place, work, late, light, settle, bare, after, top = make_plan(count)
     held = len(moves) + 1
 
     merged = [functools.reduce(list.__add__, [moves[s - 1] for s in group]) for group in joint]
@@ -556,33 +587,43 @@
         return got
 
     assert count * per <= 256
-    extra = extra_call(block_pairs, pair_count, start_panel, depth)
-    extras = [extra] + [lax.ppermute(extra, "rows", pairs) for pairs in direct]
-    unit = unit_call(embeddings)
-    settled, extras = lax.optimization_barrier((unit, extras))
-    units = {0: unit}
+    extra = extra_call(block_pairs.T, pair_count, start_panel, depth)
+    ahead = {g: lax.ppermute(extra, "rows", direct[g]) for g, group in enumerate(joint) if group[0] in light}
+    *alone, packed = pack_call(embeddings, extra, bare)
+    units = {0: packed}
     for m in range(1, len(moves) + 1):
-        outgoing = units[via[m]] if m in via else unit if m in hops or m in after.values() else settled
+        outgoing = alone[0] if m in light and bare else packed
+        if m in settle:
+            outgoing, ahead = lax.optimization_barrier((outgoing, ahead))
+        if m in via:
+            outgoing = units[via[m]]
         if m in after:
             outgoing, _ = lax.optimization_barrier((outgoing, units[after[m]]))
         for pairs in hops.get(m, [moves[m - 1]]):
             outgoing = lax.ppermute(outgoing, "rows", pairs)
         units[m] = outgoing
-    lists = [part[part.shape[0] - LIST_ROWS, : 2 * slots + 1].astype(jnp.int32) for part in extras]
-    lists = jnp.stack(lists[:1] + [part for part, group in zip(lists[1:], joint) for _ in group])
-    items, span_first, span_second = work_list(lists, hold, place, work, late, slots, per, top, me)
-    span_all = jnp.stack([span_first[0], span_second[1]])
-
-    early = [s for s in range(held) if s not in late]
+    early = [m for m in range(held) if m not in late]
+    tails = {m: units[m] for m in early if m not in light}
+    n_slab = len(tails)
+    tails.update({m: ahead[g] for g in ahead for m in joint[g]})
+    lists = jnp.stack(
+        [tails[m][tails[m].shape[0] - LIST_ROWS, : 2 * slots + 1].astype(jnp.int32) for m in range(held)]
+    )
+    items, bounds = work_list(lists, hold, place, work, late, slots, per, top, me)
+
     order = early + sorted(late)
-    state = pair_call(items, span_first, [units[s] for s in early], early, extras, joint, per, width, top, None, False)
-    *sums, aff = pair_call(
-        items, span_second, [units[s] for s in order], order, None, joint, per, width, top, state, True
-    )
+    held_at = [(m * per, per) for m in order]
+    rows_of = [units[m] for m in order]
+    shape = (n_slab, joint, per, width, top)
+    n_early = len(early)
+    acc, pan, aff = pair_call(
+        items, bounds, 0, rows_of[:n_early], held_at[:n_early], list(ahead.values()), None, *shape, False
+    )
+    *sums, aff = pair_call(items, bounds, 1, rows_of, held_at, None, (acc, aff, pan), *shape, True)
 
     for sweep in range(ITERS):
         if sweep > 0:
-            sums = apply_call(items, span_all, spread(panel), joint, aff, per, width)
+            sums = apply_call(items, bounds, spread(panel), joint, aff, per, width)
         sums, backs, gone = list(sums), [], {}
         for m in sorted(range(1, len(joint) + 1), key=lambda m: m not in via):
             outgoing = sums[m]

time: 321 us -> 319 us (level)
  Pallas kernels: 41.1 us -> 36.2 us
  starting transfers between devices: 50.5 us -> 53.8 us
  local copies, waits for them, and re-layouts: 5.87 us -> 9.13 us
    ppermute x5 -> x1, waiting for transfers between devices: 6.87 us -> 0.92 us  [on_device(): lax.ppermute(extra, 'rows', direct[g])]
    ppermute x7, waiting for transfers between devices: 165 us -> 170 us  [on_device(): outgoing = lax.ppermute(outgoing, 'rows', pairs)]
    ppermute x7, starting transfers between devices: 12.2 us -> 17.2 us  [on_device(): outgoing = lax.ppermute(outgoing, 'rows', pairs)]
    slice x6, local copies, waits for them, and re-layouts: 0.01 us -> 3.37 us  [on_device(): tails[m][tails[m].shape[0] - LIST_ROWS, :2 * slots + 1].astype(jnp.int32)]
    pallas_call x3, Pallas kernels: 25 us -> 21.7 us  [the longest x2 14.6 us: pair_call(): pl.pallas_call(functools.partial(pair_kernel, stage, held_at, n_slab, joi...]
    ppermute x5 -> x1, starting transfers between devices: 9.16 us -> 5.94 us  [on_device(): lax.ppermute(extra, 'rows', direct[g])]
  transfers between devices with their start and end apart: 39 -> 35, of which waited for: 20 -> 18; matrix products, arithmetic and copies ran while one was open for 2% -> 2% of each run, Pallas kernels for 4% -> 4%
where the time goes in v5:
time: 319 us; the launch traced here: 315 us
  waiting for transfers between devices  214 us (67%)
  starting transfers between devices  53.8 us (17%)
  Pallas kernels  36.2 us (11%)
  local copies, waits for them, and re-layouts  9.13 us (3%)
    ppermute x7, waiting for transfers between devices, on_device(): outgoing = lax.ppermute(outgoing, 'rows', pairs)  170 us
    ppermute x10, waiting for transfers between devices, on_device(): lax.ppermute(outgoing, 'rows', [(target, source) for source, target in me...  21.4 us
    ppermute x7, starting transfers between devices, on_device(): outgoing = lax.ppermute(outgoing, 'rows', pairs)  17.2 us
    pallas_call x2, Pallas kernels, pair_call(): pl.pallas_call(functools.partial(pair_kernel, stage, held_at, n_slab, joi...  14.6 us
    ppermute x12, starting transfers between devices, sum_over_rows(): lax.ppermute(value, 'rows', [(i, i ^ step * m) for i in range(count)])  12.8 us
    ppermute x12, waiting for transfers between devices, sum_over_rows(): lax.ppermute(value, 'rows', [(i, i ^ step * m) for i in range(count)])  12.3 us
    ppermute x10, starting transfers between devices, on_device(): lax.ppermute(outgoing, 'rows', [(target, source) for source, target in me...  10.9 us
    ppermute x5, waiting for transfers between devices, spread(): got.append(lax.ppermute(got[via.get(group[0], 0)], 'rows', pairs))  9.43 us
  transfers between devices with their start and end apart: 35, of which 18 were waited for; matrix products, arithmetic and copies ran while one was open for 2% of the time, Pallas kernels for 4%

profile of v5, /device:TPU:0, one launch (start us, length us, event | category | flops | bytes accessed | tf_op | source)
XLA Modules:
  0.0 314.9 jit_solution(6953828570877376499)
XLA Ops:
  0.7 1.0 copy-done.2
  1.7 0.7 copy-done.3
  2.4 0.6 extra.1
  3.0 5.9 %collective-permute-start = (bf16[144,1024]{1,0:T(8,128)(2,1)S(1)}, bf16[144,1024]{1,0:T(8,128)(2,1)S(1)}, u32[]{:S(2)}, u32[]{:S(2)}) collective-permute-start(bf16[144,1024]{1,0:T(8,128)(2,1)S(1)} %extra.1), channel_id=1, source_target_pairs={{0,8},{1,9},{2,10},{3,11},{4,12},{5,13},{6,14},{7,15},{12,0},{13,1... | collective-permute-start | bytes 884744 | tf_op jit(solution)/shard_map/ppermute | solution.py:591
  8.9 7.1 %pack.1 = (bf16[2048,1024]{1,0:T(8,128)(2,1)}, bf16[2192,1024]{1,0:T(8,128)(2,1)}) custom-call(bf16[2048,1024]{1,0:T(8,128)(2,1)} %rows.1, bf16[144,1024]{1,0:T(8,128)(2,1)} %copy-done.1), custom_call_target="tpu_custom_call" | custom-call | tf_op jit(solution)/shard_map/pack/pallas_call | solution.py:186
  16.0 0.9 collective-permute-done.refs_5_
  16.9 1.5 collective-permute-start.2
  18.5 1.3 collective-permute-start.4
  19.7 10.5 %collective-permute-start.5 = (bf16[2048,1024]{1,0:T(8,128)(2,1)}, bf16[2048,1024]{1,0:T(8,128)(2,1)}, u32[]{:S(2)}, u32[]{:S(2)}) collective-permute-start(bf16[2048,1024]{1,0:T(8,128)(2,1)} %get-tuple-element.42), channel_id=1, source_target_pairs={{0,4},{1,5},{2,6},{3,7},{4,8},{5,9},{6,10},{7,11},{16,20},{17,21},... | collective-permute-start | bytes 12582920 | tf_op jit(solution)/shard_map/ppermute | solution.py:603
  30.2 85.1 %collective-permute-done.2.refs_2_ = bf16[2192,1024]{1,0:T(8,128)(2,1)} collective-permute-done((bf16[2192,1024]{1,0:T(8,128)(2,1)}, bf16[2192,1024]{1,0:T(8,128)(2,1)}, u32[]{:S(2)}, u32[]{:S(2)}) %collective-permute-start.2) | collective-permute-done | bytes 4489248 | tf_op jit(solution)/shard_map/ppermute | solution.py:603
  115.3 3.0 collective-permute-done.5
  118.3 2.6 collective-permute-start.6
  121.0 2.5 collective-permute-done.4.refs_4_
  123.5 1.3 collective-permute-start.7
  124.8 0.7 slice.32
  125.6 0.7 dynamic-slice_bitcast_fusion
  126.3 0.7 slice.45
  127.0 0.7 slice.43
  127.6 0.7 slice.42
  128.3 0.7 slice.44
  129.5 0.2 slice_reduce_fusion
  129.7 0.3 select_reduce_fusion
  130.8 2.3 copy-done
  133.0 6.8 %pairs.2 = (f32[28,64,512]{2,1,0:T(8,128)S(1)}, bf16[2,896,512]{2,1,0:T(8,128)(2,1)S(1)}, bf16[20,512,512]{2,1,0:T(8,128)(2,1)}) custom-call(s32[2,20]{1,0:T(2,128)S(1)} %pad_add_fusion.items, s32[3]{0:T(128)S(1)} %convert_reduce_fusion.1.bounds, bf16[2192,1024]{1,0:T(8,128)(2,1)S(1)} %copy-done, bf16[2192,1024]{1,0:T(8,128)(2,1)} %collective-permute-done.1.refs_1_, ...), custom_call_target="tpu_custom_call" | custom-call | tf_op jit(solution)/shard_map/pairs/pallas_call | solution.py:371
  139.9 79.2 %collective-permute-done.7.refs_6_ = bf16[2048,1024]{1,0:T(8,128)(2,1)} collective-permute-done((bf16[2048,1024]{1,0:T(8,128)(2,1)}, bf16[2048,1024]{1,0:T(8,128)(2,1)}, u32[]{:S(2)}, u32[]{:S(2)}) %collective-permute-start.7) | collective-permute-done | bytes 4194336 | tf_op jit(solution)/shard_map/ppermute | solution.py:603
  219.1 7.8 %pairs.3 = (f32[4,64,512]{2,1,0:T(8,128)S(1)}, bf16[4,64,512]{2,1,0:T(8,128)(2,1)S(1)}, bf16[4,64,512]{2,1,0:T(8,128)(2,1)S(1)}, bf16[4,64,512]{2,1,0:T(8,128)(2...) custom-call(s32[2,20]{1,0:T(2,128)S(1)} %pad_add_fusion.items, ...), custom_call_target="tpu_custom_call", output_to_operand_aliasing={{6}: (10, {})} | custom-call | tf_op jit(solution)/shard_map/pairs/pallas_call | solution.py:371
  227.0 3.1 collective-permute-start.12
  230.1 0.3 collective-permute-start.9
  230.4 1.3 collective-permute-start.11
  231.8 10.8 %collective-permute-done.12.refs_3_ = bf16[4,64,512]{2,1,0:T(8,128)(2,1)S(1)} collective-permute-done((bf16[4,64,512]{2,1,0:T(8,128)(2,1)S(1)}, bf16[4,64,512]{2,1,0:T(8,128)(2,1)S(1)}, u32[]{:S(2)}, u32[]{:S(2)}) %collective-permute-start.12) | collective-permute-done | bytes 262176 | tf_op jit(solution)/shard_map/ppermute | solution.py:632
  242.7 0.6 gram.2
  243.4 1.7 collective-permute-start.14
  245.0 0.2 collective-permute-start.13
  245.2 1.6 collective-permute-done.15
  246.8 1.0 collective-permute-done.14
  247.8 3.6 %collective-permute-start.18 = (f32[64,64]{1,0:T(8,128)S(1)}, f32[64,64]{1,0:T(8,128)S(1)}, u32[]{:S(2)}, u32[]{:S(2)}) collective-permute-start(f32[64,64]{1,0:T(8,128)S(1)} %add_add_fusion.1.refs_0_), channel_id=1, source_target_pairs={{0,12},{1,13},{2,14},{3,15},{4,8},{5,9},{6,10},{7,11},{8,4},{9,5},... | collective-permute-start | bytes 49160 | tf_op jit(solution)/shard_map/ppermute | solution.py:561
  251.3 0.9 collective-permute-start.16
  252.2 1.3 collective-permute-done.18.refs_3_
  253.5 2.6 collective-permute-done.17.refs_2_
  256.2 3.6 %panel.4.refs_0_ = bf16[128,1024]{1,0:T(8,128)(2,1)S(1)} custom-call(f32[64,64]{1,0:T(8,128)S(1)} %add_add_fusion.1.refs_0_, f32[64,64]{1,0:T(8,128)S(1)} %collective-permute-done.16.refs_1_, f32[64,64]{1,0:T(8,128)S(1)} %collective-permute-done.17.refs_2_, f32[64,64]{1,0:T(8,128)S(1)} %collective-permute-done.18.refs_3_, ...), custom_call_target="tpu_custom_call" | custom-call | tf_op jit(solution)/shard_map/panel/pallas_call | solution.py:546
  259.8 1.3 collective-permute-start.20
  261.1 3.9 %collective-permute-start.23 = (bf16[128,1024]{1,0:T(8,128)(2,1)S(1)}, bf16[128,1024]{1,0:T(8,128)(2,1)S(1)}, u32[]{:S(2)}, u32[]{:S(2)}) collective-permute-start(bf16[128,1024]{1,0:T(8,128)(2,1)S(1)} %panel.4.refs_0_), channel_id=1, source_target_pairs={{0,8},{1,9},{2,10},{3,11},{4,12},{5,13},{6,14},{7,15},{12,0},{13,1... | collective-permute-start | bytes 786440 | tf_op jit(solution)/shard_map/ppermute | solution.py:586
  265.0 1.3 collective-permute-start.22
  266.5 0.4 collective-permute-start.21
  266.9 6.6 %collective-permute-done.23.refs_5_ = bf16[128,1024]{1,0:T(8,128)(2,1)S(1)} collective-permute-done((bf16[128,1024]{1,0:T(8,128)(2,1)S(1)}, bf16[128,1024]{1,0:T(8,128)(2,1)S(1)}, u32[]{:S(2)}, u32[]{:S(2)}) %collective-permute-start.23) | collective-permute-done | bytes 262176 | tf_op jit(solution)/shard_map/ppermute | solution.py:586
  273.6 2.7 collective-permute-done.22.refs_4_
  276.3 4.6 %apply.1 = (f32[4,64,512]{2,1,0:T(8,128)S(1)}, bf16[4,64,512]{2,1,0:T(8,128)(2,1)S(1)}, bf16[4,64,512]{2,1,0:T(8,128)(2,1)S(1)}, bf16[4,64,512]{2,1,0:T(8,128)(2...) custom-call(s32[2,20]{1,0:T(2,128)S(1)} %pad_add_fusion.items, ...), custom_call_target="tpu_custom_call" | custom-call | tf_op jit(solution)/shard_map/apply/pallas_call | solution.py:431
  280.9 0.4 collective-permute-start.24
  281.2 1.9 collective-permute-start.28
  283.2 0.3 collective-permute-start.25
  283.4 1.6 collective-permute-start.27
  285.1 2.0 collective-permute-start.26
  287.1 10.5 %collective-permute-done.28.refs_3_ = bf16[4,64,512]{2,1,0:T(8,128)(2,1)S(1)} collective-permute-done((bf16[4,64,512]{2,1,0:T(8,128)(2,1)S(1)}, bf16[4,64,512]{2,1,0:T(8,128)(2,1)S(1)}, u32[]{:S(2)}, u32[]{:S(2)}) %collective-permute-start.28) | collective-permute-done | bytes 262176 | tf_op jit(solution)/shard_map/ppermute | solution.py:632
  297.6 0.6 gram.3
  298.3 0.5 collective-permute-start.31
  298.7 1.3 collective-permute-start.30
  300.0 0.2 collective-permute-start.29
  300.2 1.6 collective-permute-done.31
  301.8 0.9 collective-permute-done.30
  302.7 2.9 collective-permute-start.34
  305.7 1.5 collective-permute-start.32
  307.2 1.4 collective-permute-done.34.refs_3_
  308.6 1.9 collective-permute-done.33.refs_2_
  310.5 4.4 %panel.5 = f32[64,2048]{1,0:T(8,128)} custom-call(f32[64,64]{1,0:T(8,128)S(1)} %add_add_fusion.refs_0_, f32[64,64]{1,0:T(8,128)S(1)} %collective-permute-done.32.refs_1_, f32[64,64]{1,0:T(8,128)S(1)} %collective-permute-done.33.refs_2_, f32[64,64]{1,0:T(8,128)S(1)} %collective-permute-done.34.refs_3_, f32[4,64,512]{2,1,0:T(8,128)S(1)} %get-tuple-element.66.refs_4_), custom_call_target="tpu_custom_call" | custom-call | tf_op jit(solution)/shard_map/panel/pallas_call | solution.py:546
  (60 shorter events, 2.0 us)
Async XLA Ops:
  0.7 1.0 copy-start.2
  1.7 0.7 copy-start.3
  3.0 6.0 %copy-start.1 = (bf16[144,1024]{1,0:T(8,128)(2,1)}, bf16[144,1024]{1,0:T(8,128)(2,1)S(1)}, u32[]{:S(2)}) copy-start(bf16[144,1024]{1,0:T(8,128)(2,1)S(1)} %extra.1) | copy-start | bytes 884740
  3.0 14.0 %collective-permute-start = (bf16[144,1024]{1,0:T(8,128)(2,1)S(1)}, bf16[144,1024]{1,0:T(8,128)(2,1)S(1)}, u32[]{:S(2)}, u32[]{:S(2)}) collective-permute-start(bf16[144,1024]{1,0:T(8,128)(2,1)S(1)} %extra.1), channel_id=1, source_target_pairs={{0,8},{1,9},{2,10},{3,11},{4,12},{5,13},{6,14},{7,15},{12,0},{13,1... | collective-permute-start | bytes 884744 | tf_op jit(solution)/shard_map/ppermute | solution.py:591
  16.9 98.4 %collective-permute-start.2 = (bf16[2192,1024]{1,0:T(8,128)(2,1)}, bf16[2192,1024]{1,0:T(8,128)(2,1)}, u32[]{:S(2)}, u32[]{:S(2)}) collective-permute-start(bf16[2192,1024]{1,0:T(8,128)(2,1)} %get-tuple-element.39.refs_0_), channel_id=1, source_target_pairs={{0,2},{1,3},{2,0},{3,1},{4,6},{5,7},{6,4},{7,5},{8,10},{9,11},{10,... | collective-permute-start | bytes 13467656 | tf_op jit(solution)/shard_map/ppermute | solution.py:603
  18.5 105.0 %collective-permute-start.4 = (bf16[2192,1024]{1,0:T(8,128)(2,1)}, bf16[2192,1024]{1,0:T(8,128)(2,1)}, u32[]{:S(2)}, u32[]{:S(2)}) collective-permute-start(bf16[2192,1024]{1,0:T(8,128)(2,1)} %get-tuple-element.39.refs_0_), channel_id=1, source_target_pairs={{4,0},{5,1},{6,2},{7,3},{8,4},{9,5},{10,6},{11,7},{12,8},{13,9},{1... | collective-permute-start | bytes 13467656 | tf_op jit(solution)/shard_map/ppermute | solution.py:603
  19.7 98.6 %collective-permute-start.5 = (bf16[2048,1024]{1,0:T(8,128)(2,1)}, bf16[2048,1024]{1,0:T(8,128)(2,1)}, u32[]{:S(2)}, u32[]{:S(2)}) collective-permute-start(bf16[2048,1024]{1,0:T(8,128)(2,1)} %get-tuple-element.42), channel_id=1, source_target_pairs={{0,4},{1,5},{2,6},{3,7},{4,8},{5,9},{6,10},{7,11},{16,20},{17,21},... | collective-permute-start | bytes 12582920 | tf_op jit(solution)/shard_map/ppermute | solution.py:603
  30.2 97.4 %collective-permute-start.1 = (bf16[2192,1024]{1,0:T(8,128)(2,1)}, bf16[2192,1024]{1,0:T(8,128)(2,1)}, u32[]{:S(2)}, u32[]{:S(2)}) collective-permute-start(bf16[2192,1024]{1,0:T(8,128)(2,1)} %get-tuple-element.39.refs_0_), channel_id=1, source_target_pairs={{0,1},{1,0},{2,3},{3,2},{4,5},{5,4},{6,7},{7,6},{8,9},{9,8},{10,11... | collective-permute-start | bytes 13467656 | tf_op jit(solution)/shard_map/ppermute | solution.py:603
  115.3 13.0 %collective-permute-start.3 = (bf16[2192,1024]{1,0:T(8,128)(2,1)}, bf16[2192,1024]{1,0:T(8,128)(2,1)}, u32[]{:S(2)}, u32[]{:S(2)}) collective-permute-start(bf16[2192,1024]{1,0:T(8,128)(2,1)} %collective-permute-done.2.refs_2_), channel_id=1, source_target_pairs={{0,1},{1,0},{2,3},{3,2},{4,5},{5,4},{6,7},{7,6},{8,9},{9,8},{10,11... | collective-permute-start | bytes 13467656 | tf_op jit(solution)/shard_map/ppermute | solution.py:603
  118.3 21.5 %collective-permute-start.6 = (bf16[2048,1024]{1,0:T(8,128)(2,1)}, bf16[2048,1024]{1,0:T(8,128)(2,1)}, u32[]{:S(2)}, u32[]{:S(2)}) collective-permute-start(bf16[2048,1024]{1,0:T(8,128)(2,1)} %collective-permute-done.5), channel_id=1, source_target_pairs={{4,8},{5,9},{6,10},{7,11},{8,12},{9,13},{10,14},{11,15},{20,24},{2... | collective-permute-start | bytes 12582920 | tf_op jit(solution)/shard_map/ppermute | solution.py:603
  123.5 95.6 %collective-permute-start.7 = (bf16[2048,1024]{1,0:T(8,128)(2,1)}, bf16[2048,1024]{1,0:T(8,128)(2,1)}, u32[]{:S(2)}, u32[]{:S(2)}) collective-permute-start(bf16[2048,1024]{1,0:T(8,128)(2,1)} %get-tuple-element.42), channel_id=1, source_target_pairs={{12,0},{13,1},{14,2},{15,3},{28,16},{29,17},{30,18},{31,19}} | collective-permute-start | bytes 12582920 | tf_op jit(solution)/shard_map/ppermute | solution.py:603
  130.7 2.3 copy-start
  226.9 3.2 %collective-permute-start.8 = (bf16[4,64,512]{2,1,0:T(8,128)(2,1)S(1)}, bf16[4,64,512]{2,1,0:T(8,128)(2,1)S(1)}, u32[]{:S(2)}, u32[]{:S(2)}) collective-permute-start(bf16[4,64,512]{2,1,0:T(8,128)(2,1)S(1)} %get-tuple-element.48), channel_id=1, source_target_pairs={{1,0},{0,1},{3,2},{2,3},{5,4},{4,5},{7,6},{6,7},{9,8},{8,9},{11,10... | collective-permute-start | bytes 786440 | tf_op jit(solution)/shard_map/ppermute | solution.py:632
  227.0 15.7 %collective-permute-start.12 = (bf16[4,64,512]{2,1,0:T(8,128)(2,1)S(1)}, bf16[4,64,512]{2,1,0:T(8,128)(2,1)S(1)}, u32[]{:S(2)}, u32[]{:S(2)}) collective-permute-start(bf16[4,64,512]{2,1,0:T(8,128)(2,1)S(1)} %get-tuple-element.53), channel_id=1, source_target_pairs={{8,0},{9,1},{10,2},{11,3},{12,4},{13,5},{14,6},{15,7},{0,12},{1,13... | collective-permute-start | bytes 786440 | tf_op jit(solution)/shard_map/ppermute | solution.py:632
  230.1 12.6 %collective-permute-start.9 = (bf16[4,64,512]{2,1,0:T(8,128)(2,1)S(1)}, bf16[4,64,512]{2,1,0:T(8,128)(2,1)S(1)}, u32[]{:S(2)}, u32[]{:S(2)}) collective-permute-start(bf16[4,64,512]{2,1,0:T(8,128)(2,1)S(1)} %get-tuple-element.49), channel_id=1, source_target_pairs={{1,0},{0,1},{3,2},{2,3},{5,4},{4,5},{7,6},{6,7},{9,8},{8,9},{11,10... | collective-permute-start | bytes 786440 | tf_op jit(solution)/shard_map/ppermute | solution.py:632
  230.4 12.3 %collective-permute-start.11 = (bf16[4,64,512]{2,1,0:T(8,128)(2,1)S(1)}, bf16[4,64,512]{2,1,0:T(8,128)(2,1)S(1)}, u32[]{:S(2)}, u32[]{:S(2)}) collective-permute-start(bf16[4,64,512]{2,1,0:T(8,128)(2,1)S(1)} %get-tuple-element.52), channel_id=1, source_target_pairs={{0,4},{1,5},{2,6},{3,7},{4,8},{5,9},{6,10},{7,11},{8,12},{9,13},{1... | collective-permute-start | bytes 786440 | tf_op jit(solution)/shard_map/ppermute | solution.py:632
  231.7 10.9 %collective-permute-start.10 = (bf16[4,64,512]{2,1,0:T(8,128)(2,1)S(1)}, bf16[4,64,512]{2,1,0:T(8,128)(2,1)S(1)}, u32[]{:S(2)}, u32[]{:S(2)}) collective-permute-start(bf16[4,64,512]{2,1,0:T(8,128)(2,1)S(1)} %add.84), channel_id=1, source_target_pairs={{2,0},{3,1},{0,2},{1,3},{6,4},{7,5},{4,6},{5,7},{10,8},{11,9},{8,1... | collective-permute-start | bytes 786440 | tf_op jit(solution)/shard_map/ppermute | solution.py:632
  243.3 3.5 %collective-permute-start.15 = (f32[64,64]{1,0:T(8,128)S(1)}, f32[64,64]{1,0:T(8,128)S(1)}, u32[]{:S(2)}, u32[]{:S(2)}) collective-permute-start(f32[64,64]{1,0:T(8,128)S(1)} %get-tuple-element.54), channel_id=1, source_target_pairs={{0,3},{1,2},{2,1},{3,0},{4,7},{5,6},{6,5},{7,4},{8,11},{9,10},{10,... | collective-permute-start | bytes 49160 | tf_op jit(solution)/shard_map/ppermute | solution.py:561
  243.4 4.4 %collective-permute-start.14 = (f32[64,64]{1,0:T(8,128)S(1)}, f32[64,64]{1,0:T(8,128)S(1)}, u32[]{:S(2)}, u32[]{:S(2)}) collective-permute-start(f32[64,64]{1,0:T(8,128)S(1)} %get-tuple-element.54), channel_id=1, source_target_pairs={{0,2},{1,3},{2,0},{3,1},{4,6},{5,7},{6,4},{7,5},{8,10},{9,11},{10,... | collective-permute-start | bytes 49160 | tf_op jit(solution)/shard_map/ppermute | solution.py:561
  245.0 2.7 collective-permute-start.13
  247.8 5.8 %collective-permute-start.18 = (f32[64,64]{1,0:T(8,128)S(1)}, f32[64,64]{1,0:T(8,128)S(1)}, u32[]{:S(2)}, u32[]{:S(2)}) collective-permute-start(f32[64,64]{1,0:T(8,128)S(1)} %add_add_fusion.1.refs_0_), channel_id=1, source_target_pairs={{0,12},{1,13},{2,14},{3,15},{4,8},{5,9},{6,10},{7,11},{8,4},{9,5},... | collective-permute-start | bytes 49160 | tf_op jit(solution)/shard_map/ppermute | solution.py:561
  251.3 4.8 %collective-permute-start.17 = (f32[64,64]{1,0:T(8,128)S(1)}, f32[64,64]{1,0:T(8,128)S(1)}, u32[]{:S(2)}, u32[]{:S(2)}) collective-permute-start(f32[64,64]{1,0:T(8,128)S(1)} %add_add_fusion.1.refs_0_), channel_id=1, source_target_pairs={{0,8},{1,9},{2,10},{3,11},{4,12},{5,13},{6,14},{7,15},{8,0},{9,1},... | collective-permute-start | bytes 49160 | tf_op jit(solution)/shard_map/ppermute | solution.py:561
  251.3 4.8 %collective-permute-start.16 = (f32[64,64]{1,0:T(8,128)S(1)}, f32[64,64]{1,0:T(8,128)S(1)}, u32[]{:S(2)}, u32[]{:S(2)}) collective-permute-start(f32[64,64]{1,0:T(8,128)S(1)} %add_add_fusion.1.refs_0_), channel_id=1, source_target_pairs={{0,4},{1,5},{2,6},{3,7},{4,0},{5,1},{6,2},{7,3},{8,12},{9,13},{10,... | collective-permute-start | bytes 49160 | tf_op jit(solution)/shard_map/ppermute | solution.py:561
  259.8 6.7 %collective-permute-start.20 = (bf16[128,1024]{1,0:T(8,128)(2,1)S(1)}, bf16[128,1024]{1,0:T(8,128)(2,1)S(1)}, u32[]{:S(2)}, u32[]{:S(2)}) collective-permute-start(bf16[128,1024]{1,0:T(8,128)(2,1)S(1)} %panel.4.refs_0_), channel_id=1, source_target_pairs={{0,2},{1,3},{2,0},{3,1},{4,6},{5,7},{6,4},{7,5},{8,10},{9,11},{10,... | collective-permute-start | bytes 786440 | tf_op jit(solution)/shard_map/ppermute | solution.py:586
  261.1 12.4 %collective-permute-start.23 = (bf16[128,1024]{1,0:T(8,128)(2,1)S(1)}, bf16[128,1024]{1,0:T(8,128)(2,1)S(1)}, u32[]{:S(2)}, u32[]{:S(2)}) collective-permute-start(bf16[128,1024]{1,0:T(8,128)(2,1)S(1)} %panel.4.refs_0_), channel_id=1, source_target_pairs={{0,8},{1,9},{2,10},{3,11},{4,12},{5,13},{6,14},{7,15},{12,0},{13,1... | collective-permute-start | bytes 786440 | tf_op jit(solution)/shard_map/ppermute | solution.py:586
  265.0 11.2 %collective-permute-start.22 = (bf16[128,1024]{1,0:T(8,128)(2,1)S(1)}, bf16[128,1024]{1,0:T(8,128)(2,1)S(1)}, u32[]{:S(2)}, u32[]{:S(2)}) collective-permute-start(bf16[128,1024]{1,0:T(8,128)(2,1)S(1)} %panel.4.refs_0_), channel_id=1, source_target_pairs={{4,0},{5,1},{6,2},{7,3},{8,4},{9,5},{10,6},{11,7},{12,8},{13,9},{1... | collective-permute-start | bytes 786440 | tf_op jit(solution)/shard_map/ppermute | solution.py:586
  266.3 9.9 %collective-permute-start.19 = (bf16[128,1024]{1,0:T(8,128)(2,1)S(1)}, bf16[128,1024]{1,0:T(8,128)(2,1)S(1)}, u32[]{:S(2)}, u32[]{:S(2)}) collective-permute-start(bf16[128,1024]{1,0:T(8,128)(2,1)S(1)} %panel.4.refs_0_), channel_id=1, source_target_pairs={{0,1},{1,0},{2,3},{3,2},{4,5},{5,4},{6,7},{7,6},{8,9},{9,8},{10,11... | collective-permute-start | bytes 786440 | tf_op jit(solution)/shard_map/ppermute | solution.py:586
  266.5 9.8 %collective-permute-start.21 = (bf16[128,1024]{1,0:T(8,128)(2,1)S(1)}, bf16[128,1024]{1,0:T(8,128)(2,1)S(1)}, u32[]{:S(2)}, u32[]{:S(2)}) collective-permute-start(bf16[128,1024]{1,0:T(8,128)(2,1)S(1)} %collective-permute-done.20.refs_2_), channel_id=1, source_target_pairs={{0,1},{1,0},{2,3},{3,2},{4,5},{5,4},{6,7},{7,6},{8,9},{9,8},{10,11... | collective-permute-start | bytes 786440 | tf_op jit(solution)/shard_map/ppermute | solution.py:586
  280.9 2.3 collective-permute-start.24
  281.2 16.4 %collective-permute-start.28 = (bf16[4,64,512]{2,1,0:T(8,128)(2,1)S(1)}, bf16[4,64,512]{2,1,0:T(8,128)(2,1)S(1)}, u32[]{:S(2)}, u32[]{:S(2)}) collective-permute-start(bf16[4,64,512]{2,1,0:T(8,128)(2,1)S(1)} %get-tuple-element.64), channel_id=1, source_target_pairs={{8,0},{9,1},{10,2},{11,3},{12,4},{13,5},{14,6},{15,7},{0,12},{1,13... | collective-permute-start | bytes 786440 | tf_op jit(solution)/shard_map/ppermute | solution.py:632
  283.2 14.4 %collective-permute-start.25 = (bf16[4,64,512]{2,1,0:T(8,128)(2,1)S(1)}, bf16[4,64,512]{2,1,0:T(8,128)(2,1)S(1)}, u32[]{:S(2)}, u32[]{:S(2)}) collective-permute-start(bf16[4,64,512]{2,1,0:T(8,128)(2,1)S(1)} %get-tuple-element.60), channel_id=1, source_target_pairs={{1,0},{0,1},{3,2},{2,3},{5,4},{4,5},{7,6},{6,7},{9,8},{8,9},{11,10... | collective-permute-start | bytes 786440 | tf_op jit(solution)/shard_map/ppermute | solution.py:632
  283.4 14.2 %collective-permute-start.27 = (bf16[4,64,512]{2,1,0:T(8,128)(2,1)S(1)}, bf16[4,64,512]{2,1,0:T(8,128)(2,1)S(1)}, u32[]{:S(2)}, u32[]{:S(2)}) collective-permute-start(bf16[4,64,512]{2,1,0:T(8,128)(2,1)S(1)} %get-tuple-element.63), channel_id=1, source_target_pairs={{0,4},{1,5},{2,6},{3,7},{4,8},{5,9},{6,10},{7,11},{8,12},{9,13},{1... | collective-permute-start | bytes 786440 | tf_op jit(solution)/shard_map/ppermute | solution.py:632
  285.1 12.5 %collective-permute-start.26 = (bf16[4,64,512]{2,1,0:T(8,128)(2,1)S(1)}, bf16[4,64,512]{2,1,0:T(8,128)(2,1)S(1)}, u32[]{:S(2)}, u32[]{:S(2)}) collective-permute-start(bf16[4,64,512]{2,1,0:T(8,128)(2,1)S(1)} %add.88), channel_id=1, source_target_pairs={{2,0},{3,1},{0,2},{1,3},{6,4},{7,5},{4,6},{5,7},{10,8},{11,9},{8,1... | collective-permute-start | bytes 786440 | tf_op jit(solution)/shard_map/ppermute | solution.py:632
  298.3 3.5 %collective-permute-start.31 = (f32[64,64]{1,0:T(8,128)S(1)}, f32[64,64]{1,0:T(8,128)S(1)}, u32[]{:S(2)}, u32[]{:S(2)}) collective-permute-start(f32[64,64]{1,0:T(8,128)S(1)} %get-tuple-element.65), channel_id=1, source_target_pairs={{0,3},{1,2},{2,1},{3,0},{4,7},{5,6},{6,5},{7,4},{8,11},{9,10},{10,... | collective-permute-start | bytes 49160 | tf_op jit(solution)/shard_map/ppermute | solution.py:561
  298.7 4.0 %collective-permute-start.30 = (f32[64,64]{1,0:T(8,128)S(1)}, f32[64,64]{1,0:T(8,128)S(1)}, u32[]{:S(2)}, u32[]{:S(2)}) collective-permute-start(f32[64,64]{1,0:T(8,128)S(1)} %get-tuple-element.65), channel_id=1, source_target_pairs={{0,2},{1,3},{2,0},{3,1},{4,6},{5,7},{6,4},{7,5},{8,10},{9,11},{10,... | collective-permute-start | bytes 49160 | tf_op jit(solution)/shard_map/ppermute | solution.py:561
  300.0 2.7 collective-permute-start.29
  302.7 5.9 %collective-permute-start.34 = (f32[64,64]{1,0:T(8,128)S(1)}, f32[64,64]{1,0:T(8,128)S(1)}, u32[]{:S(2)}, u32[]{:S(2)}) collective-permute-start(f32[64,64]{1,0:T(8,128)S(1)} %add_add_fusion.refs_0_), channel_id=1, source_target_pairs={{0,12},{1,13},{2,14},{3,15},{4,8},{5,9},{6,10},{7,11},{8,4},{9,5},... | collective-permute-start | bytes 49160 | tf_op jit(solution)/shard_map/ppermute | solution.py:561
  305.7 4.8 %collective-permute-start.33 = (f32[64,64]{1,0:T(8,128)S(1)}, f32[64,64]{1,0:T(8,128)S(1)}, u32[]{:S(2)}, u32[]{:S(2)}) collective-permute-start(f32[64,64]{1,0:T(8,128)S(1)} %add_add_fusion.refs_0_), channel_id=1, source_target_pairs={{0,8},{1,9},{2,10},{3,11},{4,12},{5,13},{6,14},{7,15},{8,0},{9,1},... | collective-permute-start | bytes 49160 | tf_op jit(solution)/shard_map/ppermute | solution.py:561
  305.7 4.8 %collective-permute-start.32 = (f32[64,64]{1,0:T(8,128)S(1)}, f32[64,64]{1,0:T(8,128)S(1)}, u32[]{:S(2)}, u32[]{:S(2)}) collective-permute-start(f32[64,64]{1,0:T(8,128)S(1)} %add_add_fusion.refs_0_), channel_id=1, source_target_pairs={{0,4},{1,5},{2,6},{3,7},{4,0},{5,1},{6,2},{7,3},{8,12},{9,13},{10,... | collective-permute-start | bytes 49160 | tf_op jit(solution)/shard_map/ppermute | solution.py:561

commit v6 on v5

--- a/solution.py
+++ b/solution.py
@@ -553,14 +553,17 @@
 
 def sum_over_rows(value):
     count = lax.axis_size("rows")
-    terms, step = [value], 1
+    rounds, step = [], 1
     while step < count:
+        radix = min(4, count // step)
+        rounds.append((step, radix))
+        step *= radix
+    terms = [value]
+    for step, radix in reversed(rounds):
         value = functools.reduce(jnp.add, terms)
-        radix = min(4, count // step)
         terms = [value] + [
             lax.ppermute(value, "rows", [(i, i ^ (step * m)) for i in range(count)]) for m in range(1, radix)
         ]
-        step *= radix
     return terms
 
 
@@ -581,10 +584,13 @@
     ]
 
     def spread(value):
-        got = [value]
-        for group, pairs in zip(joint, merged):
-            got.append(lax.ppermute(got[via.get(group[0], 0)], "rows", pairs))
-        return got
+        got = {0: value}
+        for n in sorted(range(1, len(joint) + 1), key=lambda n: n in after_back):
+            outgoing = got[via.get(joint[n - 1][0], 0)]
+            if n in after_back:
+                outgoing, _ = lax.optimization_barrier((outgoing, got[via[after_back[n]]]))
+            got[n] = lax.ppermute(outgoing, "rows", merged[n - 1])
+        return [got[n] for n in range(len(joint) + 1)]
 
     assert count * per <= 256
     extra = extra_call(block_pairs.T, pair_count, start_panel, depth)

time: 319 us -> 320 us (level)
  waiting for transfers between devices: 214 us -> 204 us
  Pallas kernels: 36.2 us -> 46.1 us
  starting transfers between devices: 53.8 us -> 57.7 us
    pallas_call x2, Pallas kernels: 14.6 us -> 22.3 us  [pair_call(): pl.pallas_call(functools.partial(pair_kernel, stage, held_at, n_slab, joi...]
    ppermute x7, waiting for transfers between devices: 170 us -> 162 us  [on_device(): outgoing = lax.ppermute(outgoing, 'rows', pairs)]
  transfers between devices with their start and end apart: 35 -> 35, of which waited for: 18 -> 17; matrix products, arithmetic and copies ran while one was open for 2% -> 2% of each run, Pallas kernels for 4% -> 7%
where the time goes in v6:
time: 320 us; the launch traced here: 319 us
  waiting for transfers between devices  204 us (64%)
  starting transfers between devices  57.7 us (18%)
  Pallas kernels  46.1 us (14%)
  local copies, waits for them, and re-layouts  9.13 us (3%)
    ppermute x7, waiting for transfers between devices, on_device(): outgoing = lax.ppermute(outgoing, 'rows', pairs)  162 us
    pallas_call x2, Pallas kernels, pair_call(): pl.pallas_call(functools.partial(pair_kernel, stage, held_at, n_slab, joi...  22.3 us
    ppermute x10, waiting for transfers between devices, on_device(): lax.ppermute(outgoing, 'rows', [(target, source) for source, target in me...  18.4 us
    ppermute x7, starting transfers between devices, on_device(): outgoing = lax.ppermute(outgoing, 'rows', pairs)  17.2 us
    ppermute x12, starting transfers between devices, sum_over_rows(): lax.ppermute(value, 'rows', [(i, i ^ step * m) for i in range(count)])  14.3 us
    ppermute x10, starting transfers between devices, on_device(): lax.ppermute(outgoing, 'rows', [(target, source) for source, target in me...  12.6 us
    ppermute x12, waiting for transfers between devices, sum_over_rows(): lax.ppermute(value, 'rows', [(i, i ^ step * m) for i in range(count)])  11.4 us
    ppermute x5, waiting for transfers between devices, spread(): got[n] = lax.ppermute(outgoing, 'rows', merged[n - 1])  11.3 us
  transfers between devices with their start and end apart: 35, of which 17 were waited for; matrix products, arithmetic and copies ran while one was open for 2% of the time, Pallas kernels for 7%

profile of v6, /device:TPU:0, one launch (start us, length us, event | category | flops | bytes accessed | tf_op | source)
XLA Modules:
  0.0 319.1 jit_solution(15931796364453045014)
XLA Ops:
  0.7 1.0 copy-done.2
  1.7 0.7 copy-done.3
  2.4 0.6 extra.1
  3.0 5.9 %collective-permute-start = (bf16[144,1024]{1,0:T(8,128)(2,1)S(1)}, bf16[144,1024]{1,0:T(8,128)(2,1)S(1)}, u32[]{:S(2)}, u32[]{:S(2)}) collective-permute-start(bf16[144,1024]{1,0:T(8,128)(2,1)S(1)} %extra.1), channel_id=1, source_target_pairs={{0,8},{1,9},{2,10},{3,11},{4,12},{5,13},{6,14},{7,15},{12,0},{13,1... | collective-permute-start | bytes 884744 | tf_op jit(solution)/shard_map/ppermute | solution.py:597
  8.9 7.1 %pack.1 = (bf16[2048,1024]{1,0:T(8,128)(2,1)}, bf16[2192,1024]{1,0:T(8,128)(2,1)}) custom-call(bf16[2048,1024]{1,0:T(8,128)(2,1)} %rows.1, bf16[144,1024]{1,0:T(8,128)(2,1)} %copy-done.1), custom_call_target="tpu_custom_call" | custom-call | tf_op jit(solution)/shard_map/pack/pallas_call | solution.py:186
  16.0 0.9 collective-permute-done.refs_5_
  16.9 1.5 collective-permute-start.2
  18.5 1.3 collective-permute-start.4
  19.7 10.5 %collective-permute-start.5 = (bf16[2048,1024]{1,0:T(8,128)(2,1)}, bf16[2048,1024]{1,0:T(8,128)(2,1)}, u32[]{:S(2)}, u32[]{:S(2)}) collective-permute-start(bf16[2048,1024]{1,0:T(8,128)(2,1)} %get-tuple-element.43), channel_id=1, source_target_pairs={{0,4},{1,5},{2,6},{3,7},{4,8},{5,9},{6,10},{7,11},{16,20},{17,21},... | collective-permute-start | bytes 12582920 | tf_op jit(solution)/shard_map/ppermute | solution.py:609
  30.2 85.1 %collective-permute-done.2.refs_2_ = bf16[2192,1024]{1,0:T(8,128)(2,1)} collective-permute-done((bf16[2192,1024]{1,0:T(8,128)(2,1)}, bf16[2192,1024]{1,0:T(8,128)(2,1)}, u32[]{:S(2)}, u32[]{:S(2)}) %collective-permute-start.2) | collective-permute-done | bytes 4489248 | tf_op jit(solution)/shard_map/ppermute | solution.py:609
  115.3 3.0 collective-permute-done.5
  118.3 2.6 collective-permute-start.6
  121.0 2.5 collective-permute-done.4.refs_4_
  123.5 1.3 collective-permute-start.7
  124.8 0.7 slice.32
  125.6 0.7 dynamic-slice_bitcast_fusion
  126.3 0.7 slice.45
  127.0 0.7 slice.43
  127.6 0.7 slice.42
  128.3 0.7 slice.44
  129.5 0.2 slice_reduce_fusion
  129.7 0.3 select_reduce_fusion
  130.8 2.3 copy-done
  133.0 14.5 %pairs.2 = (f32[28,64,512]{2,1,0:T(8,128)S(1)}, bf16[2,896,512]{2,1,0:T(8,128)(2,1)S(1)}, bf16[20,512,512]{2,1,0:T(8,128)(2,1)}) custom-call(s32[2,20]{1,0:T(2,128)S(1)} %pad_add_fusion.items, s32[3]{0:T(128)S(1)} %convert_reduce_fusion.1.bounds, bf16[2192,1024]{1,0:T(8,128)(2,1)S(1)} %copy-done, bf16[2192,1024]{1,0:T(8,128)(2,1)} %collective-permute-done.1.refs_1_, ...), custom_call_target="tpu_custom_call" | custom-call | tf_op jit(solution)/shard_map/pairs/pallas_call | solution.py:371
  147.5 71.6 %collective-permute-done.7.refs_6_ = bf16[2048,1024]{1,0:T(8,128)(2,1)} collective-permute-done((bf16[2048,1024]{1,0:T(8,128)(2,1)}, bf16[2048,1024]{1,0:T(8,128)(2,1)}, u32[]{:S(2)}, u32[]{:S(2)}) %collective-permute-start.7) | collective-permute-done | bytes 4194336 | tf_op jit(solution)/shard_map/ppermute | solution.py:609
  219.1 7.8 %pairs.3 = (f32[4,64,512]{2,1,0:T(8,128)S(1)}, bf16[4,64,512]{2,1,0:T(8,128)(2,1)S(1)}, bf16[4,64,512]{2,1,0:T(8,128)(2,1)S(1)}, bf16[4,64,512]{2,1,0:T(8,128)(2...) custom-call(s32[2,20]{1,0:T(2,128)S(1)} %pad_add_fusion.items, ...), custom_call_target="tpu_custom_call", output_to_operand_aliasing={{6}: (10, {})} | custom-call | tf_op jit(solution)/shard_map/pairs/pallas_call | solution.py:371
  226.9 0.6 collective-permute-start.8
  227.6 2.3 collective-permute-start.12
  229.9 0.3 collective-permute-start.9
  230.2 1.3 collective-permute-start.11
  231.5 3.4 %collective-permute-start.10 = (bf16[4,64,512]{2,1,0:T(8,128)(2,1)S(1)}, bf16[4,64,512]{2,1,0:T(8,128)(2,1)S(1)}, u32[]{:S(2)}, u32[]{:S(2)}) collective-permute-start(bf16[4,64,512]{2,1,0:T(8,128)(2,1)S(1)} %add.84), channel_id=1, source_target_pairs={{2,0},{3,1},{0,2},{1,3},{6,4},{7,5},{4,6},{5,7},{10,8},{11,9},{8,1... | collective-permute-start | bytes 786440 | tf_op jit(solution)/shard_map/ppermute | solution.py:638
  234.9 7.5 %collective-permute-done.12.refs_3_ = bf16[4,64,512]{2,1,0:T(8,128)(2,1)S(1)} collective-permute-done((bf16[4,64,512]{2,1,0:T(8,128)(2,1)S(1)}, bf16[4,64,512]{2,1,0:T(8,128)(2,1)S(1)}, u32[]{:S(2)}, u32[]{:S(2)}) %collective-permute-start.12) | collective-permute-done | bytes 262176 | tf_op jit(solution)/shard_map/ppermute | solution.py:638
  242.4 0.6 gram.2
  243.1 3.6 %collective-permute-start.15 = (f32[64,64]{1,0:T(8,128)S(1)}, f32[64,64]{1,0:T(8,128)S(1)}, u32[]{:S(2)}, u32[]{:S(2)}) collective-permute-start(f32[64,64]{1,0:T(8,128)S(1)} %get-tuple-element.55), channel_id=1, source_target_pairs={{0,12},{1,13},{2,14},{3,15},{4,8},{5,9},{6,10},{7,11},{8,4},{9,5},... | collective-permute-start | bytes 49160 | tf_op jit(solution)/shard_map/ppermute | solution.py:565
  246.7 0.9 collective-permute-start.13
  247.5 1.3 collective-permute-done.15
  248.9 2.6 collective-permute-done.14
  251.5 1.8 collective-permute-start.18
  253.3 1.7 collective-permute-start.17
  255.0 2.2 collective-permute-done.17.refs_2_
  257.2 3.6 %panel.4.refs_0_ = bf16[128,1024]{1,0:T(8,128)(2,1)S(1)} custom-call(f32[64,64]{1,0:T(8,128)S(1)} %add_add_fusion.1.refs_0_, f32[64,64]{1,0:T(8,128)S(1)} %collective-permute-done.16.refs_1_, f32[64,64]{1,0:T(8,128)S(1)} %collective-permute-done.17.refs_2_, f32[64,64]{1,0:T(8,128)S(1)} %collective-permute-done.18.refs_3_, ...), custom_call_target="tpu_custom_call" | custom-call | tf_op jit(solution)/shard_map/panel/pallas_call | solution.py:546
  260.8 1.8 collective-permute-start.19
  262.6 3.9 %collective-permute-start.23 = (bf16[128,1024]{1,0:T(8,128)(2,1)S(1)}, bf16[128,1024]{1,0:T(8,128)(2,1)S(1)}, u32[]{:S(2)}, u32[]{:S(2)}) collective-permute-start(bf16[128,1024]{1,0:T(8,128)(2,1)S(1)} %panel.4.refs_0_), channel_id=1, source_target_pairs={{0,8},{1,9},{2,10},{3,11},{4,12},{5,13},{6,14},{7,15},{12,0},{13,1... | collective-permute-start | bytes 786440 | tf_op jit(solution)/shard_map/ppermute | solution.py:592
  266.6 3.1 collective-permute-done.19.refs_2_
  269.7 1.3 collective-permute-start.22
  271.1 0.5 collective-permute-start.21
  271.5 2.6 collective-permute-done.23.refs_5_
  274.1 5.6 %collective-permute-done.22.refs_4_ = bf16[128,1024]{1,0:T(8,128)(2,1)S(1)} collective-permute-done((bf16[128,1024]{1,0:T(8,128)(2,1)S(1)}, bf16[128,1024]{1,0:T(8,128)(2,1)S(1)}, u32[]{:S(2)}, u32[]{:S(2)}) %collective-permute-start.22) | collective-permute-done | bytes 262176 | tf_op jit(solution)/shard_map/ppermute | solution.py:592
  279.7 6.9 %apply.1 = (f32[4,64,512]{2,1,0:T(8,128)S(1)}, bf16[4,64,512]{2,1,0:T(8,128)(2,1)S(1)}, bf16[4,64,512]{2,1,0:T(8,128)(2,1)S(1)}, bf16[4,64,512]{2,1,0:T(8,128)(2...) custom-call(s32[2,20]{1,0:T(2,128)S(1)} %pad_add_fusion.items, ...), custom_call_target="tpu_custom_call" | custom-call | tf_op jit(solution)/shard_map/apply/pallas_call | solution.py:431
  286.7 1.9 collective-permute-start.28
  288.6 0.6 collective-permute-start.25
  289.2 1.5 collective-permute-start.27
  290.7 0.8 collective-permute-start.26
  291.5 10.9 %collective-permute-done.28.refs_3_ = bf16[4,64,512]{2,1,0:T(8,128)(2,1)S(1)} collective-permute-done((bf16[4,64,512]{2,1,0:T(8,128)(2,1)S(1)}, bf16[4,64,512]{2,1,0:T(8,128)(2,1)S(1)}, u32[]{:S(2)}, u32[]{:S(2)}) %collective-permute-start.28) | collective-permute-done | bytes 262176 | tf_op jit(solution)/shard_map/ppermute | solution.py:638
  302.4 0.6 gram.3
  303.0 2.7 collective-permute-start.31
  305.7 1.8 collective-permute-start.29
  307.4 1.3 collective-permute-done.31
  308.8 1.7 collective-permute-done.30
  310.6 0.8 collective-permute-start.33
  311.3 1.1 collective-permute-start.32
  312.4 1.5 collective-permute-done.34.refs_3_
  313.9 0.8 collective-permute-done.33.refs_2_
  314.6 4.4 %panel.5 = f32[64,2048]{1,0:T(8,128)} custom-call(f32[64,64]{1,0:T(8,128)S(1)} %add_add_fusion.refs_0_, f32[64,64]{1,0:T(8,128)S(1)} %collective-permute-done.32.refs_1_, f32[64,64]{1,0:T(8,128)S(1)} %collective-permute-done.33.refs_2_, f32[64,64]{1,0:T(8,128)S(1)} %collective-permute-done.34.refs_3_, f32[4,64,512]{2,1,0:T(8,128)S(1)} %get-tuple-element.68.refs_4_), custom_call_target="tpu_custom_call" | custom-call | tf_op jit(solution)/shard_map/panel/pallas_call | solution.py:546
  (60 shorter events, 1.9 us)
Async XLA Ops:
  0.7 1.0 copy-start.2
  1.7 0.7 copy-start.3
  3.0 6.0 %copy-start.1 = (bf16[144,1024]{1,0:T(8,128)(2,1)}, bf16[144,1024]{1,0:T(8,128)(2,1)S(1)}, u32[]{:S(2)}) copy-start(bf16[144,1024]{1,0:T(8,128)(2,1)S(1)} %extra.1) | copy-start | bytes 884740
  3.0 14.0 %collective-permute-start = (bf16[144,1024]{1,0:T(8,128)(2,1)S(1)}, bf16[144,1024]{1,0:T(8,128)(2,1)S(1)}, u32[]{:S(2)}, u32[]{:S(2)}) collective-permute-start(bf16[144,1024]{1,0:T(8,128)(2,1)S(1)} %extra.1), channel_id=1, source_target_pairs={{0,8},{1,9},{2,10},{3,11},{4,12},{5,13},{6,14},{7,15},{12,0},{13,1... | collective-permute-start | bytes 884744 | tf_op jit(solution)/shard_map/ppermute | solution.py:597
  16.9 98.4 %collective-permute-start.2 = (bf16[2192,1024]{1,0:T(8,128)(2,1)}, bf16[2192,1024]{1,0:T(8,128)(2,1)}, u32[]{:S(2)}, u32[]{:S(2)}) collective-permute-start(bf16[2192,1024]{1,0:T(8,128)(2,1)} %get-tuple-element.40.refs_0_), channel_id=1, source_target_pairs={{0,2},{1,3},{2,0},{3,1},{4,6},{5,7},{6,4},{7,5},{8,10},{9,11},{10,... | collective-permute-start | bytes 13467656 | tf_op jit(solution)/shard_map/ppermute | solution.py:609
  18.5 105.0 %collective-permute-start.4 = (bf16[2192,1024]{1,0:T(8,128)(2,1)}, bf16[2192,1024]{1,0:T(8,128)(2,1)}, u32[]{:S(2)}, u32[]{:S(2)}) collective-permute-start(bf16[2192,1024]{1,0:T(8,128)(2,1)} %get-tuple-element.40.refs_0_), channel_id=1, source_target_pairs={{4,0},{5,1},{6,2},{7,3},{8,4},{9,5},{10,6},{11,7},{12,8},{13,9},{1... | collective-permute-start | bytes 13467656 | tf_op jit(solution)/shard_map/ppermute | solution.py:609
  19.7 98.6 %collective-permute-start.5 = (bf16[2048,1024]{1,0:T(8,128)(2,1)}, bf16[2048,1024]{1,0:T(8,128)(2,1)}, u32[]{:S(2)}, u32[]{:S(2)}) collective-permute-start(bf16[2048,1024]{1,0:T(8,128)(2,1)} %get-tuple-element.43), channel_id=1, source_target_pairs={{0,4},{1,5},{2,6},{3,7},{4,8},{5,9},{6,10},{7,11},{16,20},{17,21},... | collective-permute-start | bytes 12582920 | tf_op jit(solution)/shard_map/ppermute | solution.py:609
  30.2 97.4 %collective-permute-start.1 = (bf16[2192,1024]{1,0:T(8,128)(2,1)}, bf16[2192,1024]{1,0:T(8,128)(2,1)}, u32[]{:S(2)}, u32[]{:S(2)}) collective-permute-start(bf16[2192,1024]{1,0:T(8,128)(2,1)} %get-tuple-element.40.refs_0_), channel_id=1, source_target_pairs={{0,1},{1,0},{2,3},{3,2},{4,5},{5,4},{6,7},{7,6},{8,9},{9,8},{10,11... | collective-permute-start | bytes 13467656 | tf_op jit(solution)/shard_map/ppermute | solution.py:609
  115.3 13.0 %collective-permute-start.3 = (bf16[2192,1024]{1,0:T(8,128)(2,1)}, bf16[2192,1024]{1,0:T(8,128)(2,1)}, u32[]{:S(2)}, u32[]{:S(2)}) collective-permute-start(bf16[2192,1024]{1,0:T(8,128)(2,1)} %collective-permute-done.2.refs_2_), channel_id=1, source_target_pairs={{0,1},{1,0},{2,3},{3,2},{4,5},{5,4},{6,7},{7,6},{8,9},{9,8},{10,11... | collective-permute-start | bytes 13467656 | tf_op jit(solution)/shard_map/ppermute | solution.py:609
  118.3 29.2 %collective-permute-start.6 = (bf16[2048,1024]{1,0:T(8,128)(2,1)}, bf16[2048,1024]{1,0:T(8,128)(2,1)}, u32[]{:S(2)}, u32[]{:S(2)}) collective-permute-start(bf16[2048,1024]{1,0:T(8,128)(2,1)} %collective-permute-done.5), channel_id=1, source_target_pairs={{4,8},{5,9},{6,10},{7,11},{8,12},{9,13},{10,14},{11,15},{20,24},{2... | collective-permute-start | bytes 12582920 | tf_op jit(solution)/shard_map/ppermute | solution.py:609
  123.5 95.6 %collective-permute-start.7 = (bf16[2048,1024]{1,0:T(8,128)(2,1)}, bf16[2048,1024]{1,0:T(8,128)(2,1)}, u32[]{:S(2)}, u32[]{:S(2)}) collective-permute-start(bf16[2048,1024]{1,0:T(8,128)(2,1)} %get-tuple-element.43), channel_id=1, source_target_pairs={{12,0},{13,1},{14,2},{15,3},{28,16},{29,17},{30,18},{31,19}} | collective-permute-start | bytes 12582920 | tf_op jit(solution)/shard_map/ppermute | solution.py:609
  130.7 2.3 copy-start
  226.9 2.9 collective-permute-start.8
  227.6 14.9 %collective-permute-start.12 = (bf16[4,64,512]{2,1,0:T(8,128)(2,1)S(1)}, bf16[4,64,512]{2,1,0:T(8,128)(2,1)S(1)}, u32[]{:S(2)}, u32[]{:S(2)}) collective-permute-start(bf16[4,64,512]{2,1,0:T(8,128)(2,1)S(1)} %get-tuple-element.54), channel_id=1, source_target_pairs={{8,0},{9,1},{10,2},{11,3},{12,4},{13,5},{14,6},{15,7},{0,12},{1,13... | collective-permute-start | bytes 786440 | tf_op jit(solution)/shard_map/ppermute | solution.py:638
  229.9 12.6 %collective-permute-start.9 = (bf16[4,64,512]{2,1,0:T(8,128)(2,1)S(1)}, bf16[4,64,512]{2,1,0:T(8,128)(2,1)S(1)}, u32[]{:S(2)}, u32[]{:S(2)}) collective-permute-start(bf16[4,64,512]{2,1,0:T(8,128)(2,1)S(1)} %get-tuple-element.50), channel_id=1, source_target_pairs={{1,0},{0,1},{3,2},{2,3},{5,4},{4,5},{7,6},{6,7},{9,8},{8,9},{11,10... | collective-permute-start | bytes 786440 | tf_op jit(solution)/shard_map/ppermute | solution.py:638
  230.2 12.3 %collective-permute-start.11 = (bf16[4,64,512]{2,1,0:T(8,128)(2,1)S(1)}, bf16[4,64,512]{2,1,0:T(8,128)(2,1)S(1)}, u32[]{:S(2)}, u32[]{:S(2)}) collective-permute-start(bf16[4,64,512]{2,1,0:T(8,128)(2,1)S(1)} %get-tuple-element.53), channel_id=1, source_target_pairs={{0,4},{1,5},{2,6},{3,7},{4,8},{5,9},{6,10},{7,11},{8,12},{9,13},{1... | collective-permute-start | bytes 786440 | tf_op jit(solution)/shard_map/ppermute | solution.py:638
  231.5 10.9 %collective-permute-start.10 = (bf16[4,64,512]{2,1,0:T(8,128)(2,1)S(1)}, bf16[4,64,512]{2,1,0:T(8,128)(2,1)S(1)}, u32[]{:S(2)}, u32[]{:S(2)}) collective-permute-start(bf16[4,64,512]{2,1,0:T(8,128)(2,1)S(1)} %add.84), channel_id=1, source_target_pairs={{2,0},{3,1},{0,2},{1,3},{6,4},{7,5},{4,6},{5,7},{10,8},{11,9},{8,1... | collective-permute-start | bytes 786440 | tf_op jit(solution)/shard_map/ppermute | solution.py:638
  243.1 5.8 %collective-permute-start.15 = (f32[64,64]{1,0:T(8,128)S(1)}, f32[64,64]{1,0:T(8,128)S(1)}, u32[]{:S(2)}, u32[]{:S(2)}) collective-permute-start(f32[64,64]{1,0:T(8,128)S(1)} %get-tuple-element.55), channel_id=1, source_target_pairs={{0,12},{1,13},{2,14},{3,15},{4,8},{5,9},{6,10},{7,11},{8,4},{9,5},... | collective-permute-start | bytes 49160 | tf_op jit(solution)/shard_map/ppermute | solution.py:565
  246.7 4.8 %collective-permute-start.14 = (f32[64,64]{1,0:T(8,128)S(1)}, f32[64,64]{1,0:T(8,128)S(1)}, u32[]{:S(2)}, u32[]{:S(2)}) collective-permute-start(f32[64,64]{1,0:T(8,128)S(1)} %get-tuple-element.55), channel_id=1, source_target_pairs={{0,8},{1,9},{2,10},{3,11},{4,12},{5,13},{6,14},{7,15},{8,0},{9,1},... | collective-permute-start | bytes 49160 | tf_op jit(solution)/shard_map/ppermute | solution.py:565
  246.7 4.8 %collective-permute-start.13 = (f32[64,64]{1,0:T(8,128)S(1)}, f32[64,64]{1,0:T(8,128)S(1)}, u32[]{:S(2)}, u32[]{:S(2)}) collective-permute-start(f32[64,64]{1,0:T(8,128)S(1)} %get-tuple-element.55), channel_id=1, source_target_pairs={{0,4},{1,5},{2,6},{3,7},{4,0},{5,1},{6,2},{7,3},{8,12},{9,13},{10,... | collective-permute-start | bytes 49160 | tf_op jit(solution)/shard_map/ppermute | solution.py:565
  251.5 3.5 %collective-permute-start.18 = (f32[64,64]{1,0:T(8,128)S(1)}, f32[64,64]{1,0:T(8,128)S(1)}, u32[]{:S(2)}, u32[]{:S(2)}) collective-permute-start(f32[64,64]{1,0:T(8,128)S(1)} %add_add_fusion.1.refs_0_), channel_id=1, source_target_pairs={{0,3},{1,2},{2,1},{3,0},{4,7},{5,6},{6,5},{7,4},{8,11},{9,10},{10,... | collective-permute-start | bytes 49160 | tf_op jit(solution)/shard_map/ppermute | solution.py:565
  253.3 3.9 %collective-permute-start.17 = (f32[64,64]{1,0:T(8,128)S(1)}, f32[64,64]{1,0:T(8,128)S(1)}, u32[]{:S(2)}, u32[]{:S(2)}) collective-permute-start(f32[64,64]{1,0:T(8,128)S(1)} %add_add_fusion.1.refs_0_), channel_id=1, source_target_pairs={{0,2},{1,3},{2,0},{3,1},{4,6},{5,7},{6,4},{7,5},{8,10},{9,11},{10,... | collective-permute-start | bytes 49160 | tf_op jit(solution)/shard_map/ppermute | solution.py:565
  255.0 2.2 collective-permute-start.16
  260.8 8.9 %collective-permute-start.19 = (bf16[128,1024]{1,0:T(8,128)(2,1)S(1)}, bf16[128,1024]{1,0:T(8,128)(2,1)S(1)}, u32[]{:S(2)}, u32[]{:S(2)}) collective-permute-start(bf16[128,1024]{1,0:T(8,128)(2,1)S(1)} %panel.4.refs_0_), channel_id=1, source_target_pairs={{0,2},{1,3},{2,0},{3,1},{4,6},{5,7},{6,4},{7,5},{8,10},{9,11},{10,... | collective-permute-start | bytes 786440 | tf_op jit(solution)/shard_map/ppermute | solution.py:592
  262.6 11.5 %collective-permute-start.23 = (bf16[128,1024]{1,0:T(8,128)(2,1)S(1)}, bf16[128,1024]{1,0:T(8,128)(2,1)S(1)}, u32[]{:S(2)}, u32[]{:S(2)}) collective-permute-start(bf16[128,1024]{1,0:T(8,128)(2,1)S(1)} %panel.4.refs_0_), channel_id=1, source_target_pairs={{0,8},{1,9},{2,10},{3,11},{4,12},{5,13},{6,14},{7,15},{12,0},{13,1... | collective-permute-start | bytes 786440 | tf_op jit(solution)/shard_map/ppermute | solution.py:592
  269.7 10.0 %collective-permute-start.22 = (bf16[128,1024]{1,0:T(8,128)(2,1)S(1)}, bf16[128,1024]{1,0:T(8,128)(2,1)S(1)}, u32[]{:S(2)}, u32[]{:S(2)}) collective-permute-start(bf16[128,1024]{1,0:T(8,128)(2,1)S(1)} %panel.4.refs_0_), channel_id=1, source_target_pairs={{4,0},{5,1},{6,2},{7,3},{8,4},{9,5},{10,6},{11,7},{12,8},{13,9},{1... | collective-permute-start | bytes 786440 | tf_op jit(solution)/shard_map/ppermute | solution.py:592
  271.0 8.7 %collective-permute-start.20 = (bf16[128,1024]{1,0:T(8,128)(2,1)S(1)}, bf16[128,1024]{1,0:T(8,128)(2,1)S(1)}, u32[]{:S(2)}, u32[]{:S(2)}) collective-permute-start(bf16[128,1024]{1,0:T(8,128)(2,1)S(1)} %panel.4.refs_0_), channel_id=1, source_target_pairs={{0,1},{1,0},{2,3},{3,2},{4,5},{5,4},{6,7},{7,6},{8,9},{9,8},{10,11... | collective-permute-start | bytes 786440 | tf_op jit(solution)/shard_map/ppermute | solution.py:592
  271.1 8.7 %collective-permute-start.21 = (bf16[128,1024]{1,0:T(8,128)(2,1)S(1)}, bf16[128,1024]{1,0:T(8,128)(2,1)S(1)}, u32[]{:S(2)}, u32[]{:S(2)}) collective-permute-start(bf16[128,1024]{1,0:T(8,128)(2,1)S(1)} %collective-permute-done.19.refs_2_), channel_id=1, source_target_pairs={{0,1},{1,0},{2,3},{3,2},{4,5},{5,4},{6,7},{7,6},{8,9},{9,8},{10,11... | collective-permute-start | bytes 786440 | tf_op jit(solution)/shard_map/ppermute | solution.py:592
  286.6 2.0 collective-permute-start.24
  286.7 15.7 %collective-permute-start.28 = (bf16[4,64,512]{2,1,0:T(8,128)(2,1)S(1)}, bf16[4,64,512]{2,1,0:T(8,128)(2,1)S(1)}, u32[]{:S(2)}, u32[]{:S(2)}) collective-permute-start(bf16[4,64,512]{2,1,0:T(8,128)(2,1)S(1)} %get-tuple-element.66), channel_id=1, source_target_pairs={{8,0},{9,1},{10,2},{11,3},{12,4},{13,5},{14,6},{15,7},{0,12},{1,13... | collective-permute-start | bytes 786440 | tf_op jit(solution)/shard_map/ppermute | solution.py:638
  288.6 13.8 %collective-permute-start.25 = (bf16[4,64,512]{2,1,0:T(8,128)(2,1)S(1)}, bf16[4,64,512]{2,1,0:T(8,128)(2,1)S(1)}, u32[]{:S(2)}, u32[]{:S(2)}) collective-permute-start(bf16[4,64,512]{2,1,0:T(8,128)(2,1)S(1)} %get-tuple-element.62), channel_id=1, source_target_pairs={{1,0},{0,1},{3,2},{2,3},{5,4},{4,5},{7,6},{6,7},{9,8},{8,9},{11,10... | collective-permute-start | bytes 786440 | tf_op jit(solution)/shard_map/ppermute | solution.py:638
  289.2 13.2 %collective-permute-start.27 = (bf16[4,64,512]{2,1,0:T(8,128)(2,1)S(1)}, bf16[4,64,512]{2,1,0:T(8,128)(2,1)S(1)}, u32[]{:S(2)}, u32[]{:S(2)}) collective-permute-start(bf16[4,64,512]{2,1,0:T(8,128)(2,1)S(1)} %get-tuple-element.65), channel_id=1, source_target_pairs={{0,4},{1,5},{2,6},{3,7},{4,8},{5,9},{6,10},{7,11},{8,12},{9,13},{1... | collective-permute-start | bytes 786440 | tf_op jit(solution)/shard_map/ppermute | solution.py:638
  290.7 11.7 %collective-permute-start.26 = (bf16[4,64,512]{2,1,0:T(8,128)(2,1)S(1)}, bf16[4,64,512]{2,1,0:T(8,128)(2,1)S(1)}, u32[]{:S(2)}, u32[]{:S(2)}) collective-permute-start(bf16[4,64,512]{2,1,0:T(8,128)(2,1)S(1)} %add.88), channel_id=1, source_target_pairs={{2,0},{3,1},{0,2},{1,3},{6,4},{7,5},{4,6},{5,7},{10,8},{11,9},{8,1... | collective-permute-start | bytes 786440 | tf_op jit(solution)/shard_map/ppermute | solution.py:638
  303.0 5.8 %collective-permute-start.31 = (f32[64,64]{1,0:T(8,128)S(1)}, f32[64,64]{1,0:T(8,128)S(1)}, u32[]{:S(2)}, u32[]{:S(2)}) collective-permute-start(f32[64,64]{1,0:T(8,128)S(1)} %get-tuple-element.67), channel_id=1, source_target_pairs={{0,12},{1,13},{2,14},{3,15},{4,8},{5,9},{6,10},{7,11},{8,4},{9,5},... | collective-permute-start | bytes 49160 | tf_op jit(solution)/shard_map/ppermute | solution.py:565
  305.7 4.8 %collective-permute-start.30 = (f32[64,64]{1,0:T(8,128)S(1)}, f32[64,64]{1,0:T(8,128)S(1)}, u32[]{:S(2)}, u32[]{:S(2)}) collective-permute-start(f32[64,64]{1,0:T(8,128)S(1)} %get-tuple-element.67), channel_id=1, source_target_pairs={{0,8},{1,9},{2,10},{3,11},{4,12},{5,13},{6,14},{7,15},{8,0},{9,1},... | collective-permute-start | bytes 49160 | tf_op jit(solution)/shard_map/ppermute | solution.py:565
  305.7 4.8 %collective-permute-start.29 = (f32[64,64]{1,0:T(8,128)S(1)}, f32[64,64]{1,0:T(8,128)S(1)}, u32[]{:S(2)}, u32[]{:S(2)}) collective-permute-start(f32[64,64]{1,0:T(8,128)S(1)} %get-tuple-element.67), channel_id=1, source_target_pairs={{0,4},{1,5},{2,6},{3,7},{4,0},{5,1},{6,2},{7,3},{8,12},{9,13},{10,... | collective-permute-start | bytes 49160 | tf_op jit(solution)/shard_map/ppermute | solution.py:565
  310.5 3.4 %collective-permute-start.34 = (f32[64,64]{1,0:T(8,128)S(1)}, f32[64,64]{1,0:T(8,128)S(1)}, u32[]{:S(2)}, u32[]{:S(2)}) collective-permute-start(f32[64,64]{1,0:T(8,128)S(1)} %add_add_fusion.refs_0_), channel_id=1, source_target_pairs={{0,3},{1,2},{2,1},{3,0},{4,7},{5,6},{6,5},{7,4},{8,11},{9,10},{10,... | collective-permute-start | bytes 49160 | tf_op jit(solution)/shard_map/ppermute | solution.py:565
  310.6 4.1 %collective-permute-start.33 = (f32[64,64]{1,0:T(8,128)S(1)}, f32[64,64]{1,0:T(8,128)S(1)}, u32[]{:S(2)}, u32[]{:S(2)}) collective-permute-start(f32[64,64]{1,0:T(8,128)S(1)} %add_add_fusion.refs_0_), channel_id=1, source_target_pairs={{0,2},{1,3},{2,0},{3,1},{4,6},{5,7},{6,4},{7,5},{8,10},{9,11},{10,... | collective-permute-start | bytes 49160 | tf_op jit(solution)/shard_map/ppermute | solution.py:565
  311.3 3.3 %collective-permute-start.32 = (f32[64,64]{1,0:T(8,128)S(1)}, f32[64,64]{1,0:T(8,128)S(1)}, u32[]{:S(2)}, u32[]{:S(2)}) collective-permute-start(f32[64,64]{1,0:T(8,128)S(1)} %add_add_fusion.refs_0_), channel_id=1, source_target_pairs={{0,1},{1,0},{2,3},{3,2},{4,5},{5,4},{6,7},{7,6},{8,9},{9,8},{10,11... | collective-permute-start | bytes 49160 | tf_op jit(solution)/shard_map/ppermute | solution.py:565

commit v7 on v5

--- a/solution.py
+++ b/solution.py
@@ -15,6 +15,7 @@
 LOG2E = 1.4426950408889634
 LIST_ROWS = 16
 RING = 4
+APPLY_RING = 8
 LANES = 128
 VMEM_LIMIT = 32 * 1024 * 1024
 VMEM_MOST = 55 * 1024 * 1024
@@ -397,7 +398,7 @@
     def load(i, slot):
         return pltpu.make_async_copy(aff_in.at[i], affbuf.at[slot], asem.at[slot])
 
-    for ahead in range(3):
+    for ahead in range(APPLY_RING - 1):
 
         @pl.when(ahead < end)
         def _():
@@ -410,11 +411,11 @@
 
     @pl.loop(0, end)
     def _(i):
-        slot = i % 4
-
-        @pl.when(i + 3 < end)
+        slot = i % APPLY_RING
+
+        @pl.when(i + APPLY_RING - 1 < end)
         def _():
-            load(i + 3, (i + 3) % 4).start()
+            load(i + APPLY_RING - 1, (i + APPLY_RING - 1) % APPLY_RING).start()
 
         load(i, slot).wait()
         add_products(pan, acc, affbuf[slot], items[0, i], items[1, i])
@@ -436,9 +437,9 @@
         scratch_shapes=[
             pltpu.VMEM((blocks, width, BLOCK), jnp.float32),
             pltpu.VMEM((per_row, blocks * width // per_row, BLOCK), jnp.bfloat16),
-            pltpu.VMEM((4, BLOCK, BLOCK), jnp.bfloat16),
+            pltpu.VMEM((APPLY_RING, BLOCK, BLOCK), jnp.bfloat16),
             pltpu.SemaphoreType.DMA((held * per_row,)),
-            pltpu.SemaphoreType.DMA((4,)),
+            pltpu.SemaphoreType.DMA((APPLY_RING,)),
         ],
         compiler_params=pltpu.CompilerParams(vmem_limit_bytes=50 * 1024 * 1024),
         name="apply",

time: 319 us -> 319 us (level)
  Pallas kernels: 36.2 us -> 47.7 us
  waiting for transfers between devices: 214 us -> 206 us
    pallas_call x2, Pallas kernels: 14.6 us -> 23.4 us  [pair_call(): pl.pallas_call(functools.partial(pair_kernel, stage, held_at, n_slab, joi...]
    ppermute x7, waiting for transfers between devices: 170 us -> 163 us  [on_device(): outgoing = lax.ppermute(outgoing, 'rows', pairs)]
  transfers between devices with their start and end apart: 35 -> 35, of which waited for: 18 -> 17; matrix products, arithmetic and copies ran while one was open for 2% -> 2% of each run, Pallas kernels for 4% -> 6%
where the time goes in v7:
time: 319 us; the launch traced here: 318 us
  waiting for transfers between devices  206 us (65%)
  starting transfers between devices  52.6 us (16%)
  Pallas kernels  47.7 us (15%)
  local copies, waits for them, and re-layouts  9.13 us (3%)
    ppermute x7, waiting for transfers between devices, on_device(): outgoing = lax.ppermute(outgoing, 'rows', pairs)  163 us
    pallas_call x2, Pallas kernels, pair_call(): pl.pallas_call(functools.partial(pair_kernel, stage, held_at, n_slab, joi...  23.4 us
    ppermute x10, waiting for transfers between devices, on_device(): lax.ppermute(outgoing, 'rows', [(target, source) for source, target in me...  19.3 us
    ppermute x7, starting transfers between devices, on_device(): outgoing = lax.ppermute(outgoing, 'rows', pairs)  17.2 us
    ppermute x12, starting transfers between devices, sum_over_rows(): lax.ppermute(value, 'rows', [(i, i ^ step * m) for i in range(count)])  13.8 us
    ppermute x12, waiting for transfers between devices, sum_over_rows(): lax.ppermute(value, 'rows', [(i, i ^ step * m) for i in range(count)])  13.4 us
    ppermute x5, waiting for transfers between devices, spread(): got.append(lax.ppermute(got[via.get(group[0], 0)], 'rows', pairs))  9.36 us
    ppermute x10, starting transfers between devices, on_device(): lax.ppermute(outgoing, 'rows', [(target, source) for source, target in me...  8.71 us
  transfers between devices with their start and end apart: 35, of which 17 were waited for; matrix products, arithmetic and copies ran while one was open for 2% of the time, Pallas kernels for 6%

profile of v7, /device:TPU:0, one launch (start us, length us, event | category | flops | bytes accessed | tf_op | source)
XLA Modules:
  0.0 317.7 jit_solution(375050783202414318)
XLA Ops:
  0.7 1.0 copy-done.2
  1.7 0.7 copy-done.3
  2.4 0.6 extra.1
  3.0 5.9 %collective-permute-start = (bf16[144,1024]{1,0:T(8,128)(2,1)S(1)}, bf16[144,1024]{1,0:T(8,128)(2,1)S(1)}, u32[]{:S(2)}, u32[]{:S(2)}) collective-permute-start(bf16[144,1024]{1,0:T(8,128)(2,1)S(1)} %extra.1), channel_id=1, source_target_pairs={{0,8},{1,9},{2,10},{3,11},{4,12},{5,13},{6,14},{7,15},{12,0},{13,1... | collective-permute-start | bytes 884744 | tf_op jit(solution)/shard_map/ppermute | solution.py:592
  8.9 7.1 %pack.1 = (bf16[2048,1024]{1,0:T(8,128)(2,1)}, bf16[2192,1024]{1,0:T(8,128)(2,1)}) custom-call(bf16[2048,1024]{1,0:T(8,128)(2,1)} %rows.1, bf16[144,1024]{1,0:T(8,128)(2,1)} %copy-done.1), custom_call_target="tpu_custom_call" | custom-call | tf_op jit(solution)/shard_map/pack/pallas_call | solution.py:187
  16.0 0.9 collective-permute-done.refs_5_
  16.9 1.5 collective-permute-start.2
  18.5 1.3 collective-permute-start.4
  19.7 10.5 %collective-permute-start.5 = (bf16[2048,1024]{1,0:T(8,128)(2,1)}, bf16[2048,1024]{1,0:T(8,128)(2,1)}, u32[]{:S(2)}, u32[]{:S(2)}) collective-permute-start(bf16[2048,1024]{1,0:T(8,128)(2,1)} %get-tuple-element.42), channel_id=1, source_target_pairs={{0,4},{1,5},{2,6},{3,7},{4,8},{5,9},{6,10},{7,11},{16,20},{17,21},... | collective-permute-start | bytes 12582920 | tf_op jit(solution)/shard_map/ppermute | solution.py:604
  30.2 85.1 %collective-permute-done.2.refs_2_ = bf16[2192,1024]{1,0:T(8,128)(2,1)} collective-permute-done((bf16[2192,1024]{1,0:T(8,128)(2,1)}, bf16[2192,1024]{1,0:T(8,128)(2,1)}, u32[]{:S(2)}, u32[]{:S(2)}) %collective-permute-start.2) | collective-permute-done | bytes 4489248 | tf_op jit(solution)/shard_map/ppermute | solution.py:604
  115.3 3.0 collective-permute-done.5
  118.3 2.6 collective-permute-start.6
  121.0 2.5 collective-permute-done.4.refs_4_
  123.5 1.3 collective-permute-start.7
  124.8 0.7 slice.32
  125.6 0.7 dynamic-slice_bitcast_fusion
  126.3 0.7 slice.45
  127.0 0.7 slice.43
  127.6 0.7 slice.42
  128.3 0.7 slice.44
  129.5 0.2 slice_reduce_fusion
  129.7 0.3 select_reduce_fusion
  130.6 0.1 convert_reduce_fusion.1.bounds
  130.8 2.3 copy-done
  133.0 13.4 %pairs.2 = (f32[28,64,512]{2,1,0:T(8,128)S(1)}, bf16[2,896,512]{2,1,0:T(8,128)(2,1)S(1)}, bf16[20,512,512]{2,1,0:T(8,128)(2,1)}) custom-call(s32[2,20]{1,0:T(2,128)S(1)} %pad_add_fusion.items, s32[3]{0:T(128)S(1)} %convert_reduce_fusion.1.bounds, bf16[2192,1024]{1,0:T(8,128)(2,1)S(1)} %copy-done, bf16[2192,1024]{1,0:T(8,128)(2,1)} %collective-permute-done.1.refs_1_, ...), custom_call_target="tpu_custom_call" | custom-call | tf_op jit(solution)/shard_map/pairs/pallas_call | solution.py:372
  146.5 72.7 %collective-permute-done.7.refs_6_ = bf16[2048,1024]{1,0:T(8,128)(2,1)} collective-permute-done((bf16[2048,1024]{1,0:T(8,128)(2,1)}, bf16[2048,1024]{1,0:T(8,128)(2,1)}, u32[]{:S(2)}, u32[]{:S(2)}) %collective-permute-start.7) | collective-permute-done | bytes 4194336 | tf_op jit(solution)/shard_map/ppermute | solution.py:604
  219.1 10.0 %pairs.3 = (f32[4,64,512]{2,1,0:T(8,128)S(1)}, bf16[4,64,512]{2,1,0:T(8,128)(2,1)S(1)}, bf16[4,64,512]{2,1,0:T(8,128)(2,1)S(1)}, bf16[4,64,512]{2,1,0:T(8,128)(2...) custom-call(s32[2,20]{1,0:T(2,128)S(1)} %pad_add_fusion.items, ...), custom_call_target="tpu_custom_call", output_to_operand_aliasing={{6}: (10, {})} | custom-call | tf_op jit(solution)/shard_map/pairs/pallas_call | solution.py:372
  229.2 1.9 collective-permute-start.12
  231.2 0.6 collective-permute-start.9
  231.7 1.3 collective-permute-start.11
  233.1 0.8 collective-permute-start.10
  233.9 9.3 %collective-permute-done.12.refs_3_ = bf16[4,64,512]{2,1,0:T(8,128)(2,1)S(1)} collective-permute-done((bf16[4,64,512]{2,1,0:T(8,128)(2,1)S(1)}, bf16[4,64,512]{2,1,0:T(8,128)(2,1)S(1)}, u32[]{:S(2)}, u32[]{:S(2)}) %collective-permute-start.12) | collective-permute-done | bytes 262176 | tf_op jit(solution)/shard_map/ppermute | solution.py:633
  243.3 0.6 gram.2
  243.9 0.5 collective-permute-start.15
  244.4 1.2 collective-permute-start.14
  245.6 0.2 collective-permute-start.13
  245.8 1.6 collective-permute-done.15
  247.4 0.9 collective-permute-done.14
  248.4 4.3 %collective-permute-start.18 = (f32[64,64]{1,0:T(8,128)S(1)}, f32[64,64]{1,0:T(8,128)S(1)}, u32[]{:S(2)}, u32[]{:S(2)}) collective-permute-start(f32[64,64]{1,0:T(8,128)S(1)} %add_add_fusion.1.refs_0_), channel_id=1, source_target_pairs={{0,12},{1,13},{2,14},{3,15},{4,8},{5,9},{6,10},{7,11},{8,4},{9,5},... | collective-permute-start | bytes 49160 | tf_op jit(solution)/shard_map/ppermute | solution.py:562
  252.7 0.6 collective-permute-start.16
  253.3 1.3 collective-permute-done.18.refs_3_
  254.6 2.9 collective-permute-done.17.refs_2_
  257.5 3.6 %panel.4.refs_0_ = bf16[128,1024]{1,0:T(8,128)(2,1)S(1)} custom-call(f32[64,64]{1,0:T(8,128)S(1)} %add_add_fusion.1.refs_0_, f32[64,64]{1,0:T(8,128)S(1)} %collective-permute-done.16.refs_1_, f32[64,64]{1,0:T(8,128)S(1)} %collective-permute-done.17.refs_2_, f32[64,64]{1,0:T(8,128)S(1)} %collective-permute-done.18.refs_3_, ...), custom_call_target="tpu_custom_call" | custom-call | tf_op jit(solution)/shard_map/panel/pallas_call | solution.py:547
  261.2 1.3 collective-permute-start.20
  262.4 3.9 %collective-permute-start.23 = (bf16[128,1024]{1,0:T(8,128)(2,1)S(1)}, bf16[128,1024]{1,0:T(8,128)(2,1)S(1)}, u32[]{:S(2)}, u32[]{:S(2)}) collective-permute-start(bf16[128,1024]{1,0:T(8,128)(2,1)S(1)} %panel.4.refs_0_), channel_id=1, source_target_pairs={{0,8},{1,9},{2,10},{3,11},{4,12},{5,13},{6,14},{7,15},{12,0},{13,1... | collective-permute-start | bytes 786440 | tf_op jit(solution)/shard_map/ppermute | solution.py:587
  266.4 1.3 collective-permute-start.22
  267.8 0.5 collective-permute-start.21
  268.3 6.6 %collective-permute-done.23.refs_5_ = bf16[128,1024]{1,0:T(8,128)(2,1)S(1)} collective-permute-done((bf16[128,1024]{1,0:T(8,128)(2,1)S(1)}, bf16[128,1024]{1,0:T(8,128)(2,1)S(1)}, u32[]{:S(2)}, u32[]{:S(2)}) %collective-permute-start.23) | collective-permute-done | bytes 262176 | tf_op jit(solution)/shard_map/ppermute | solution.py:587
  274.9 2.7 collective-permute-done.22.refs_4_
  277.6 7.3 %apply.1 = (f32[4,64,512]{2,1,0:T(8,128)S(1)}, bf16[4,64,512]{2,1,0:T(8,128)(2,1)S(1)}, bf16[4,64,512]{2,1,0:T(8,128)(2,1)S(1)}, bf16[4,64,512]{2,1,0:T(8,128)(2...) custom-call(s32[2,20]{1,0:T(2,128)S(1)} %pad_add_fusion.items, ...), custom_call_target="tpu_custom_call" | custom-call | tf_op jit(solution)/shard_map/apply/pallas_call | solution.py:432
  284.9 1.9 collective-permute-start.28
  286.9 0.6 collective-permute-start.25
  287.4 1.5 collective-permute-start.27
  289.1 9.9 %collective-permute-done.28.refs_3_ = bf16[4,64,512]{2,1,0:T(8,128)(2,1)S(1)} collective-permute-done((bf16[4,64,512]{2,1,0:T(8,128)(2,1)S(1)}, bf16[4,64,512]{2,1,0:T(8,128)(2,1)S(1)}, u32[]{:S(2)}, u32[]{:S(2)}) %collective-permute-start.28) | collective-permute-done | bytes 262176 | tf_op jit(solution)/shard_map/ppermute | solution.py:633
  299.0 0.6 gram.3
  299.7 1.7 collective-permute-start.30
  301.4 0.2 collective-permute-start.29
  301.6 1.6 collective-permute-done.31
  303.1 1.0 collective-permute-done.30
  304.1 4.3 %collective-permute-start.34 = (f32[64,64]{1,0:T(8,128)S(1)}, f32[64,64]{1,0:T(8,128)S(1)}, u32[]{:S(2)}, u32[]{:S(2)}) collective-permute-start(f32[64,64]{1,0:T(8,128)S(1)} %add_add_fusion.refs_0_), channel_id=1, source_target_pairs={{0,12},{1,13},{2,14},{3,15},{4,8},{5,9},{6,10},{7,11},{8,4},{9,5},... | collective-permute-start | bytes 49160 | tf_op jit(solution)/shard_map/ppermute | solution.py:562
  308.4 0.6 collective-permute-start.32
  309.1 1.3 collective-permute-done.34.refs_3_
  310.3 2.9 collective-permute-done.33.refs_2_
  313.2 4.4 %panel.5 = f32[64,2048]{1,0:T(8,128)} custom-call(f32[64,64]{1,0:T(8,128)S(1)} %add_add_fusion.refs_0_, f32[64,64]{1,0:T(8,128)S(1)} %collective-permute-done.32.refs_1_, f32[64,64]{1,0:T(8,128)S(1)} %collective-permute-done.33.refs_2_, f32[64,64]{1,0:T(8,128)S(1)} %collective-permute-done.34.refs_3_, f32[4,64,512]{2,1,0:T(8,128)S(1)} %get-tuple-element.66.refs_4_), custom_call_target="tpu_custom_call" | custom-call | tf_op jit(solution)/shard_map/panel/pallas_call | solution.py:547
  (60 shorter events, 2.0 us)
Async XLA Ops:
  0.7 1.0 copy-start.2
  1.7 0.7 copy-start.3
  3.0 6.0 %copy-start.1 = (bf16[144,1024]{1,0:T(8,128)(2,1)}, bf16[144,1024]{1,0:T(8,128)(2,1)S(1)}, u32[]{:S(2)}) copy-start(bf16[144,1024]{1,0:T(8,128)(2,1)S(1)} %extra.1) | copy-start | bytes 884740
  3.0 14.0 %collective-permute-start = (bf16[144,1024]{1,0:T(8,128)(2,1)S(1)}, bf16[144,1024]{1,0:T(8,128)(2,1)S(1)}, u32[]{:S(2)}, u32[]{:S(2)}) collective-permute-start(bf16[144,1024]{1,0:T(8,128)(2,1)S(1)} %extra.1), channel_id=1, source_target_pairs={{0,8},{1,9},{2,10},{3,11},{4,12},{5,13},{6,14},{7,15},{12,0},{13,1... | collective-permute-start | bytes 884744 | tf_op jit(solution)/shard_map/ppermute | solution.py:592
  16.9 98.4 %collective-permute-start.2 = (bf16[2192,1024]{1,0:T(8,128)(2,1)}, bf16[2192,1024]{1,0:T(8,128)(2,1)}, u32[]{:S(2)}, u32[]{:S(2)}) collective-permute-start(bf16[2192,1024]{1,0:T(8,128)(2,1)} %get-tuple-element.39.refs_0_), channel_id=1, source_target_pairs={{0,2},{1,3},{2,0},{3,1},{4,6},{5,7},{6,4},{7,5},{8,10},{9,11},{10,... | collective-permute-start | bytes 13467656 | tf_op jit(solution)/shard_map/ppermute | solution.py:604
  18.5 105.0 %collective-permute-start.4 = (bf16[2192,1024]{1,0:T(8,128)(2,1)}, bf16[2192,1024]{1,0:T(8,128)(2,1)}, u32[]{:S(2)}, u32[]{:S(2)}) collective-permute-start(bf16[2192,1024]{1,0:T(8,128)(2,1)} %get-tuple-element.39.refs_0_), channel_id=1, source_target_pairs={{4,0},{5,1},{6,2},{7,3},{8,4},{9,5},{10,6},{11,7},{12,8},{13,9},{1... | collective-permute-start | bytes 13467656 | tf_op jit(solution)/shard_map/ppermute | solution.py:604
  19.7 98.6 %collective-permute-start.5 = (bf16[2048,1024]{1,0:T(8,128)(2,1)}, bf16[2048,1024]{1,0:T(8,128)(2,1)}, u32[]{:S(2)}, u32[]{:S(2)}) collective-permute-start(bf16[2048,1024]{1,0:T(8,128)(2,1)} %get-tuple-element.42), channel_id=1, source_target_pairs={{0,4},{1,5},{2,6},{3,7},{4,8},{5,9},{6,10},{7,11},{16,20},{17,21},... | collective-permute-start | bytes 12582920 | tf_op jit(solution)/shard_map/ppermute | solution.py:604
  30.2 97.4 %collective-permute-start.1 = (bf16[2192,1024]{1,0:T(8,128)(2,1)}, bf16[2192,1024]{1,0:T(8,128)(2,1)}, u32[]{:S(2)}, u32[]{:S(2)}) collective-permute-start(bf16[2192,1024]{1,0:T(8,128)(2,1)} %get-tuple-element.39.refs_0_), channel_id=1, source_target_pairs={{0,1},{1,0},{2,3},{3,2},{4,5},{5,4},{6,7},{7,6},{8,9},{9,8},{10,11... | collective-permute-start | bytes 13467656 | tf_op jit(solution)/shard_map/ppermute | solution.py:604
  115.3 13.0 %collective-permute-start.3 = (bf16[2192,1024]{1,0:T(8,128)(2,1)}, bf16[2192,1024]{1,0:T(8,128)(2,1)}, u32[]{:S(2)}, u32[]{:S(2)}) collective-permute-start(bf16[2192,1024]{1,0:T(8,128)(2,1)} %collective-permute-done.2.refs_2_), channel_id=1, source_target_pairs={{0,1},{1,0},{2,3},{3,2},{4,5},{5,4},{6,7},{7,6},{8,9},{9,8},{10,11... | collective-permute-start | bytes 13467656 | tf_op jit(solution)/shard_map/ppermute | solution.py:604
  118.3 28.1 %collective-permute-start.6 = (bf16[2048,1024]{1,0:T(8,128)(2,1)}, bf16[2048,1024]{1,0:T(8,128)(2,1)}, u32[]{:S(2)}, u32[]{:S(2)}) collective-permute-start(bf16[2048,1024]{1,0:T(8,128)(2,1)} %collective-permute-done.5), channel_id=1, source_target_pairs={{4,8},{5,9},{6,10},{7,11},{8,12},{9,13},{10,14},{11,15},{20,24},{2... | collective-permute-start | bytes 12582920 | tf_op jit(solution)/shard_map/ppermute | solution.py:604
  123.5 95.6 %collective-permute-start.7 = (bf16[2048,1024]{1,0:T(8,128)(2,1)}, bf16[2048,1024]{1,0:T(8,128)(2,1)}, u32[]{:S(2)}, u32[]{:S(2)}) collective-permute-start(bf16[2048,1024]{1,0:T(8,128)(2,1)} %get-tuple-element.42), channel_id=1, source_target_pairs={{12,0},{13,1},{14,2},{15,3},{28,16},{29,17},{30,18},{31,19}} | collective-permute-start | bytes 12582920 | tf_op jit(solution)/shard_map/ppermute | solution.py:604
  130.7 2.3 copy-start
  229.1 2.0 collective-permute-start.8
  229.2 14.0 %collective-permute-start.12 = (bf16[4,64,512]{2,1,0:T(8,128)(2,1)S(1)}, bf16[4,64,512]{2,1,0:T(8,128)(2,1)S(1)}, u32[]{:S(2)}, u32[]{:S(2)}) collective-permute-start(bf16[4,64,512]{2,1,0:T(8,128)(2,1)S(1)} %get-tuple-element.53), channel_id=1, source_target_pairs={{8,0},{9,1},{10,2},{11,3},{12,4},{13,5},{14,6},{15,7},{0,12},{1,13... | collective-permute-start | bytes 786440 | tf_op jit(solution)/shard_map/ppermute | solution.py:633
  231.2 12.1 %collective-permute-start.9 = (bf16[4,64,512]{2,1,0:T(8,128)(2,1)S(1)}, bf16[4,64,512]{2,1,0:T(8,128)(2,1)S(1)}, u32[]{:S(2)}, u32[]{:S(2)}) collective-permute-start(bf16[4,64,512]{2,1,0:T(8,128)(2,1)S(1)} %get-tuple-element.49), channel_id=1, source_target_pairs={{1,0},{0,1},{3,2},{2,3},{5,4},{4,5},{7,6},{6,7},{9,8},{8,9},{11,10... | collective-permute-start | bytes 786440 | tf_op jit(solution)/shard_map/ppermute | solution.py:633
  231.7 11.6 %collective-permute-start.11 = (bf16[4,64,512]{2,1,0:T(8,128)(2,1)S(1)}, bf16[4,64,512]{2,1,0:T(8,128)(2,1)S(1)}, u32[]{:S(2)}, u32[]{:S(2)}) collective-permute-start(bf16[4,64,512]{2,1,0:T(8,128)(2,1)S(1)} %get-tuple-element.52), channel_id=1, source_target_pairs={{0,4},{1,5},{2,6},{3,7},{4,8},{5,9},{6,10},{7,11},{8,12},{9,13},{1... | collective-permute-start | bytes 786440 | tf_op jit(solution)/shard_map/ppermute | solution.py:633
  233.1 10.2 %collective-permute-start.10 = (bf16[4,64,512]{2,1,0:T(8,128)(2,1)S(1)}, bf16[4,64,512]{2,1,0:T(8,128)(2,1)S(1)}, u32[]{:S(2)}, u32[]{:S(2)}) collective-permute-start(bf16[4,64,512]{2,1,0:T(8,128)(2,1)S(1)} %add.84), channel_id=1, source_target_pairs={{2,0},{3,1},{0,2},{1,3},{6,4},{7,5},{4,6},{5,7},{10,8},{11,9},{8,1... | collective-permute-start | bytes 786440 | tf_op jit(solution)/shard_map/ppermute | solution.py:633
  243.9 3.5 %collective-permute-start.15 = (f32[64,64]{1,0:T(8,128)S(1)}, f32[64,64]{1,0:T(8,128)S(1)}, u32[]{:S(2)}, u32[]{:S(2)}) collective-permute-start(f32[64,64]{1,0:T(8,128)S(1)} %get-tuple-element.54), channel_id=1, source_target_pairs={{0,3},{1,2},{2,1},{3,0},{4,7},{5,6},{6,5},{7,4},{8,11},{9,10},{10,... | collective-permute-start | bytes 49160 | tf_op jit(solution)/shard_map/ppermute | solution.py:562
  244.4 3.9 %collective-permute-start.14 = (f32[64,64]{1,0:T(8,128)S(1)}, f32[64,64]{1,0:T(8,128)S(1)}, u32[]{:S(2)}, u32[]{:S(2)}) collective-permute-start(f32[64,64]{1,0:T(8,128)S(1)} %get-tuple-element.54), channel_id=1, source_target_pairs={{0,2},{1,3},{2,0},{3,1},{4,6},{5,7},{6,4},{7,5},{8,10},{9,11},{10,... | collective-permute-start | bytes 49160 | tf_op jit(solution)/shard_map/ppermute | solution.py:562
  245.6 2.7 collective-permute-start.13
  248.4 6.2 %collective-permute-start.18 = (f32[64,64]{1,0:T(8,128)S(1)}, f32[64,64]{1,0:T(8,128)S(1)}, u32[]{:S(2)}, u32[]{:S(2)}) collective-permute-start(f32[64,64]{1,0:T(8,128)S(1)} %add_add_fusion.1.refs_0_), channel_id=1, source_target_pairs={{0,12},{1,13},{2,14},{3,15},{4,8},{5,9},{6,10},{7,11},{8,4},{9,5},... | collective-permute-start | bytes 49160 | tf_op jit(solution)/shard_map/ppermute | solution.py:562
  252.7 4.8 %collective-permute-start.17 = (f32[64,64]{1,0:T(8,128)S(1)}, f32[64,64]{1,0:T(8,128)S(1)}, u32[]{:S(2)}, u32[]{:S(2)}) collective-permute-start(f32[64,64]{1,0:T(8,128)S(1)} %add_add_fusion.1.refs_0_), channel_id=1, source_target_pairs={{0,8},{1,9},{2,10},{3,11},{4,12},{5,13},{6,14},{7,15},{8,0},{9,1},... | collective-permute-start | bytes 49160 | tf_op jit(solution)/shard_map/ppermute | solution.py:562
  252.7 4.8 %collective-permute-start.16 = (f32[64,64]{1,0:T(8,128)S(1)}, f32[64,64]{1,0:T(8,128)S(1)}, u32[]{:S(2)}, u32[]{:S(2)}) collective-permute-start(f32[64,64]{1,0:T(8,128)S(1)} %add_add_fusion.1.refs_0_), channel_id=1, source_target_pairs={{0,4},{1,5},{2,6},{3,7},{4,0},{5,1},{6,2},{7,3},{8,12},{9,13},{10,... | collective-permute-start | bytes 49160 | tf_op jit(solution)/shard_map/ppermute | solution.py:562
  261.2 6.7 %collective-permute-start.20 = (bf16[128,1024]{1,0:T(8,128)(2,1)S(1)}, bf16[128,1024]{1,0:T(8,128)(2,1)S(1)}, u32[]{:S(2)}, u32[]{:S(2)}) collective-permute-start(bf16[128,1024]{1,0:T(8,128)(2,1)S(1)} %panel.4.refs_0_), channel_id=1, source_target_pairs={{0,2},{1,3},{2,0},{3,1},{4,6},{5,7},{6,4},{7,5},{8,10},{9,11},{10,... | collective-permute-start | bytes 786440 | tf_op jit(solution)/shard_map/ppermute | solution.py:587
  262.4 12.4 %collective-permute-start.23 = (bf16[128,1024]{1,0:T(8,128)(2,1)S(1)}, bf16[128,1024]{1,0:T(8,128)(2,1)S(1)}, u32[]{:S(2)}, u32[]{:S(2)}) collective-permute-start(bf16[128,1024]{1,0:T(8,128)(2,1)S(1)} %panel.4.refs_0_), channel_id=1, source_target_pairs={{0,8},{1,9},{2,10},{3,11},{4,12},{5,13},{6,14},{7,15},{12,0},{13,1... | collective-permute-start | bytes 786440 | tf_op jit(solution)/shard_map/ppermute | solution.py:587
  266.4 11.2 %collective-permute-start.22 = (bf16[128,1024]{1,0:T(8,128)(2,1)S(1)}, bf16[128,1024]{1,0:T(8,128)(2,1)S(1)}, u32[]{:S(2)}, u32[]{:S(2)}) collective-permute-start(bf16[128,1024]{1,0:T(8,128)(2,1)S(1)} %panel.4.refs_0_), channel_id=1, source_target_pairs={{4,0},{5,1},{6,2},{7,3},{8,4},{9,5},{10,6},{11,7},{12,8},{13,9},{1... | collective-permute-start | bytes 786440 | tf_op jit(solution)/shard_map/ppermute | solution.py:587
  267.7 9.9 %collective-permute-start.19 = (bf16[128,1024]{1,0:T(8,128)(2,1)S(1)}, bf16[128,1024]{1,0:T(8,128)(2,1)S(1)}, u32[]{:S(2)}, u32[]{:S(2)}) collective-permute-start(bf16[128,1024]{1,0:T(8,128)(2,1)S(1)} %panel.4.refs_0_), channel_id=1, source_target_pairs={{0,1},{1,0},{2,3},{3,2},{4,5},{5,4},{6,7},{7,6},{8,9},{9,8},{10,11... | collective-permute-start | bytes 786440 | tf_op jit(solution)/shard_map/ppermute | solution.py:587
  267.8 9.8 %collective-permute-start.21 = (bf16[128,1024]{1,0:T(8,128)(2,1)S(1)}, bf16[128,1024]{1,0:T(8,128)(2,1)S(1)}, u32[]{:S(2)}, u32[]{:S(2)}) collective-permute-start(bf16[128,1024]{1,0:T(8,128)(2,1)S(1)} %collective-permute-done.20.refs_2_), channel_id=1, source_target_pairs={{0,1},{1,0},{2,3},{3,2},{4,5},{5,4},{6,7},{7,6},{8,9},{9,8},{10,11... | collective-permute-start | bytes 786440 | tf_op jit(solution)/shard_map/ppermute | solution.py:587
  284.9 2.0 collective-permute-start.24
  284.9 14.1 %collective-permute-start.28 = (bf16[4,64,512]{2,1,0:T(8,128)(2,1)S(1)}, bf16[4,64,512]{2,1,0:T(8,128)(2,1)S(1)}, u32[]{:S(2)}, u32[]{:S(2)}) collective-permute-start(bf16[4,64,512]{2,1,0:T(8,128)(2,1)S(1)} %get-tuple-element.64), channel_id=1, source_target_pairs={{8,0},{9,1},{10,2},{11,3},{12,4},{13,5},{14,6},{15,7},{0,12},{1,13... | collective-permute-start | bytes 786440 | tf_op jit(solution)/shard_map/ppermute | solution.py:633
  286.9 12.1 %collective-permute-start.25 = (bf16[4,64,512]{2,1,0:T(8,128)(2,1)S(1)}, bf16[4,64,512]{2,1,0:T(8,128)(2,1)S(1)}, u32[]{:S(2)}, u32[]{:S(2)}) collective-permute-start(bf16[4,64,512]{2,1,0:T(8,128)(2,1)S(1)} %get-tuple-element.60), channel_id=1, source_target_pairs={{1,0},{0,1},{3,2},{2,3},{5,4},{4,5},{7,6},{6,7},{9,8},{8,9},{11,10... | collective-permute-start | bytes 786440 | tf_op jit(solution)/shard_map/ppermute | solution.py:633
  287.4 11.6 %collective-permute-start.27 = (bf16[4,64,512]{2,1,0:T(8,128)(2,1)S(1)}, bf16[4,64,512]{2,1,0:T(8,128)(2,1)S(1)}, u32[]{:S(2)}, u32[]{:S(2)}) collective-permute-start(bf16[4,64,512]{2,1,0:T(8,128)(2,1)S(1)} %get-tuple-element.63), channel_id=1, source_target_pairs={{0,4},{1,5},{2,6},{3,7},{4,8},{5,9},{6,10},{7,11},{8,12},{9,13},{1... | collective-permute-start | bytes 786440 | tf_op jit(solution)/shard_map/ppermute | solution.py:633
  289.0 10.0 %collective-permute-start.26 = (bf16[4,64,512]{2,1,0:T(8,128)(2,1)S(1)}, bf16[4,64,512]{2,1,0:T(8,128)(2,1)S(1)}, u32[]{:S(2)}, u32[]{:S(2)}) collective-permute-start(bf16[4,64,512]{2,1,0:T(8,128)(2,1)S(1)} %add.88), channel_id=1, source_target_pairs={{2,0},{3,1},{0,2},{1,3},{6,4},{7,5},{4,6},{5,7},{10,8},{11,9},{8,1... | collective-permute-start | bytes 786440 | tf_op jit(solution)/shard_map/ppermute | solution.py:633
  299.6 3.5 %collective-permute-start.31 = (f32[64,64]{1,0:T(8,128)S(1)}, f32[64,64]{1,0:T(8,128)S(1)}, u32[]{:S(2)}, u32[]{:S(2)}) collective-permute-start(f32[64,64]{1,0:T(8,128)S(1)} %get-tuple-element.65), channel_id=1, source_target_pairs={{0,3},{1,2},{2,1},{3,0},{4,7},{5,6},{6,5},{7,4},{8,11},{9,10},{10,... | collective-permute-start | bytes 49160 | tf_op jit(solution)/shard_map/ppermute | solution.py:562
  299.7 4.4 %collective-permute-start.30 = (f32[64,64]{1,0:T(8,128)S(1)}, f32[64,64]{1,0:T(8,128)S(1)}, u32[]{:S(2)}, u32[]{:S(2)}) collective-permute-start(f32[64,64]{1,0:T(8,128)S(1)} %get-tuple-element.65), channel_id=1, source_target_pairs={{0,2},{1,3},{2,0},{3,1},{4,6},{5,7},{6,4},{7,5},{8,10},{9,11},{10,... | collective-permute-start | bytes 49160 | tf_op jit(solution)/shard_map/ppermute | solution.py:562
  301.4 2.7 collective-permute-start.29
  304.1 6.2 %collective-permute-start.34 = (f32[64,64]{1,0:T(8,128)S(1)}, f32[64,64]{1,0:T(8,128)S(1)}, u32[]{:S(2)}, u32[]{:S(2)}) collective-permute-start(f32[64,64]{1,0:T(8,128)S(1)} %add_add_fusion.refs_0_), channel_id=1, source_target_pairs={{0,12},{1,13},{2,14},{3,15},{4,8},{5,9},{6,10},{7,11},{8,4},{9,5},... | collective-permute-start | bytes 49160 | tf_op jit(solution)/shard_map/ppermute | solution.py:562
  308.4 4.8 %collective-permute-start.33 = (f32[64,64]{1,0:T(8,128)S(1)}, f32[64,64]{1,0:T(8,128)S(1)}, u32[]{:S(2)}, u32[]{:S(2)}) collective-permute-start(f32[64,64]{1,0:T(8,128)S(1)} %add_add_fusion.refs_0_), channel_id=1, source_target_pairs={{0,8},{1,9},{2,10},{3,11},{4,12},{5,13},{6,14},{7,15},{8,0},{9,1},... | collective-permute-start | bytes 49160 | tf_op jit(solution)/shard_map/ppermute | solution.py:562
  308.4 4.8 %collective-permute-start.32 = (f32[64,64]{1,0:T(8,128)S(1)}, f32[64,64]{1,0:T(8,128)S(1)}, u32[]{:S(2)}, u32[]{:S(2)}) collective-permute-start(f32[64,64]{1,0:T(8,128)S(1)} %add_add_fusion.refs_0_), channel_id=1, source_target_pairs={{0,4},{1,5},{2,6},{3,7},{4,0},{5,1},{6,2},{7,3},{8,12},{9,13},{10,... | collective-permute-start | bytes 49160 | tf_op jit(solution)/shard_map/ppermute | solution.py:562
